TPU v7x, 512 devices: a whole 4x4x16 slice. The times are simulated.
512 devices in a mesh: section: 8 (over y, z_hi), dp: 64 (over z_lo, x, core).
Axes of the slice: x: 4, y: 4, z: 16 (z_hi: 2, z_lo: 8; z = z_hi * 8 + z_lo), core: 2. Of those that a mesh axis runs over, the one named last changes fastest.
Arguments:
- images: bfloat16 [256, 128, 1664], P('dp'), may hold values from -6 to 6
- text_pooled: bfloat16 [256, 1280], P('dp'), may hold values from -6 to 6
- image_weight: bfloat16 [8, 1664, 1664], P('section', 'dp'), may hold values from -0.15625 to 0.15625
- proj_image: bfloat16 [1664, 1280], P(None, 'dp'), may hold values from -0.15625 to 0.15625
- proj_text: bfloat16 [1280, 1280], P(None, 'dp'), may hold values from -0.15625 to 0.15625
- logit_scale: float32 [1], replicated, may hold values from 20 to 60
- pairing: int32 [256], replicated, may hold values from 0 to 255, each once
Outputs:
- logits: float32 [256, 256], P('dp', 'section')
- image_loss: float32 [256], P('dp')
- text_loss: float32 [256], P('dp')
Inputs may be any that keep to these rules, and one draw needn't show every extreme that they name: `pairing`: each caption index appears exactly once.
All inputs are finite; a program needn't handle non-finite values.
Results may differ from a plain program's by a relative error of at most 0.02.
Values may be sent and summed in bfloat16 or wider, within the bound.
No kernel may reach another device: no remote copies, remote signals or barrier semaphores. Data moves between devices by JAX's collectives and lax.ppermute only.
A program may use at most 64 MiB of HBM per device.

v0:
```python
import jax
import jax.numpy as jnp
from jax import lax
from jax.sharding import PartitionSpec as P


def shifted(value, axis, steps):
    count = lax.axis_size(axis)
    leading, last = (max(0, -steps), min(count, count - steps))
    return lax.ppermute(value, axis, [(source, source + steps) for source in range(leading, last)])


def from_root(value, axis, source):
    kept = jnp.where(lax.axis_index(axis) == source, value, 0).astype(value.dtype)
    return lax.psum(kept, axis)


def normalize(values_in):
    values_in = values_in.astype(jnp.float32)
    center = jnp.mean(values_in, axis=-1, keepdims=True)
    spread = jnp.mean((values_in - center) ** 2, axis=-1, keepdims=True)
    return (values_in - center) / jnp.sqrt(spread + 1e-05)


def run_sections(images, weight, pieces, passer):
    sections = lax.axis_size("section")
    section_index = lax.axis_index("section")
    micro_count = images.shape[0]
    tokens = images.shape[1]
    width = images.shape[2]
    block = tokens // pieces
    units = micro_count * pieces
    flat = images.reshape(micro_count * tokens, width)

    def apply_layer(values_in):
        normed = normalize(values_in).astype(jnp.bfloat16)
        update = jnp.dot(normed, weight, preferred_element_type=jnp.float32)
        return (values_in.astype(jnp.float32) + jax.nn.gelu(update)).astype(jnp.bfloat16)

    def unchanged(values_in):
        return values_in

    def advance(turn_index, carried):
        arrived, pooled = carried
        feed_start = (jnp.minimum(turn_index, units - 1) * block).astype(jnp.int32)
        fed_input = lax.dynamic_slice_in_dim(flat, feed_start, block, 0)
        current = jnp.where(section_index == 0, fed_input, arrived)
        slot_index = turn_index - section_index
        active = (slot_index >= 0) & (slot_index < units)
        result = lax.cond(active, apply_layer, unchanged, current)
        storing = active & (section_index == sections - 1)
        place = jnp.clip(slot_index // pieces, 0, micro_count - 1)
        earlier = lax.dynamic_slice_in_dim(pooled, place, 1, 0)
        fresh = (jnp.sum(normalize(result), axis=0) / tokens)[None, :]
        pooled = lax.dynamic_update_slice_in_dim(
            pooled, earlier + jnp.where(storing, fresh, 0.0), place, 0
        )
        arrived = passer(result)
        return (arrived, pooled)

    start_state = (
        jnp.zeros((block, width), jnp.bfloat16),
        jnp.zeros((micro_count, width), jnp.float32),
    )
    arrived, pooled = lax.fori_loop(0, units + sections - 1, advance, start_state)
    return pooled


def on_device(images, text_pooled, image_weight, proj_image, proj_text, logit_scale, pairing):
    weight = lax.all_gather(image_weight[0], "dp", axis=0, tiled=True)
    sections = lax.axis_size("section")
    micro_count = images.shape[0]

    def passer(result):
        return shifted(result, "section", 1)

    pooled = run_sections(images, weight, 1, passer)
    pooled_image = from_root(pooled.astype(jnp.bfloat16), "section", sections - 1)
    image_all, text_all = (
        lax.all_gather(pooled_image, "dp", axis=0, tiled=True),
        lax.all_gather(text_pooled, "dp", axis=0, tiled=True),
    )
    image_part = jnp.dot(image_all, proj_image, preferred_element_type=jnp.float32)
    text_part = jnp.dot(text_all, proj_text, preferred_element_type=jnp.float32)
    scale_value = logit_scale[0]
    row_start = lax.axis_index("dp") * micro_count
    contract = (((1,), (1,)), ((), ()))
    image_square, text_square = lax.psum(
        (jnp.sum(image_part * image_part, axis=1), jnp.sum(text_part * text_part, axis=1)), "dp"
    )
    image_unit = (image_part / jnp.sqrt(image_square + 1e-06)[:, None]).astype(jnp.bfloat16)
    text_unit = (text_part / jnp.sqrt(text_square + 1e-06)[:, None]).astype(jnp.bfloat16)
    partial_dots = lax.dot_general(
        image_unit, text_unit, contract, preferred_element_type=jnp.float32
    )
    logits_all = scale_value * lax.psum(partial_dots, "dp")
    own_logits = lax.dynamic_slice_in_dim(logits_all, row_start, micro_count, 0)
    column_lse = jnp.log(jnp.sum(jnp.exp(logits_all), axis=0))
    own_pairs = lax.dynamic_slice_in_dim(pairing, row_start, micro_count, 0)
    positive = jnp.take_along_axis(own_logits, own_pairs[:, None], axis=1)[:, 0]
    image_loss = jnp.log(jnp.sum(jnp.exp(own_logits), axis=1)) - positive
    text_loss = jnp.take(column_lse, own_pairs) - positive
    column_count = own_logits.shape[1] // sections
    column_start = lax.axis_index("section") * column_count
    logit_block = lax.dynamic_slice_in_dim(own_logits, column_start, column_count, 1)
    return (logit_block, image_loss, text_loss)


def solution(mesh):
    in_specs = (
        P("dp", None, None),
        P("dp", None),
        P("section", "dp", None),
        P(None, "dp"),
        P(None, "dp"),
        P(),
        P(),
    )
    out_specs = (P("dp", "section"), P("dp"), P("dp"))
    return jax.shard_map(
        on_device, mesh=mesh, in_specs=in_specs, out_specs=out_specs, check_vma=False
    )
```

profile of v0, /device:TPU:1, one launch (start us, length us, event | category | flops | bytes accessed | tf_op | source)
XLA Modules:
  0.0 1851.0 jit_solution(10682650525161477165)
XLA Ops:
  9.0 131.2 %all-gather.2 = bf16[64,4,1280]{2,1,0:T(4,128)(2,1)S(1)} all-gather(bf16[1,4,1280]{2,1,0:T(4,128)(2,1)} %bitcast.22), channel_id=1, replica_groups=mesh['section'=8,'dp'=64] {'dp'}, dimensions={0}, use_global_device_ids=true | all-gather | bytes 665600 | tf_op jit(solution)/shard_map/all_gather | solution.py:81
  143.1 5.0 all-gather.5.cloned.1.call-done
  148.1 7.4 copy.14
  155.5 403.1 %while.17 = (s32[]{:T(128)}, bf16[128,1664]{1,0:T(8,128)(2,1)S(1)}, f32[4,1664]{1,0:T(4,128)S(1)}, s32[]{:T(128)}, pred[]{:T(512)}, /*index=5*/bf16[512,1664]{1,...) while((s32[]{:T(128)}, bf16[128,1664]{1,0:T(8,128)(2,1)S(1)}, ...), condition=%wide.region_9.10_spmd, body=%wide.region_0.9_spmd.sunk | while | flops 715230720 | bytes 13694302 | solution.py:65
  156.7 4.3 conditional.2
  164.5 17.8 collective-permute-done
  183.4 4.3 conditional.2
  187.8 13.1 collective-permute-start
  201.4 14.5 collective-permute-done
  217.0 4.3 conditional.2
  221.4 13.0 collective-permute-start
  235.0 25.1 %collective-permute-done = bf16[128,1664]{1,0:T(8,128)(2,1)S(1)} collective-permute-done((bf16[128,1664]{1,0:T(8,128)(2,1)S(1)}, bf16[128,1664]{1,0:T(8,128)(2,1)S(1)}, u32[]{:S(2)}, u32[]{:S(2)}) %collective-permute-start) | collective-permute-done | bytes 426016 | tf_op jit(solution)/shard_map/while/body/eval_jaxpr/ppermute | solution.py:10
  265.5 15.9 collective-permute-start
  282.0 13.8 collective-permute-done
  297.2 17.0 collective-permute-start
  314.8 22.5 %collective-permute-done = bf16[128,1664]{1,0:T(8,128)(2,1)S(1)} collective-permute-done((bf16[128,1664]{1,0:T(8,128)(2,1)S(1)}, bf16[128,1664]{1,0:T(8,128)(2,1)S(1)}, u32[]{:S(2)}, u32[]{:S(2)}) %collective-permute-start) | collective-permute-done | bytes 426016 | tf_op jit(solution)/shard_map/while/body/eval_jaxpr/ppermute | solution.py:10
  338.6 12.8 collective-permute-start
  352.0 16.7 collective-permute-done
  370.1 12.8 collective-permute-start
  383.5 27.6 %collective-permute-done = bf16[128,1664]{1,0:T(8,128)(2,1)S(1)} collective-permute-done((bf16[128,1664]{1,0:T(8,128)(2,1)S(1)}, bf16[128,1664]{1,0:T(8,128)(2,1)S(1)}, u32[]{:S(2)}, u32[]{:S(2)}) %collective-permute-start) | collective-permute-done | bytes 426016 | tf_op jit(solution)/shard_map/while/body/eval_jaxpr/ppermute | solution.py:10
  412.5 12.8 collective-permute-start
  425.9 16.4 collective-permute-done
  443.7 12.8 collective-permute-start
  457.2 27.6 %collective-permute-done = bf16[128,1664]{1,0:T(8,128)(2,1)S(1)} collective-permute-done((bf16[128,1664]{1,0:T(8,128)(2,1)S(1)}, bf16[128,1664]{1,0:T(8,128)(2,1)S(1)}, u32[]{:S(2)}, u32[]{:S(2)}) %collective-permute-start) | collective-permute-done | bytes 426016 | tf_op jit(solution)/shard_map/while/body/eval_jaxpr/ppermute | solution.py:10
  486.0 12.8 collective-permute-start
  499.5 16.5 collective-permute-done
  517.4 12.8 collective-permute-start
  530.8 27.8 %collective-permute-done = bf16[128,1664]{1,0:T(8,128)(2,1)S(1)} collective-permute-done((bf16[128,1664]{1,0:T(8,128)(2,1)S(1)}, bf16[128,1664]{1,0:T(8,128)(2,1)S(1)}, u32[]{:S(2)}, u32[]{:S(2)}) %collective-permute-start) | collective-permute-done | bytes 426016 | tf_op jit(solution)/shard_map/while/body/eval_jaxpr/ppermute | solution.py:10
  558.6 80.7 %psum.28 = bf16[4,1664]{1,0:T(4,128)(2,1)S(1)} all-reduce(bf16[4,1664]{1,0:T(4,128)(2,1)S(1)} %convert_select_fusion), channel_id=1, replica_groups=mesh['section'=8,'dp'=64] {'section'}, use_global_device_ids=true, to_apply=%region_10.11 | all-reduce | flops 6656 | bytes 26624 | tf_op jit(solution)/shard_map/psum | solution.py:15
  639.4 219.8 %all-gather.1 = bf16[64,4,1664]{2,1,0:T(4,128)(2,1)S(1)} all-gather(bf16[1,4,1664]{2,1,0:T(4,128)(2,1)S(1)} %bitcast.21), channel_id=1, replica_groups=mesh['section'=8,'dp'=64] {'dp'}, dimensions={0}, use_global_device_ids=true | all-gather | bytes 865280 | tf_op jit(solution)/shard_map/all_gather | solution.py:80
  859.7 209.9 %all-reduce = (f32[256]{0:T(256)S(1)}, f32[256]{0:T(256)S(1)}) all-reduce(f32[256]{0:T(256)S(1)} %get-tuple-element.239, f32[256]{0:T(256)S(1)} %get-tuple-element.241), channel_id=1, replica_groups=mesh['section'=8,'dp'=64] {'dp'}, use_global_device_ids=true, to_apply=%region_14.15 | all-reduce | flops 512 | bytes 4096 | tf_op jit(solution)/shard_map/psum | solution.py:88
  1071.3 769.2 %all-reduce.3.cloned.1.call-done = f32[256,256]{1,0:T(8,128)} async-done(((f32[256,256]{1,0:T(8,128)}), f32[256,256]{1,0:T(8,128)}) %all-reduce.3.cloned.1.call-update) | async-done | bytes 262160 | tf_op jit(solution)/shard_map/psum | solution.py:96
  (159 shorter events, 55.4 us)
Async XLA Ops:
  7.2 852.2 %copy-start = (bf16[1664,20]{0,1:T(8,128)(2,1)S(1)}, bf16[1664,20]{0,1:T(8,128)(2,1)}, u32[]{:S(2)}) copy-start(bf16[1664,20]{0,1:T(8,128)(2,1)} %param.14) | copy-start | bytes 199684
  7.2 140.9 %all-gather.5.cloned.1.call-start = ((), (), s32[]{:S(2)}) async-start(), calls=%async_computation.1 | async-start | bytes 11248640 | tf_op jit(solution)/shard_map/all_gather | solution.py:70
  9.0 1831.5 %all-reduce.3.cloned.1.call-start = ((), (), s32[]{:S(2)}) async-start(), calls=%async_computation | async-start | bytes 524288 | tf_op jit(solution)/shard_map/psum | solution.py:96
  161.0 21.3 %collective-permute-start = (bf16[128,1664]{1,0:T(8,128)(2,1)S(1)}, bf16[128,1664]{1,0:T(8,128)(2,1)S(1)}, u32[]{:S(2)}, u32[]{:S(2)}) collective-permute-start(bf16[128,1664]{1,0:T(8,128)(2,1)S(1)} %get-tuple-element.297), channel_id=1, source_target_pairs={{0,64},{64,128},{128,192},{192,256},{256,320},{320,384},{384,448},... | collective-permute-start | bytes 1277960 | tf_op jit(solution)/shard_map/while/body/eval_jaxpr/ppermute | solution.py:10
  187.8 28.1 %collective-permute-start = (bf16[128,1664]{1,0:T(8,128)(2,1)S(1)}, bf16[128,1664]{1,0:T(8,128)(2,1)S(1)}, u32[]{:S(2)}, u32[]{:S(2)}) collective-permute-start(bf16[128,1664]{1,0:T(8,128)(2,1)S(1)} %get-tuple-element.297), channel_id=1, source_target_pairs={{0,64},{64,128},{128,192},{192,256},{256,320},{320,384},{384,448},... | collective-permute-start | bytes 1277960 | tf_op jit(solution)/shard_map/while/body/eval_jaxpr/ppermute | solution.py:10
  221.4 38.7 %collective-permute-start = (bf16[128,1664]{1,0:T(8,128)(2,1)S(1)}, bf16[128,1664]{1,0:T(8,128)(2,1)S(1)}, u32[]{:S(2)}, u32[]{:S(2)}) collective-permute-start(bf16[128,1664]{1,0:T(8,128)(2,1)S(1)} %get-tuple-element.297), channel_id=1, source_target_pairs={{0,64},{64,128},{128,192},{192,256},{256,320},{320,384},{384,448},... | collective-permute-start | bytes 1277960 | tf_op jit(solution)/shard_map/while/body/eval_jaxpr/ppermute | solution.py:10
  265.5 30.4 %collective-permute-start = (bf16[128,1664]{1,0:T(8,128)(2,1)S(1)}, bf16[128,1664]{1,0:T(8,128)(2,1)S(1)}, u32[]{:S(2)}, u32[]{:S(2)}) collective-permute-start(bf16[128,1664]{1,0:T(8,128)(2,1)S(1)} %get-tuple-element.297), channel_id=1, source_target_pairs={{0,64},{64,128},{128,192},{192,256},{256,320},{320,384},{384,448},... | collective-permute-start | bytes 1277960 | tf_op jit(solution)/shard_map/while/body/eval_jaxpr/ppermute | solution.py:10
  297.2 40.1 %collective-permute-start = (bf16[128,1664]{1,0:T(8,128)(2,1)S(1)}, bf16[128,1664]{1,0:T(8,128)(2,1)S(1)}, u32[]{:S(2)}, u32[]{:S(2)}) collective-permute-start(bf16[128,1664]{1,0:T(8,128)(2,1)S(1)} %get-tuple-element.297), channel_id=1, source_target_pairs={{0,64},{64,128},{128,192},{192,256},{256,320},{320,384},{384,448},... | collective-permute-start | bytes 1277960 | tf_op jit(solution)/shard_map/while/body/eval_jaxpr/ppermute | solution.py:10
  338.6 30.2 %collective-permute-start = (bf16[128,1664]{1,0:T(8,128)(2,1)S(1)}, bf16[128,1664]{1,0:T(8,128)(2,1)S(1)}, u32[]{:S(2)}, u32[]{:S(2)}) collective-permute-start(bf16[128,1664]{1,0:T(8,128)(2,1)S(1)} %get-tuple-element.297), channel_id=1, source_target_pairs={{0,64},{64,128},{128,192},{192,256},{256,320},{320,384},{384,448},... | collective-permute-start | bytes 1277960 | tf_op jit(solution)/shard_map/while/body/eval_jaxpr/ppermute | solution.py:10
  370.1 41.1 %collective-permute-start = (bf16[128,1664]{1,0:T(8,128)(2,1)S(1)}, bf16[128,1664]{1,0:T(8,128)(2,1)S(1)}, u32[]{:S(2)}, u32[]{:S(2)}) collective-permute-start(bf16[128,1664]{1,0:T(8,128)(2,1)S(1)} %get-tuple-element.297), channel_id=1, source_target_pairs={{0,64},{64,128},{128,192},{192,256},{256,320},{320,384},{384,448},... | collective-permute-start | bytes 1277960 | tf_op jit(solution)/shard_map/while/body/eval_jaxpr/ppermute | solution.py:10
  412.5 29.9 %collective-permute-start = (bf16[128,1664]{1,0:T(8,128)(2,1)S(1)}, bf16[128,1664]{1,0:T(8,128)(2,1)S(1)}, u32[]{:S(2)}, u32[]{:S(2)}) collective-permute-start(bf16[128,1664]{1,0:T(8,128)(2,1)S(1)} %get-tuple-element.297), channel_id=1, source_target_pairs={{0,64},{64,128},{128,192},{192,256},{256,320},{320,384},{384,448},... | collective-permute-start | bytes 1277960 | tf_op jit(solution)/shard_map/while/body/eval_jaxpr/ppermute | solution.py:10
  443.7 41.0 %collective-permute-start = (bf16[128,1664]{1,0:T(8,128)(2,1)S(1)}, bf16[128,1664]{1,0:T(8,128)(2,1)S(1)}, u32[]{:S(2)}, u32[]{:S(2)}) collective-permute-start(bf16[128,1664]{1,0:T(8,128)(2,1)S(1)} %get-tuple-element.297), channel_id=1, source_target_pairs={{0,64},{64,128},{128,192},{192,256},{256,320},{320,384},{384,448},... | collective-permute-start | bytes 1277960 | tf_op jit(solution)/shard_map/while/body/eval_jaxpr/ppermute | solution.py:10
  486.0 30.0 %collective-permute-start = (bf16[128,1664]{1,0:T(8,128)(2,1)S(1)}, bf16[128,1664]{1,0:T(8,128)(2,1)S(1)}, u32[]{:S(2)}, u32[]{:S(2)}) collective-permute-start(bf16[128,1664]{1,0:T(8,128)(2,1)S(1)} %get-tuple-element.297), channel_id=1, source_target_pairs={{0,64},{64,128},{128,192},{192,256},{256,320},{320,384},{384,448},... | collective-permute-start | bytes 1277960 | tf_op jit(solution)/shard_map/while/body/eval_jaxpr/ppermute | solution.py:10
  517.4 41.2 %collective-permute-start = (bf16[128,1664]{1,0:T(8,128)(2,1)S(1)}, bf16[128,1664]{1,0:T(8,128)(2,1)S(1)}, u32[]{:S(2)}, u32[]{:S(2)}) collective-permute-start(bf16[128,1664]{1,0:T(8,128)(2,1)S(1)} %get-tuple-element.297), channel_id=1, source_target_pairs={{0,64},{64,128},{128,192},{192,256},{256,320},{320,384},{384,448},... | collective-permute-start | bytes 1277960 | tf_op jit(solution)/shard_map/while/body/eval_jaxpr/ppermute | solution.py:10
  558.6 1285.0 %copy-start.1 = (s32[256]{0:T(256)S(1)}, s32[256]{0:T(256)}, u32[]{:S(2)}) copy-start(s32[256]{0:T(256)} %param.17) | copy-start | bytes 3076
Sparse Core Ops, SparseCore 0:
  10.2 137.8 all-gather.4
  1070.7 769.7 all-reduce.2
where the time goes:
time: 1850 us
  waiting for transfers between devices  1000 us (54%)
  blocking collectives  642 us (35%)
  starting transfers between devices  139 us (8%)
  other arithmetic  23.5 us (1%)
    psum x1, waiting for transfers between devices, on_device(): logits_all = scale_value * lax.psum(partial_dots, 'dp')  769 us
    ppermute x11, waiting for transfers between devices, shifted(): lax.ppermute(value, axis, [(source, source + steps) for source in range(l...  226 us
    all_gather x1, blocking collectives, on_device(): lax.all_gather(pooled_image, 'dp', axis=0, tiled=True)  220 us
    psum x1, blocking collectives, on_device(): lax.psum((jnp.sum(image_part * image_part, axis=1), jnp.sum(text_part * t...  210 us
    ppermute x11, starting transfers between devices, shifted(): lax.ppermute(value, axis, [(source, source + steps) for source in range(l...  139 us
    all_gather x1, blocking collectives, on_device(): lax.all_gather(text_pooled, 'dp', axis=0, tiled=True)  131 us
    psum x1, blocking collectives, from_root(): return lax.psum(kept, axis)  80.7 us
  transfers between devices with their start and end apart: 13, of which 13 were waited for; matrix products, arithmetic and copies ran while one was open for 0% of the time, Pallas kernels for 0%

commit v1 on v0

v1 whole, which is shorter than its diff:
```python
import functools

import jax
import jax.numpy as jnp
from jax import lax
from jax.experimental import pallas as pl
from jax.experimental.pallas import tpu as pltpu
from jax.sharding import Mesh, PartitionSpec as P

AXES = ("y", "zh", "zl", "x", "c")
SIZES = (4, 2, 8, 4, 2)
CHIPS = ("y", "zh", "zl", "x")
Z = ("zh", "zl")
bf16, f32 = jnp.bfloat16, jnp.float32


def shift(value, axis, steps):
    count = lax.axis_size(axis)
    return lax.ppermute(value, axis, [(i, (i + steps) % count) for i in range(count)])


def swap(value):
    return lax.ppermute(value, "c", [(0, 1), (1, 0)])


def normalize(values):
    values = values.astype(f32)
    center = jnp.mean(values, axis=-1, keepdims=True)
    spread = jnp.mean((values - center) ** 2, axis=-1, keepdims=True)
    return (values - center) / jnp.sqrt(spread + 1e-05)


def feature_order(rows, head):
    width = rows * 64
    tail = rows - head
    natural = lax.broadcasted_iota(jnp.int32, (width, 1), 0)
    row = natural % rows
    core = (natural // rows) % 2
    x = (natural // (rows * 2)) % 4
    zl = natural // (rows * 8)
    first = (x * 2 + core) * (8 * head) + zl * head + row
    second = 64 * head + zl * (8 * tail) + (core * 4 + x) * tail + row - head
    place = jnp.where(row < head, first, second)
    return (place == lax.broadcasted_iota(jnp.int32, (1, width), 1)).astype(bf16)


def place_of(x, y, ox, oy, head):
    from_x, from_y = (x + ox) % 4, (y + oy) % 4
    return from_y % 2, (from_x * 2 + from_y // 2) * (8 * head)


def tower_kernel(head, tail, place_ref, act_ref, *refs):
    by_y, by_x, ring, out_ref, pooled_ref, weight, normed, sems = (
        refs[0:5], refs[5:10], refs[10], refs[11], refs[12], refs[13], refs[14], refs[15]
    )
    x, y = place_ref[0], place_ref[1]
    rows = 8 * head
    width = act_ref.shape[1]

    def fetch(source, layer, first, count):
        pltpu.make_async_copy(
            source, weight.at[layer, pl.ds(pl.multiple_of(first, 16), count), :], sems.at[layer]
        ).start()

    for zh in range(2):
        for pair in range(2):
            for zl in range(8):
                fetch(
                    ring.at[zh * 8 + zl, pl.ds(pair * 8 * tail, 8 * tail), :],
                    2 * pair + zh, 8 * rows + zl * 8 * tail, 8 * tail,
                )
        own, one, two_a, two_b, three = by_y if zh == 0 else by_x
        for outer in range(4):
            for inner in range(4):
                source = (
                    own.at[inner], one.at[inner],
                    two_a.at[inner] if inner < 2 else two_b.at[inner - 2], three.at[inner],
                )[outer]
                ox, oy = (inner, outer) if zh == 0 else (outer, inner)
                pair, first = place_of(x, y, ox, oy, head)
                fetch(source, 2 * pair + zh, first, rows)

    out_ref[...] = act_ref[...]

    def layer_step(layer, carry):
        normed[...] = normalize(out_ref[...]).astype(bf16)
        pltpu.make_async_copy(weight.at[layer], weight.at[layer], sems.at[layer]).wait()
        for start in range(0, width, 256):
            cols = pl.ds(start, min(256, width - start))
            update = jnp.dot(normed[...], weight[layer, :, cols], preferred_element_type=f32)
            out_ref[:, cols] = (out_ref[:, cols].astype(f32) + jax.nn.gelu(update)).astype(bf16)
        return carry

    lax.fori_loop(0, 4, layer_step, 0)
    pooled_ref[...] = jnp.mean(normalize(out_ref[...]), axis=0, keepdims=True)


def tower(act, pieces, place, head, tail):
    tokens, width = act.shape
    vmem, anywhere = pl.BlockSpec(memory_space=pltpu.VMEM), pl.BlockSpec(memory_space=pl.ANY)
    return pl.pallas_call(
        functools.partial(tower_kernel, head, tail),
        out_shape=(
            jax.ShapeDtypeStruct((tokens, width), bf16),
            jax.ShapeDtypeStruct((1, width), f32),
        ),
        in_specs=[pl.BlockSpec(memory_space=pltpu.SMEM), vmem] + [anywhere] * 11,
        out_specs=(vmem, vmem),
        scratch_shapes=[
            pltpu.VMEM((4, width, width), bf16),
            pltpu.VMEM((tokens, width), bf16),
            pltpu.SemaphoreType.DMA((4,)),
        ],
        compiler_params=pltpu.CompilerParams(vmem_limit_bytes=40 * 1024 * 1024),
        cost_estimate=pl.CostEstimate(
            flops=8 * tokens * width * width, bytes_accessed=8 * width * width, transcendentals=0
        ),
    )(place, act, *pieces)


def gather_plane(block, axis_one, axis_two):
    near = (block, shift(block, axis_one, -1), shift(block, axis_one, 2), shift(block, axis_one, 1))
    stack = jnp.stack(near)
    one, three = shift(stack, axis_two, -1), shift(stack, axis_two, 1)
    two_a, two_b = shift(one[:2], axis_two, -1), shift(three[2:], axis_two, 1)
    return stack, one, two_a, two_b, three


def gather_ring(block, position):
    near = {0: block}
    for ahead in (4, 8, 12):
        near[ahead] = shift(block, Z, -ahead)
    stack = jnp.stack([near[ahead] for ahead in (0, 4, 8, 12)])
    one, three = shift(stack, Z, -1), shift(stack, Z, 1)
    two_a = shift(jnp.stack([near[0], near[4]]), Z, -2)
    two_b = shift(jnp.stack([near[0], near[12]]), Z, 2)
    ahead = {}
    for k in range(4):
        ahead[4 * k] = stack[k]
        ahead[4 * k + 1] = one[k]
        ahead[(4 * k + 15) % 16] = three[k]
    ahead[2], ahead[6], ahead[14], ahead[10] = two_a[0], two_a[1], two_b[0], two_b[1]
    line = jnp.stack([ahead[k % 16] for k in range(32)])
    return lax.dynamic_slice_in_dim(line, (16 - position) % 16, 16, 0)


def on_device(images, text_pooled, image_weight, proj_image, proj_text, logit_scale, pairing):
    y, zh, zl, x, c = (lax.axis_index(name) for name in AXES)
    rows = image_weight.shape[1]
    width, text_width = proj_image.shape[0], proj_text.shape[0]
    micro = images.shape[0]
    head = 18 if rows == 26 else rows // 2
    tail = rows - head
    share = proj_image.shape[1] // 4
    section = y * 2 + zh
    within = section % 4
    at_home = (y // 2) == c

    order = feature_order(rows, head)

    def ordered(values):
        return jnp.dot(values, order, preferred_element_type=f32).astype(bf16)

    weight = ordered(image_weight[0])
    crossing = [(p * 2 + 1, (p + 2) * 2) for p in (0, 1)] + [(p * 2, (p - 2) * 2 + 1) for p in (2, 3)]
    weight = jnp.where(at_home, weight, lax.ppermute(weight, ("y", "c"), crossing))

    def share_of(projection):
        return lax.dynamic_slice_in_dim(projection, within * share, share, 1).T

    text_row = lax.dynamic_slice_in_dim(text_pooled, within, 1, 0)
    widen = ((0, 0), (0, width - text_width))
    text_rows = jnp.pad(jnp.concatenate([share_of(proj_text), text_row]), widen)
    image_rows = jnp.pad(ordered(share_of(proj_image)), ((0, 1), (0, 0)))
    first_core = c == 0
    extra = jnp.where(
        at_home,
        jnp.where(first_core, text_rows, image_rows),
        swap(jnp.where(first_core, image_rows, text_rows)),
    )
    image = ordered(lax.dynamic_index_in_dim(images, within, 0, False))
    image = jnp.where(at_home, image, swap(image))

    small = jnp.concatenate([weight[head:], extra])
    spread = lax.all_to_all(
        jnp.broadcast_to(small[None], (16,) + small.shape), ("y", "x"), 0, 0, tiled=True
    )
    weight_part = spread[:, :tail].reshape(2, 2, 4, tail, width).transpose(1, 0, 2, 3, 4)
    plane_rows = jnp.concatenate([
        weight_part.reshape(16 * tail, width),
        spread[:, tail:tail + share].reshape(16 * share, width),
        spread[:, tail + share],
    ])
    ring = lax.all_gather(plane_rows, Z, axis=0)

    column = gather_ring(weight[:head], zh * 8 + zl).reshape(2, 8 * head, width)
    by_y = gather_plane(column[0], "x", "y")
    by_x = gather_plane(column[1], "y", "x")
    pieces = (*by_y, *by_x, ring)

    contract = (((1,), (1,)), ((), ()))
    projection = ring[:, 16 * tail:16 * (tail + share)].reshape(256 * share, width)
    texts = ring[:, 16 * (tail + share):, :text_width].reshape(2, 8, 2, 2, 4, text_width)
    texts = texts.transpose(1, 4, 2, 3, 0, 5).reshape(256, text_width)
    text_emb = lax.dot_general(texts, projection[:, :text_width], contract, preferred_element_type=f32)
    text_square = jnp.sum(text_emb * text_emb, axis=1, keepdims=True)
    text_unit = swap((text_emb / jnp.sqrt(text_square + 1e-06)).astype(bf16))

    place = jnp.stack([x, y]).astype(jnp.int32)
    act, _ = tower(image, pieces, place, head, tail)
    _, pooled = tower(swap(act), pieces, place, head, tail)
    image_emb = lax.dot_general(pooled.astype(bf16), projection, contract, preferred_element_type=f32)
    image_square = jnp.sum(image_emb * image_emb, axis=1, keepdims=True)
    image_unit = (image_emb / jnp.sqrt(image_square + 1e-06)).astype(bf16)
    row = logit_scale[0] * lax.dot_general(image_unit, text_unit, contract, preferred_element_type=f32)
    row = jnp.where(first_core, swap(row), row)

    count = row.shape[1]
    logits = lax.all_to_all(jnp.broadcast_to(row[None], (256, 1, count)), CHIPS, 0, 0, tiled=True)
    logits = logits.reshape(2, 2, 2, 8, 4, count).transpose(3, 4, 0, 1, 2, 5).reshape(256, count)
    row_start = ((zl * 4 + x) * 2 + c) * micro
    own_logits = lax.dynamic_slice_in_dim(logits, row_start, micro, 0)
    column_lse = jnp.log(jnp.sum(jnp.exp(logits), axis=0))
    own_pairs = lax.dynamic_slice_in_dim(pairing, row_start, micro, 0)
    paired = own_pairs[:, None] == lax.broadcasted_iota(jnp.int32, (1, count), 1)
    positive = jnp.sum(jnp.where(paired, own_logits, 0.0), axis=1)
    image_loss = jnp.log(jnp.sum(jnp.exp(own_logits), axis=1)) - positive
    text_loss = jnp.sum(jnp.where(paired, column_lse[None, :], 0.0), axis=1) - positive
    columns = count // 8
    logit_block = lax.dynamic_slice_in_dim(own_logits, section * columns, columns, 1)
    return (logit_block, image_loss, text_loss)


def solution(mesh):
    fine = Mesh(mesh.devices.reshape(SIZES), AXES)
    section, dp = ("y", "zh"), ("zl", "x", "c")
    in_specs = (
        P(dp, None, None),
        P(dp, None),
        P(section, dp, None),
        P(None, dp),
        P(None, dp),
        P(),
        P(),
    )
    out_specs = (P(dp, section), P(dp), P(dp))
    return jax.shard_map(on_device, mesh=fine, in_specs=in_specs, out_specs=out_specs, check_vma=False)
```

time: 1850 us -> 333 us (0.18)
  waiting for transfers between devices: 1000 us -> 95.9 us
  blocking collectives: 642 us -> 17.4 us
  Pallas kernels: 0 us -> 28.4 us
    psum x1 -> x0, waiting for transfers between devices: 769 us -> none  [on_device(): logits_all = scale_value * lax.psum(partial_dots, 'dp')]
    all_gather x2 -> x0, blocking collectives: 351 us -> none  [the longest x1 220 us: on_device(): lax.all_gather(pooled_image, 'dp', axis=0, tiled=True)]
    psum x2 -> x0, blocking collectives: 291 us -> none  [the longest x1 210 us: on_device(): lax.psum((jnp.sum(image_part * image_part, axis=1), jnp.sum(text_part * t...]
    ppermute x11 -> x27, waiting for transfers between devices: 226 us -> 72.5 us  [the longest x21 65.4 us: shift(): lax.ppermute(value, axis, [(i, (i + steps) % count) for i in range(count)])]
    ppermute x11 -> x27, starting transfers between devices: 139 us -> 105 us  [the longest x21 78 us: shift(): lax.ppermute(value, axis, [(i, (i + steps) % count) for i in range(count)])]
    pallas_call x0 -> x2, Pallas kernels: none -> 28.4 us  [tower(): pl.pallas_call(functools.partial(tower_kernel, head, tail), out_shape=(ja...]
    all_to_all x0 -> x1, waiting for transfers between devices: none -> 23.4 us  [on_device(): lax.all_to_all(jnp.broadcast_to(row[None], (256, 1, count)), CHIPS, 0, 0,...]
  transfers between devices with their start and end apart: 13 -> 29, of which waited for: 13 -> 12; matrix products, arithmetic and copies ran while one was open for 0% -> 11% of each run, Pallas kernels for 0% -> 4%
where the time goes in v1:
time: 333 us; the launch traced here: 332 us
  starting transfers between devices  121 us (36%)
  waiting for transfers between devices  95.9 us (29%)
  local copies, waits for them, and re-layouts  30 us (9%)
  Pallas kernels  28.4 us (9%)
  blocking collectives  17.4 us (5%)
  between operations  16.4 us (5%)
  matrix products  13.5 us (4%)
  other arithmetic  9.65 us (3%)
    ppermute x21, starting transfers between devices, shift(): lax.ppermute(value, axis, [(i, (i + steps) % count) for i in range(count)])  78 us
    ppermute x21, waiting for transfers between devices, shift(): lax.ppermute(value, axis, [(i, (i + steps) % count) for i in range(count)])  65.4 us
    pallas_call x2, Pallas kernels, tower(): pl.pallas_call(functools.partial(tower_kernel, head, tail), out_shape=(ja...  28.4 us
    ppermute x5, starting transfers between devices, swap(): return lax.ppermute(value, 'c', [(0, 1), (1, 0)])  24.9 us
    all_to_all x1, waiting for transfers between devices, on_device(): lax.all_to_all(jnp.broadcast_to(row[None], (256, 1, count)), CHIPS, 0, 0,...  23.4 us
    all_to_all x1, blocking collectives, on_device(): lax.all_to_all(jnp.broadcast_to(small[None], (16,) + small.shape), ('y',...  17.4 us
    all_to_all x1, starting transfers between devices, on_device(): lax.all_to_all(jnp.broadcast_to(row[None], (256, 1, count)), CHIPS, 0, 0,...  15.8 us
    dot_general x3, matrix products, ordered(): return jnp.dot(values, order, preferred_element_type=f32).astype(bf16)  7.56 us
  transfers between devices with their start and end apart: 29, of which 12 were waited for; matrix products, arithmetic and copies ran while one was open for 11% of the time, Pallas kernels for 4%

profile of v1, /device:TPU:1, one launch (start us, length us, event | category | flops | bytes accessed | tf_op | source)
XLA Modules:
  0.0 331.9 jit_solution(4331718961409055992)
XLA Ops:
  8.9 2.9 fusion.11
  11.9 8.8 %collective-permute-start.23 = (bf16[6,1664]{1,0:T(8,128)(2,1)S(1)}, bf16[6,1664]{1,0:T(8,128)(2,1)S(1)}, u32[]{:S(2)}, u32[]{:S(2)}) collective-permute-start(bf16[6,1664]{1,0:T(8,128)(2,1)S(1)} %broadcast_select_fusion.2), channel_id=1, source_target_pairs={{0,1},{1,0},{2,3},{3,2},{4,5},{5,4},{6,7},{7,6},{8,9},{9,8},{10,11... | collective-permute-start | bytes 59912 | tf_op jit(solution)/shard_map/ppermute | solution.py:23
  24.8 5.5 %collective-permute-done.1 = bf16[26,1664]{1,0:T(8,128)(2,1)S(1)} collective-permute-done((bf16[26,1664]{1,0:T(8,128)(2,1)S(1)}, bf16[26,1664]{1,0:T(8,128)(2,1)S(1)}, u32[]{:S(2)}, u32[]{:S(2)}) %collective-permute-start.1) | collective-permute-done | bytes 86560 | tf_op jit(solution)/shard_map/ppermute | solution.py:166
  30.5 17.4 %all_to_all.10 = bf16[16,14,1664]{2,1,0:T(8,128)(2,1)S(1)} all-to-all(bf16[16,14,1664]{2,1,0:T(8,128)(2,1)S(1)} %broadcast_in_dim.16), channel_id=1, replica_groups=mesh['y'=4,'zh'=2,'zl'=8,'x'=4,'c'=2] {'y','x'}, dimensions={0} | all-to-all | bytes 1490944 | tf_op jit(solution)/shard_map/all_to_all | solution.py:185
  50.9 7.8 %collective-permute-start.2 = (bf16[18,1664]{1,0:T(8,128)(2,1)S(1)}, bf16[18,1664]{1,0:T(8,128)(2,1)S(1)}, u32[]{:S(2)}, u32[]{:S(2)}) collective-permute-start(bf16[18,1664]{1,0:T(8,128)(2,1)S(1)} %get-tuple-element.13), channel_id=1, source_target_pairs={{0,96},{8,104},{16,112},{24,120},{32,0},{40,8},{48,16},{56,24},{64... | collective-permute-start | bytes 179720 | tf_op jit(solution)/shard_map/ppermute | solution.py:19
  60.6 10.3 %collective-permute-start.3 = (bf16[18,1664]{1,0:T(8,128)(2,1)S(1)}, bf16[18,1664]{1,0:T(8,128)(2,1)S(1)}, u32[]{:S(2)}, u32[]{:S(2)}) collective-permute-start(bf16[18,1664]{1,0:T(8,128)(2,1)S(1)} %get-tuple-element.13), channel_id=1, source_target_pairs={{0,64},{8,72},{16,80},{24,88},{32,96},{40,104},{48,112},{56,120},{... | collective-permute-start | bytes 179720 | tf_op jit(solution)/shard_map/ppermute | solution.py:19
  70.9 6.1 %collective-permute-done.3 = bf16[18,1664]{1,0:T(8,128)(2,1)S(1)} collective-permute-done((bf16[18,1664]{1,0:T(8,128)(2,1)S(1)}, bf16[18,1664]{1,0:T(8,128)(2,1)S(1)}, u32[]{:S(2)}, u32[]{:S(2)}) %collective-permute-start.3) | collective-permute-done | bytes 59936 | tf_op jit(solution)/shard_map/ppermute | solution.py:19
  77.1 7.7 %collective-permute-start.5 = (bf16[4,18,1664]{2,1,0:T(8,128)(2,1)S(1)}, bf16[4,18,1664]{2,1,0:T(8,128)(2,1)S(1)}, u32[]{:S(2)}, u32[]{:S(2)}) collective-permute-start(bf16[4,18,1664]{2,1,0:T(8,128)(2,1)S(1)} %pad_maximum_fusion.3), channel_id=1, source_target_pairs={{0,120},{8,0},{16,8},{24,16},{32,24},{40,32},{48,40},{56,48},{64,5... | collective-permute-start | bytes 718856 | tf_op jit(solution)/shard_map/ppermute | solution.py:19
  86.7 4.8 %collective-permute-start.6 = (bf16[2,18,1664]{2,1,0:T(8,128)(2,1)S(1)}, bf16[2,18,1664]{2,1,0:T(8,128)(2,1)S(1)}, u32[]{:S(2)}, u32[]{:S(2)}) collective-permute-start(bf16[2,18,1664]{2,1,0:T(8,128)(2,1)S(1)} %get-tuple-element.15), channel_id=1, source_target_pairs={{0,112},{8,120},{16,0},{24,8},{32,16},{40,24},{48,32},{56,40},{64,... | collective-permute-start | bytes 359432 | tf_op jit(solution)/shard_map/ppermute | solution.py:19
  93.5 3.6 %collective-permute-done.5 = bf16[4,18,1664]{2,1,0:T(8,128)(2,1)S(1)} collective-permute-done((bf16[4,18,1664]{2,1,0:T(8,128)(2,1)S(1)}, bf16[4,18,1664]{2,1,0:T(8,128)(2,1)S(1)}, u32[]{:S(2)}, u32[]{:S(2)}) %collective-permute-start.5) | collective-permute-done | bytes 239648 | tf_op jit(solution)/shard_map/ppermute | solution.py:19
  97.1 9.9 %collective-permute-done.6 = bf16[2,18,1664]{2,1,0:T(8,128)(2,1)S(1)} collective-permute-done((bf16[2,18,1664]{2,1,0:T(8,128)(2,1)S(1)}, bf16[2,18,1664]{2,1,0:T(8,128)(2,1)S(1)}, u32[]{:S(2)}, u32[]{:S(2)}) %collective-permute-start.6) | collective-permute-done | bytes 119840 | tf_op jit(solution)/shard_map/ppermute | solution.py:19
  107.2 4.0 %collective-permute-done.8 = bf16[2,18,1664]{2,1,0:T(8,128)(2,1)S(1)} collective-permute-done((bf16[2,18,1664]{2,1,0:T(8,128)(2,1)S(1)}, bf16[2,18,1664]{2,1,0:T(8,128)(2,1)S(1)}, u32[]{:S(2)}, u32[]{:S(2)}) %collective-permute-start.8) | collective-permute-done | bytes 119840 | tf_op jit(solution)/shard_map/ppermute | solution.py:19
  112.6 3.3 collective-permute-start.16
  115.9 2.8 collective-permute-start.17
  121.9 3.7 %collective-permute-start.9 = (bf16[144,1664]{1,0:T(8,128)(2,1)}, bf16[144,1664]{1,0:T(8,128)(2,1)}, u32[]{:S(2)}, u32[]{:S(2)}) collective-permute-start(bf16[144,1664]{1,0:T(8,128)(2,1)} %squeeze.22), channel_id=1, source_target_pairs={{0,6},{2,0},{4,2},{6,4},{1,7},{3,1},{5,3},{7,5},{8,14},{10,8},{12,... | collective-permute-start | bytes 1437704 | tf_op jit(solution)/shard_map/ppermute | solution.py:19
  131.2 8.8 %collective-permute-done.18 = bf16[144,1664]{1,0:T(8,128)(2,1)} collective-permute-done((bf16[144,1664]{1,0:T(8,128)(2,1)}, bf16[144,1664]{1,0:T(8,128)(2,1)}, u32[]{:S(2)}, u32[]{:S(2)}) %collective-permute-start.18) | collective-permute-done | bytes 479264 | tf_op jit(solution)/shard_map/ppermute | solution.py:19
  141.6 4.9 %collective-permute-start.19 = (bf16[4,144,1664]{2,1,0:T(8,128)(2,1)S(1)}, bf16[4,144,1664]{2,1,0:T(8,128)(2,1)S(1)}, u32[]{:S(2)}, u32[]{:S(2)}) collective-permute-start(bf16[4,144,1664]{2,1,0:T(8,128)(2,1)S(1)} %pad_maximum_fusion.1.refs_5_), channel_id=1, source_target_pairs={{0,6},{2,0},{4,2},{6,4},{1,7},{3,1},{5,3},{7,5},{8,14},{10,8},{12,... | collective-permute-start | bytes 5750792 | tf_op jit(solution)/shard_map/ppermute | solution.py:19
  153.7 3.3 collective-permute-start.14
  157.0 29.1 %collective-permute-done.19.refs_6_ = bf16[4,144,1664]{2,1,0:T(8,128)(2,1)S(1)} collective-permute-done((bf16[4,144,1664]{2,1,0:T(8,128)(2,1)S(1)}, bf16[4,144,1664]{2,1,0:T(8,128)(2,1)S(1)}, u32[]{:S(2)}, u32[]{:S(2)}) %collective-permute-start.19) | collective-permute-done | bytes 1916960 | tf_op jit(solution)/shard_map/ppermute | solution.py:19
  187.1 5.4 %collective-permute-start.20 = (bf16[2,144,1664]{2,1,0:T(8,128)(2,1)}, bf16[2,144,1664]{2,1,0:T(8,128)(2,1)S(1)}, u32[]{:S(2)}, u32[]{:S(2)}) collective-permute-start(bf16[2,144,1664]{2,1,0:T(8,128)(2,1)} %slice.127), channel_id=1, source_target_pairs={{0,6},{2,0},{4,2},{6,4},{1,7},{3,1},{5,3},{7,5},{8,14},{10,8},{12,... | collective-permute-start | bytes 2875400 | tf_op jit(solution)/shard_map/ppermute | solution.py:19
  196.8 3.7 %collective-permute-start.13 = (bf16[2,144,1664]{2,1,0:T(8,128)(2,1)}, bf16[2,144,1664]{2,1,0:T(8,128)(2,1)}, u32[]{:S(2)}, u32[]{:S(2)}) collective-permute-start(bf16[2,144,1664]{2,1,0:T(8,128)(2,1)} %slice.125), channel_id=1, source_target_pairs={{0,384},{128,0},{256,128},{384,256},{1,385},{129,1},{257,129},{385... | collective-permute-start | bytes 2875400 | tf_op jit(solution)/shard_map/ppermute | solution.py:19
  206.7 5.4 %collective-permute-start = (bf16[128,1664]{1,0:T(8,128)(2,1)S(1)}, bf16[128,1664]{1,0:T(8,128)(2,1)}, u32[]{:S(2)}, u32[]{:S(2)}) collective-permute-start(bf16[128,1664]{1,0:T(8,128)(2,1)S(1)} %fusion.8), channel_id=1, source_target_pairs={{0,1},{1,0},{2,3},{3,2},{4,5},{5,4},{6,7},{7,6},{8,9},{9,8},{10,11... | collective-permute-start | bytes 1277960 | tf_op jit(solution)/shard_map/ppermute | solution.py:23
  214.8 4.8 %slice.133 = bf16[16,80,1664]{2,1,0:T(8,128)(2,1)} slice(bf16[16,224,1664]{2,1,0:T(8,128)(2,1)} %bitcast.57), slice={[0:16], [128:208], [0:1664]} | slice | bytes 8519680 | tf_op jit(solution)/shard_map/slice | solution.py:202
  219.7 2.7 slice.134
  224.8 14.3 %shard_map.94 = (bf16[128,1664]{1,0:T(8,128)(2,1)S(1)}, f32[1,1664]{1,0:T(1,128)}) custom-call(s32[2]{0:T(128)S(1)} %pad_add_fusion.place_ref, bf16[128,1664]{1,0:T(8,128)(2,1)S(1)} %broadcast_select_fusion.act_ref, bf16[4,144,1664]{2,1,0:T(8,128)(2,1)S(1)} %copy-done.5, bf16[4,144,1664]{2,1,0:T(8,128)(2,1)S(1)} %copy-done.11, ...), custom_call_target="tpu_custom_call" | custom-call | flops 2835349504 | bytes 22151168 | tf_op jit(solution)/shard_map/pallas_call | solution.py:101
  239.1 6.3 %collective-permute-start.24 = (bf16[128,1664]{1,0:T(8,128)(2,1)S(1)}, bf16[128,1664]{1,0:T(8,128)(2,1)S(1)}, u32[]{:S(2)}, u32[]{:S(2)}) collective-permute-start(bf16[128,1664]{1,0:T(8,128)(2,1)S(1)} %get-tuple-element.5), channel_id=1, source_target_pairs={{0,1},{1,0},{2,3},{3,2},{4,5},{5,4},{6,7},{7,6},{8,9},{9,8},{10,11... | collective-permute-start | bytes 1277960 | tf_op jit(solution)/shard_map/ppermute | solution.py:23
  247.7 2.6 copy.25
  250.4 2.7 reshape.208
  253.1 3.4 %multiply_reduce_fusion = (f32[256]{0:T(256)S(1)}, f32[256,1280]{1,0:T(8,128)S(1)}) fusion(bf16[256,1280]{1,0:T(8,128)(2,1)} %reshape.208, bf16[1280,1664]{1,0:T(8,128)(2,1)} %bitcast.61), kind=kOutput, calls=%fused_computation.16 | convolution fusion | flops 839515904 | bytes 5243904 | tf_op jit(solution)/shard_map/dot_general | solution.py:205
  261.0 14.1 %shard_map.95 = (bf16[128,1664]{1,0:T(8,128)(2,1)}, f32[1,1664]{1,0:T(1,128)S(1)}) custom-call(s32[2]{0:T(128)S(1)} %pad_add_fusion.place_ref, bf16[128,1664]{1,0:T(8,128)(2,1)S(1)} %collective-permute-done.24.act_ref, bf16[4,144,1664]{2,1,0:T(8,128)(2,1)S(1)} %copy-done.6, bf16[4,144,1664]{2,1,0:T(8,128)(2,1)S(1)} %copy-done.12, ...), custom_call_target="tpu_custom_call" | custom-call | flops 2835349504 | bytes 22151168 | tf_op jit(solution)/shard_map/pallas_call | solution.py:101
  283.2 15.8 %all-to-all-start.1 = ((f32[256,1,256]{2,1,0:T(1,128)}), f32[256,1,256]{2,1,0:T(1,128)S(1)}, u32[]{:S(2)}, u32[]{:S(2)}) async-start(f32[256,1,256]{2,1,0:T(1,128)} %broadcast_in_dim.34), calls=%async_computation.1 | async-start | bytes 524288 | tf_op jit(solution)/shard_map/all_to_all | solution.py:219
  299.1 23.4 %all-to-all-done.1 = f32[256,1,256]{2,1,0:T(1,128)S(1)} async-done(((f32[256,1,256]{2,1,0:T(1,128)}), f32[256,1,256]{2,1,0:T(1,128)S(1)}, u32[]{:S(2)}, u32[]{:S(2)}) %all-to-all-start.1) | async-done | bytes 262176 | tf_op jit(solution)/shard_map/all_to_all | solution.py:219
  (165 shorter events, 66.2 us)
Async XLA Ops:
  7.2 197.0 %copy-start = (bf16[4,128,1664]{2,1,0:T(8,128)(2,1)S(1)}, bf16[4,128,1664]{2,1,0:T(8,128)(2,1)}, u32[]{:S(2)}) copy-start(bf16[4,128,1664]{2,1,0:T(8,128)(2,1)} %param.7) | copy-start | bytes 5111812
  7.2 207.6 %all-gather.3.cloned.1.call-start = ((), (), s32[]{:S(2)}) async-start(), calls=%async_computation.2 | async-start | bytes 12673024 | tf_op jit(solution)/shard_map/all_gather | solution.py:194
  11.9 12.9 %collective-permute-start.23 = (bf16[6,1664]{1,0:T(8,128)(2,1)S(1)}, bf16[6,1664]{1,0:T(8,128)(2,1)S(1)}, u32[]{:S(2)}, u32[]{:S(2)}) collective-permute-start(bf16[6,1664]{1,0:T(8,128)(2,1)S(1)} %broadcast_select_fusion.2), channel_id=1, source_target_pairs={{0,1},{1,0},{2,3},{3,2},{4,5},{5,4},{6,7},{7,6},{8,9},{9,8},{10,11... | collective-permute-start | bytes 59912 | tf_op jit(solution)/shard_map/ppermute | solution.py:23
  22.8 7.5 %collective-permute-start.1 = (bf16[26,1664]{1,0:T(8,128)(2,1)S(1)}, bf16[26,1664]{1,0:T(8,128)(2,1)S(1)}, u32[]{:S(2)}, u32[]{:S(2)}) collective-permute-start(bf16[26,1664]{1,0:T(8,128)(2,1)S(1)} %fusion.10), channel_id=1, source_target_pairs={{1,256},{129,384},{256,1},{384,129},{3,258},{131,386},{258,3},{386... | collective-permute-start | bytes 259592 | tf_op jit(solution)/shard_map/ppermute | solution.py:166
  50.9 20.0 %collective-permute-start.2 = (bf16[18,1664]{1,0:T(8,128)(2,1)S(1)}, bf16[18,1664]{1,0:T(8,128)(2,1)S(1)}, u32[]{:S(2)}, u32[]{:S(2)}) collective-permute-start(bf16[18,1664]{1,0:T(8,128)(2,1)S(1)} %get-tuple-element.13), channel_id=1, source_target_pairs={{0,96},{8,104},{16,112},{24,120},{32,0},{40,8},{48,16},{56,24},{64... | collective-permute-start | bytes 179720 | tf_op jit(solution)/shard_map/ppermute | solution.py:19
  58.7 12.2 %collective-permute-start.4 = (bf16[18,1664]{1,0:T(8,128)(2,1)S(1)}, bf16[18,1664]{1,0:T(8,128)(2,1)S(1)}, u32[]{:S(2)}, u32[]{:S(2)}) collective-permute-start(bf16[18,1664]{1,0:T(8,128)(2,1)S(1)} %get-tuple-element.13), channel_id=1, source_target_pairs={{0,32},{8,40},{16,48},{24,56},{32,64},{40,72},{48,80},{56,88},{64,... | collective-permute-start | bytes 179720 | tf_op jit(solution)/shard_map/ppermute | solution.py:19
  60.6 16.4 %collective-permute-start.3 = (bf16[18,1664]{1,0:T(8,128)(2,1)S(1)}, bf16[18,1664]{1,0:T(8,128)(2,1)S(1)}, u32[]{:S(2)}, u32[]{:S(2)}) collective-permute-start(bf16[18,1664]{1,0:T(8,128)(2,1)S(1)} %get-tuple-element.13), channel_id=1, source_target_pairs={{0,64},{8,72},{16,80},{24,88},{32,96},{40,104},{48,112},{56,120},{... | collective-permute-start | bytes 179720 | tf_op jit(solution)/shard_map/ppermute | solution.py:19
  77.1 20.1 %collective-permute-start.5 = (bf16[4,18,1664]{2,1,0:T(8,128)(2,1)S(1)}, bf16[4,18,1664]{2,1,0:T(8,128)(2,1)S(1)}, u32[]{:S(2)}, u32[]{:S(2)}) collective-permute-start(bf16[4,18,1664]{2,1,0:T(8,128)(2,1)S(1)} %pad_maximum_fusion.3), channel_id=1, source_target_pairs={{0,120},{8,0},{16,8},{24,16},{32,24},{40,32},{48,40},{56,48},{64,5... | collective-permute-start | bytes 718856 | tf_op jit(solution)/shard_map/ppermute | solution.py:19
  84.8 22.3 %collective-permute-start.7 = (bf16[4,18,1664]{2,1,0:T(8,128)(2,1)S(1)}, bf16[4,18,1664]{2,1,0:T(8,128)(2,1)S(1)}, u32[]{:S(2)}, u32[]{:S(2)}) collective-permute-start(bf16[4,18,1664]{2,1,0:T(8,128)(2,1)S(1)} %pad_maximum_fusion.3), channel_id=1, source_target_pairs={{0,8},{8,16},{16,24},{24,32},{32,40},{40,48},{48,56},{56,64},{64,7... | collective-permute-start | bytes 718856 | tf_op jit(solution)/shard_map/ppermute | solution.py:19
  86.7 20.3 %collective-permute-start.6 = (bf16[2,18,1664]{2,1,0:T(8,128)(2,1)S(1)}, bf16[2,18,1664]{2,1,0:T(8,128)(2,1)S(1)}, u32[]{:S(2)}, u32[]{:S(2)}) collective-permute-start(bf16[2,18,1664]{2,1,0:T(8,128)(2,1)S(1)} %get-tuple-element.15), channel_id=1, source_target_pairs={{0,112},{8,120},{16,0},{24,8},{32,16},{40,24},{48,32},{56,40},{64,... | collective-permute-start | bytes 359432 | tf_op jit(solution)/shard_map/ppermute | solution.py:19
  91.6 19.6 %collective-permute-start.8 = (bf16[2,18,1664]{2,1,0:T(8,128)(2,1)S(1)}, bf16[2,18,1664]{2,1,0:T(8,128)(2,1)S(1)}, u32[]{:S(2)}, u32[]{:S(2)}) collective-permute-start(bf16[2,18,1664]{2,1,0:T(8,128)(2,1)S(1)} %get-tuple-element.14), channel_id=1, source_target_pairs={{0,16},{8,24},{16,32},{24,40},{32,48},{40,56},{48,64},{56,72},{64,... | collective-permute-start | bytes 359432 | tf_op jit(solution)/shard_map/ppermute | solution.py:19
  112.6 15.0 %collective-permute-start.16 = (bf16[144,1664]{1,0:T(8,128)(2,1)}, bf16[144,1664]{1,0:T(8,128)(2,1)S(1)}, u32[]{:S(2)}, u32[]{:S(2)}) collective-permute-start(bf16[144,1664]{1,0:T(8,128)(2,1)} %squeeze.23), channel_id=1, source_target_pairs={{0,384},{128,0},{256,128},{384,256},{1,385},{129,1},{257,129},{385... | collective-permute-start | bytes 1437704 | tf_op jit(solution)/shard_map/ppermute | solution.py:19
  115.9 15.3 %collective-permute-start.17 = (bf16[144,1664]{1,0:T(8,128)(2,1)}, bf16[144,1664]{1,0:T(8,128)(2,1)}, u32[]{:S(2)}, u32[]{:S(2)}) collective-permute-start(bf16[144,1664]{1,0:T(8,128)(2,1)} %squeeze.23), channel_id=1, source_target_pairs={{0,256},{128,384},{256,0},{384,128},{1,257},{129,385},{257,1},{385... | collective-permute-start | bytes 1437704 | tf_op jit(solution)/shard_map/ppermute | solution.py:19
  118.6 21.3 %collective-permute-start.18 = (bf16[144,1664]{1,0:T(8,128)(2,1)}, bf16[144,1664]{1,0:T(8,128)(2,1)}, u32[]{:S(2)}, u32[]{:S(2)}) collective-permute-start(bf16[144,1664]{1,0:T(8,128)(2,1)} %squeeze.23), channel_id=1, source_target_pairs={{0,128},{128,256},{256,384},{384,0},{1,129},{129,257},{257,385},{3... | collective-permute-start | bytes 1437704 | tf_op jit(solution)/shard_map/ppermute | solution.py:19
  121.9 26.5 %collective-permute-start.9 = (bf16[144,1664]{1,0:T(8,128)(2,1)}, bf16[144,1664]{1,0:T(8,128)(2,1)}, u32[]{:S(2)}, u32[]{:S(2)}) collective-permute-start(bf16[144,1664]{1,0:T(8,128)(2,1)} %squeeze.22), channel_id=1, source_target_pairs={{0,6},{2,0},{4,2},{6,4},{1,7},{3,1},{5,3},{7,5},{8,14},{10,8},{12,... | collective-permute-start | bytes 1437704 | tf_op jit(solution)/shard_map/ppermute | solution.py:19
  125.7 22.8 %collective-permute-start.10 = (bf16[144,1664]{1,0:T(8,128)(2,1)}, bf16[144,1664]{1,0:T(8,128)(2,1)}, u32[]{:S(2)}, u32[]{:S(2)}) collective-permute-start(bf16[144,1664]{1,0:T(8,128)(2,1)} %squeeze.22), channel_id=1, source_target_pairs={{0,4},{2,6},{4,0},{6,2},{1,5},{3,7},{5,1},{7,3},{8,12},{10,14},{12... | collective-permute-start | bytes 1437704 | tf_op jit(solution)/shard_map/ppermute | solution.py:19
  128.4 21.7 %collective-permute-start.11 = (bf16[144,1664]{1,0:T(8,128)(2,1)}, bf16[144,1664]{1,0:T(8,128)(2,1)}, u32[]{:S(2)}, u32[]{:S(2)}) collective-permute-start(bf16[144,1664]{1,0:T(8,128)(2,1)} %squeeze.22), channel_id=1, source_target_pairs={{0,2},{2,4},{4,6},{6,0},{1,3},{3,5},{5,7},{7,1},{8,10},{10,12},{12... | collective-permute-start | bytes 1437704 | tf_op jit(solution)/shard_map/ppermute | solution.py:19
  141.6 45.6 %copy-start.1 = (bf16[4,144,1664]{2,1,0:T(8,128)(2,1)}, bf16[4,144,1664]{2,1,0:T(8,128)(2,1)S(1)}, u32[]{:S(2)}) copy-start(bf16[4,144,1664]{2,1,0:T(8,128)(2,1)S(1)} %pad_maximum_fusion.1.refs_5_) | copy-start | bytes 5750788
  141.6 44.5 %collective-permute-start.19 = (bf16[4,144,1664]{2,1,0:T(8,128)(2,1)S(1)}, bf16[4,144,1664]{2,1,0:T(8,128)(2,1)S(1)}, u32[]{:S(2)}, u32[]{:S(2)}) collective-permute-start(bf16[4,144,1664]{2,1,0:T(8,128)(2,1)S(1)} %pad_maximum_fusion.1.refs_5_), channel_id=1, source_target_pairs={{0,6},{2,0},{4,2},{6,4},{1,7},{3,1},{5,3},{7,5},{8,14},{10,8},{12,... | collective-permute-start | bytes 5750792 | tf_op jit(solution)/shard_map/ppermute | solution.py:19
  146.5 46.1 %collective-permute-start.21 = (bf16[4,144,1664]{2,1,0:T(8,128)(2,1)S(1)}, bf16[4,144,1664]{2,1,0:T(8,128)(2,1)S(1)}, u32[]{:S(2)}, u32[]{:S(2)}) collective-permute-start(bf16[4,144,1664]{2,1,0:T(8,128)(2,1)S(1)} %pad_maximum_fusion.1.refs_5_), channel_id=1, source_target_pairs={{0,2},{2,4},{4,6},{6,0},{1,3},{3,5},{5,7},{7,1},{8,10},{10,12},{12... | collective-permute-start | bytes 5750792 | tf_op jit(solution)/shard_map/ppermute | solution.py:19
  151.7 45.0 %copy-start.4 = (bf16[4,144,1664]{2,1,0:T(8,128)(2,1)}, bf16[4,144,1664]{2,1,0:T(8,128)(2,1)S(1)}, u32[]{:S(2)}) copy-start(bf16[4,144,1664]{2,1,0:T(8,128)(2,1)S(1)} %pad_maximum_fusion.refs_0_) | copy-start | bytes 5750788
  151.7 43.9 %collective-permute-start.12 = (bf16[4,144,1664]{2,1,0:T(8,128)(2,1)S(1)}, bf16[4,144,1664]{2,1,0:T(8,128)(2,1)S(1)}, u32[]{:S(2)}, u32[]{:S(2)}) collective-permute-start(bf16[4,144,1664]{2,1,0:T(8,128)(2,1)S(1)} %pad_maximum_fusion.refs_0_), channel_id=1, source_target_pairs={{0,384},{128,0},{256,128},{384,256},{1,385},{129,1},{257,129},{385... | collective-permute-start | bytes 5750792 | tf_op jit(solution)/shard_map/ppermute | solution.py:19
  153.7 46.8 %collective-permute-start.14 = (bf16[4,144,1664]{2,1,0:T(8,128)(2,1)S(1)}, bf16[4,144,1664]{2,1,0:T(8,128)(2,1)S(1)}, u32[]{:S(2)}, u32[]{:S(2)}) collective-permute-start(bf16[4,144,1664]{2,1,0:T(8,128)(2,1)S(1)} %pad_maximum_fusion.refs_0_), channel_id=1, source_target_pairs={{0,128},{128,256},{256,384},{384,0},{1,129},{129,257},{257,385},{3... | collective-permute-start | bytes 5750792 | tf_op jit(solution)/shard_map/ppermute | solution.py:19
  187.1 35.3 %collective-permute-start.20 = (bf16[2,144,1664]{2,1,0:T(8,128)(2,1)}, bf16[2,144,1664]{2,1,0:T(8,128)(2,1)S(1)}, u32[]{:S(2)}, u32[]{:S(2)}) collective-permute-start(bf16[2,144,1664]{2,1,0:T(8,128)(2,1)} %slice.127), channel_id=1, source_target_pairs={{0,6},{2,0},{4,2},{6,4},{1,7},{3,1},{5,3},{7,5},{8,14},{10,8},{12,... | collective-permute-start | bytes 2875400 | tf_op jit(solution)/shard_map/ppermute | solution.py:19
  193.7 28.8 %collective-permute-start.22 = (bf16[2,144,1664]{2,1,0:T(8,128)(2,1)}, bf16[2,144,1664]{2,1,0:T(8,128)(2,1)}, u32[]{:S(2)}, u32[]{:S(2)}) collective-permute-start(bf16[2,144,1664]{2,1,0:T(8,128)(2,1)} %slice.128), channel_id=1, source_target_pairs={{0,2},{2,4},{4,6},{6,0},{1,3},{3,5},{5,7},{7,1},{8,10},{10,12},{12... | collective-permute-start | bytes 2875400 | tf_op jit(solution)/shard_map/ppermute | solution.py:19
  196.8 25.7 %collective-permute-start.13 = (bf16[2,144,1664]{2,1,0:T(8,128)(2,1)}, bf16[2,144,1664]{2,1,0:T(8,128)(2,1)}, u32[]{:S(2)}, u32[]{:S(2)}) collective-permute-start(bf16[2,144,1664]{2,1,0:T(8,128)(2,1)} %slice.125), channel_id=1, source_target_pairs={{0,384},{128,0},{256,128},{384,256},{1,385},{129,1},{257,129},{385... | collective-permute-start | bytes 2875400 | tf_op jit(solution)/shard_map/ppermute | solution.py:19
  202.1 22.6 %collective-permute-start.15 = (bf16[2,144,1664]{2,1,0:T(8,128)(2,1)}, bf16[2,144,1664]{2,1,0:T(8,128)(2,1)}, u32[]{:S(2)}, u32[]{:S(2)}) collective-permute-start(bf16[2,144,1664]{2,1,0:T(8,128)(2,1)} %slice.126), channel_id=1, source_target_pairs={{0,128},{128,256},{256,384},{384,0},{1,129},{129,257},{257,385},{3... | collective-permute-start | bytes 2875400 | tf_op jit(solution)/shard_map/ppermute | solution.py:19
  206.7 6.9 %collective-permute-start = (bf16[128,1664]{1,0:T(8,128)(2,1)S(1)}, bf16[128,1664]{1,0:T(8,128)(2,1)}, u32[]{:S(2)}, u32[]{:S(2)}) collective-permute-start(bf16[128,1664]{1,0:T(8,128)(2,1)S(1)} %fusion.8), channel_id=1, source_target_pairs={{0,1},{1,0},{2,3},{3,2},{4,5},{5,4},{6,7},{7,6},{8,9},{9,8},{10,11... | collective-permute-start | bytes 1277960 | tf_op jit(solution)/shard_map/ppermute | solution.py:23
  239.1 20.3 %collective-permute-start.24 = (bf16[128,1664]{1,0:T(8,128)(2,1)S(1)}, bf16[128,1664]{1,0:T(8,128)(2,1)S(1)}, u32[]{:S(2)}, u32[]{:S(2)}) collective-permute-start(bf16[128,1664]{1,0:T(8,128)(2,1)S(1)} %get-tuple-element.5), channel_id=1, source_target_pairs={{0,1},{1,0},{2,3},{3,2},{4,5},{5,4},{6,7},{7,6},{8,9},{9,8},{10,11... | collective-permute-start | bytes 1277960 | tf_op jit(solution)/shard_map/ppermute | solution.py:23
  257.5 20.2 %collective-permute-start.25 = (bf16[256,1280]{1,0:T(8,128)(2,1)}, bf16[256,1280]{1,0:T(8,128)(2,1)}, u32[]{:S(2)}, u32[]{:S(2)}) collective-permute-start(bf16[256,1280]{1,0:T(8,128)(2,1)} %divide_convert_fusion), channel_id=1, source_target_pairs={{0,1},{1,0},{2,3},{3,2},{4,5},{5,4},{6,7},{7,6},{8,9},{9,8},{10,11... | collective-permute-start | bytes 1966088 | tf_op jit(solution)/shard_map/ppermute | solution.py:23
  279.0 3.3 collective-permute-start.26
  283.2 39.3 %all-to-all-start.1 = ((f32[256,1,256]{2,1,0:T(1,128)}), f32[256,1,256]{2,1,0:T(1,128)S(1)}, u32[]{:S(2)}, u32[]{:S(2)}) async-start(f32[256,1,256]{2,1,0:T(1,128)} %broadcast_in_dim.34), calls=%async_computation.1 | async-start | bytes 524288 | tf_op jit(solution)/shard_map/all_to_all | solution.py:219
  (18 other events, 154.5 us)
Sparse Core Ops, SparseCore 0:
  51.0 163.1 all-gather.2

commit v2 on v1

v2 whole, which is shorter than its diff:
```python
import functools

import jax
import jax.numpy as jnp
from jax import lax
from jax.experimental import pallas as pl
from jax.experimental.pallas import tpu as pltpu
from jax.sharding import Mesh, PartitionSpec as P

AXES = ("y", "zh", "zl", "x", "c")
SIZES = (4, 2, 8, 4, 2)
CHIPS = ("y", "zh", "zl", "x")
Z = ("zh", "zl")
bf16, f32 = jnp.bfloat16, jnp.float32


def swap(value):
    return lax.ppermute(value, "c", [(0, 1), (1, 0)])


def normalize(values):
    values = values.astype(f32)
    center = jnp.mean(values, axis=-1, keepdims=True)
    spread = jnp.mean((values - center) ** 2, axis=-1, keepdims=True)
    return (values - center) / jnp.sqrt(spread + 1e-05)


def feature_order(rows, head):
    width = rows * 64
    tail = rows - head
    natural = lax.broadcasted_iota(jnp.int32, (width, 1), 0)
    row = natural % rows
    core = (natural // rows) % 2
    x = (natural // (rows * 2)) % 4
    zl = natural // (rows * 8)
    first = (x * 2 + core) * (8 * head) + zl * head + row
    second = 64 * head + zl * (8 * tail) + (core * 4 + x) * tail + row - head
    place = jnp.where(row < head, first, second)
    return (place == lax.broadcasted_iota(jnp.int32, (1, width), 1)).astype(bf16)


def fetch(source, target, sem):
    copy = pltpu.make_async_copy(source, target, sem)
    copy.start()
    return copy


def fetch_extra(ring_ref, first, share, proj, texts, sem):
    copies = []
    for z in range(16):
        rows = 16 * share
        copies.append(fetch(ring_ref.at[z, pl.ds(first, rows), :], proj.at[pl.ds(z * rows, rows), :], sem))
        if texts is not None:
            copies.append(fetch(
                ring_ref.at[z, pl.ds(first + rows, 16), :], texts.at[pl.ds(z * 16, 16), :], sem
            ))
    return copies


NT = (((1,), (1,)), ((), ()))


def unit_rows(emb):
    square = jnp.sum(emb * emb, axis=1, keepdims=True)
    return (emb / jnp.sqrt(square + 1e-06)).astype(bf16)


def texts_kernel(first, share, ring_ref, out_ref, proj, texts, sem):
    for copy in fetch_extra(ring_ref, first, share, proj, texts, sem):
        copy.wait()
    count, width = out_ref.shape
    emb = lax.dot_general(texts[:, :width], proj[:, :width], NT, preferred_element_type=f32)
    held = lax.broadcasted_iota(jnp.int32, (count, count), 1)
    zh, zl, y, x = held >> 7, (held >> 4) & 7, (held >> 2) & 3, held & 3
    index = zl * 32 + x * 8 + (y >> 1) * 4 + (y & 1) * 2 + zh
    order = (index == lax.broadcasted_iota(jnp.int32, (count, count), 0)).astype(bf16)
    out_ref[...] = jnp.dot(order, unit_rows(emb), preferred_element_type=f32).astype(bf16)


def text_units(ring, first, share, count, text_width):
    width = ring.shape[2]
    return pl.pallas_call(
        functools.partial(texts_kernel, first, share),
        out_shape=jax.ShapeDtypeStruct((count, text_width), bf16),
        in_specs=[pl.BlockSpec(memory_space=pl.ANY)],
        out_specs=pl.BlockSpec(memory_space=pltpu.VMEM),
        scratch_shapes=[
            pltpu.VMEM((256 * share, width), bf16),
            pltpu.VMEM((count, width), bf16),
            pltpu.SemaphoreType.DMA,
        ],
        compiler_params=pltpu.CompilerParams(vmem_limit_bytes=32 * 1024 * 1024),
        cost_estimate=pl.CostEstimate(
            flops=2 * count * text_width * text_width,
            bytes_accessed=512 * share * width, transcendentals=0,
        ),
    )(ring)


def tower_kernel(head, tail, share, last, place_ref, act_ref, *refs):
    pieces, ring, refs = refs[:16], refs[16], refs[17:]
    if last:
        scale_ref, units_ref, row_ref, act, weight, normed, sems, proj, extra_sem = refs
    else:
        act, weight, normed, sems = refs
    x, y, sign = place_ref[0], place_ref[1], place_ref[2]
    rows = 8 * head
    width = act_ref.shape[1]

    for zh in range(2):
        for pair in range(2):
            layer = 2 * pair + zh
            for zl in range(8):
                fetch(
                    ring.at[zh * 8 + zl, pl.ds(pair * 8 * tail, 8 * tail), :],
                    weight.at[layer, pl.ds(8 * rows + zl * 8 * tail, 8 * tail), :],
                    sems.at[layer],
                )
        for inner in range(4):
            for outer in range(4):
                source = pieces[zh * 8 + (inner // 2) * 4 + outer].at[inner % 2]
                by_x, by_y = (inner, outer) if zh == 0 else (outer, inner)
                from_x, from_y = (x + 4 + sign * by_x) % 4, (y + 4 + sign * by_y) % 4
                layer = 2 * (from_y % 2) + zh
                first = pl.multiple_of((from_x * 2 + from_y // 2) * rows, 16)
                fetch(source, weight.at[layer, pl.ds(first, rows), :], sems.at[layer])
    if last:
        extra = fetch_extra(ring, 16 * tail, share, proj, None, extra_sem)

    act[...] = act_ref[...]

    def layer_step(layer, carry):
        normed[...] = normalize(act[...]).astype(bf16)
        pltpu.make_async_copy(weight.at[layer], weight.at[layer], sems.at[layer]).wait()
        for start in range(0, width, 256):
            cols = pl.ds(start, min(256, width - start))
            update = jnp.dot(normed[...], weight[layer, :, cols], preferred_element_type=f32)
            act[:, cols] = (act[:, cols].astype(f32) + jax.nn.gelu(update)).astype(bf16)
        return carry

    lax.fori_loop(0, 4, layer_step, 0)
    if last:
        for copy in extra:
            copy.wait()
        pooled = jnp.mean(normalize(act[...]), axis=0, keepdims=True)
        pooled = jnp.broadcast_to(pooled, (8, width)).astype(bf16)
        emb = lax.dot_general(pooled, proj[...], NT, preferred_element_type=f32)
        row_ref[...] = scale_ref[0] * lax.dot_general(
            unit_rows(emb), units_ref[...], NT, preferred_element_type=f32
        )


def tower(act, pieces, ring, place, head, tail, share, scale=None, units=None):
    tokens, width = act.shape
    last = units is not None
    vmem, anywhere = pl.BlockSpec(memory_space=pltpu.VMEM), pl.BlockSpec(memory_space=pl.ANY)
    smem = pl.BlockSpec(memory_space=pltpu.SMEM)
    scratch = [
        pltpu.VMEM((4, width, width), bf16),
        pltpu.VMEM((tokens, width), bf16),
        pltpu.SemaphoreType.DMA((4,)),
    ]
    if last:
        out_shape = jax.ShapeDtypeStruct((8, units.shape[0]), f32)
        scratch = [pltpu.VMEM((tokens, width), bf16)] + scratch
        scratch += [pltpu.VMEM((256 * share, width), bf16), pltpu.SemaphoreType.DMA]
        more, more_specs = (scale, units), [smem, vmem]
    else:
        out_shape = jax.ShapeDtypeStruct((tokens, width), bf16)
        more, more_specs = (), []
    return pl.pallas_call(
        functools.partial(tower_kernel, head, tail, share, last),
        out_shape=out_shape,
        in_specs=[smem, vmem] + [anywhere] * 17 + more_specs,
        out_specs=vmem,
        scratch_shapes=scratch,
        compiler_params=pltpu.CompilerParams(vmem_limit_bytes=40 * 1024 * 1024),
        cost_estimate=pl.CostEstimate(
            flops=8 * tokens * width * width, bytes_accessed=8 * width * width, transcendentals=0
        ),
    )(place, act, *pieces, ring, *more)


def hop(value, axis):
    return lax.ppermute(
        value, (axis, "c"),
        [(i * 2 + c, (i + 1 - 2 * c) % 4 * 2 + c) for i in range(4) for c in range(2)],
    )


def gather_plane(block, axis_one, axis_two):
    line = [block]
    for _ in range(3):
        line.append(hop(line[-1], axis_one))
    pairs = []
    for pair in (jnp.stack(line[:2]), jnp.stack(line[2:])):
        pairs.append(pair)
        for _ in range(3):
            pair = hop(pair, axis_two)
            pairs.append(pair)
    return pairs


def on_device(images, text_pooled, image_weight, proj_image, proj_text, logit_scale, pairing):
    y, zh, zl, x, c = (lax.axis_index(name) for name in AXES)
    rows = image_weight.shape[1]
    width, text_width = proj_image.shape[0], proj_text.shape[0]
    micro = images.shape[0]
    head = 22
    tail = rows - head
    share = proj_image.shape[1] // 4
    section = y * 2 + zh
    within = section % 4
    at_home = (y // 2) == c

    order = feature_order(rows, head)

    def ordered(values):
        return jnp.dot(values, order, preferred_element_type=f32).astype(bf16)

    crossing = [(p * 2 + 1, (p + 2) * 2) for p in (0, 1)] + [(p * 2, (p - 2) * 2 + 1) for p in (2, 3)]
    weight = image_weight[0]
    weight = ordered(jnp.where(at_home, weight, lax.ppermute(weight, ("y", "c"), crossing)))

    def share_of(projection):
        return lax.dynamic_slice_in_dim(projection, within * share, share, 1).T

    text_row = lax.dynamic_slice_in_dim(text_pooled, within, 1, 0)
    widen = ((0, 0), (0, width - text_width))
    text_rows = jnp.pad(jnp.concatenate([share_of(proj_text), text_row]), widen)
    image_rows = jnp.pad(ordered(share_of(proj_image)), ((0, 1), (0, 0)))
    first_core = c == 0
    extra = jnp.where(
        at_home,
        jnp.where(first_core, text_rows, image_rows),
        swap(jnp.where(first_core, image_rows, text_rows)),
    )
    image = ordered(lax.dynamic_index_in_dim(images, within, 0, False))
    image = jnp.where(at_home, image, swap(image))

    column = lax.all_gather(weight[:head], Z, axis=0).reshape(2, 8 * head, width)
    small = jnp.concatenate([weight[head:], extra])
    spread = lax.all_to_all(
        jnp.broadcast_to(small[None], (16,) + small.shape), ("y", "x"), 0, 0, tiled=True
    )
    weight_part = spread[:, :tail].reshape(2, 2, 4, tail, width).transpose(1, 0, 2, 3, 4)
    plane_rows = jnp.concatenate([
        weight_part.reshape(16 * tail, width),
        spread[:, tail:tail + share].reshape(16 * share, width),
        spread[:, tail + share],
    ])
    ring = lax.all_gather(plane_rows, Z, axis=0)
    pieces = gather_plane(column[0], "x", "y") + gather_plane(column[1], "y", "x")

    units = swap(text_units(ring, 16 * tail, share, 256, text_width))
    place = jnp.stack([x, y, 2 * c - 1]).astype(jnp.int32)
    act = tower(image, pieces, ring, place, head, tail, share)
    row = tower(swap(act), pieces, ring, place, head, tail, share, logit_scale, units)[:1]
    row = jnp.where(first_core, swap(row), row)

    count = row.shape[1]
    rows_of_z = lax.all_to_all(jnp.broadcast_to(row[None], (16, 1, count)), Z, 0, 0, tiled=True)
    logits = lax.all_to_all(
        jnp.broadcast_to(rows_of_z.reshape(1, 16, count), (16, 16, count)), ("y", "x"), 0, 0, tiled=True
    )
    by_chip = logits.reshape(2, 2, 4, 2, 8, count)
    zero = jnp.int32(0)
    own_logits = lax.dynamic_slice(
        by_chip, (c, zero, x, zero, zl, zero), (1, 2, 1, 2, 1, count)
    ).reshape(micro, count)
    row_start = ((zl * 4 + x) * 2 + c) * micro
    column_lse = jnp.log(jnp.sum(jnp.exp(logits.reshape(256, count)), axis=0))
    own_pairs = lax.dynamic_slice_in_dim(pairing, row_start, micro, 0)
    paired = own_pairs[:, None] == lax.broadcasted_iota(jnp.int32, (1, count), 1)
    positive = jnp.sum(jnp.where(paired, own_logits, 0.0), axis=1)
    image_loss = jnp.log(jnp.sum(jnp.exp(own_logits), axis=1)) - positive
    text_loss = jnp.sum(jnp.where(paired, column_lse[None, :], 0.0), axis=1) - positive
    columns = count // 8
    logit_block = lax.dynamic_slice_in_dim(own_logits, section * columns, columns, 1)
    return (logit_block, image_loss, text_loss)


def solution(mesh):
    fine = Mesh(mesh.devices.reshape(SIZES), AXES)
    section, dp = ("y", "zh"), ("zl", "x", "c")
    in_specs = (
        P(dp, None, None),
        P(dp, None),
        P(section, dp, None),
        P(None, dp),
        P(None, dp),
        P(),
        P(),
    )
    out_specs = (P(dp, section), P(dp), P(dp))
    return jax.shard_map(on_device, mesh=fine, in_specs=in_specs, out_specs=out_specs, check_vma=False)
```

time: 333 us -> 292 us (0.88)
  waiting for transfers between devices: 95.9 us -> 71.3 us
  blocking collectives: 17.4 us -> 39.9 us
  starting transfers between devices: 121 us -> 106 us
  local copies, waits for them, and re-layouts: 30 us -> 16 us
  matrix products: 13.5 us -> 8.62 us
  Pallas kernels: 28.4 us -> 24.7 us
    ppermute x21 -> x18, waiting for transfers between devices: 65.4 us -> 20.7 us  [hop(): lax.ppermute(value, (axis, 'c'), [(i * 2 + c, (i + 1 - 2 * c) % 4 * 2 + c...]
    all_gather x0 -> x1, waiting for transfers between devices: none -> 36.8 us  [on_device(): lax.all_gather(weight[:head], Z, axis=0).reshape(2, 8 * head, width)]
    all_to_all x0 -> x1, blocking collectives: none -> 18.7 us  [on_device(): lax.all_to_all(jnp.broadcast_to(row[None], (16, 1, count)), Z, 0, 0, tile...]
    all_to_all x1, waiting for transfers between devices: 23.4 us -> 7.36 us  [on_device(): lax.all_to_all(jnp.broadcast_to(rows_of_z.reshape(1, 16, count), (16, 16,...]
    ppermute x21 -> x18, starting transfers between devices: 78 us -> 67.3 us  [hop(): lax.ppermute(value, (axis, 'c'), [(i * 2 + c, (i + 1 - 2 * c) % 4 * 2 + c...]
    all_to_all x1, starting transfers between devices: 15.8 us -> 6.15 us  [on_device(): lax.all_to_all(jnp.broadcast_to(rows_of_z.reshape(1, 16, count), (16, 16,...]
    slice x9 -> x6, local copies, waits for them, and re-layouts: 12.4 us -> 4.5 us  [the longest x3 3.34 us: on_device(): column[1]]
    reshape x5 -> x3, local copies, waits for them, and re-layouts: 7.9 us -> 0.14 us  [the longest x1 0.08 us: on_device(): spread[:, :tail].reshape(2, 2, 4, tail, width).transpose(1, 0, 2, 3, 4)]
  transfers between devices with their start and end apart: 29 -> 27, of which waited for: 12 -> 14; matrix products, arithmetic and copies ran while one was open for 11% -> 6% of each run, Pallas kernels for 4% -> 4%
where the time goes in v2:
time: 292 us; the launch traced here: 290 us
  starting transfers between devices  106 us (36%)
  waiting for transfers between devices  71.3 us (24%)
  blocking collectives  39.9 us (14%)
  Pallas kernels  24.7 us (8%)
  local copies, waits for them, and re-layouts  16 us (5%)
  between operations  15.4 us (5%)
  matrix products  8.62 us (3%)
  other arithmetic  8.15 us (3%)
    ppermute x18, starting transfers between devices, hop(): lax.ppermute(value, (axis, 'c'), [(i * 2 + c, (i + 1 - 2 * c) % 4 * 2 + c...  67.3 us
    all_gather x1, waiting for transfers between devices, on_device(): lax.all_gather(weight[:head], Z, axis=0).reshape(2, 8 * head, width)  36.8 us
    ppermute x5, starting transfers between devices, swap(): return lax.ppermute(value, 'c', [(0, 1), (1, 0)])  25.8 us
    pallas_call x2, Pallas kernels, tower(): pl.pallas_call(functools.partial(tower_kernel, head, tail, share, last),...  21.5 us
    all_to_all x1, blocking collectives, on_device(): lax.all_to_all(jnp.broadcast_to(small[None], (16,) + small.shape), ('y',...  21.2 us
    ppermute x18, waiting for transfers between devices, hop(): lax.ppermute(value, (axis, 'c'), [(i * 2 + c, (i + 1 - 2 * c) % 4 * 2 + c...  20.7 us
    all_to_all x1, blocking collectives, on_device(): lax.all_to_all(jnp.broadcast_to(row[None], (16, 1, count)), Z, 0, 0, tile...  18.7 us
    dot_general x3, matrix products, ordered(): return jnp.dot(values, order, preferred_element_type=f32).astype(bf16)  8.62 us
  transfers between devices with their start and end apart: 27, of which 14 were waited for; matrix products, arithmetic and copies ran while one was open for 6% of the time, Pallas kernels for 4%

profile of v2, /device:TPU:1, one launch (start us, length us, event | category | flops | bytes accessed | tf_op | source)
XLA Modules:
  0.0 289.7 jit_solution(17980756770576413381)
XLA Ops:
  7.2 6.3 %collective-permute-start.1 = (bf16[26,1664]{1,0:T(8,128)(2,1)}, bf16[26,1664]{1,0:T(8,128)(2,1)S(1)}, u32[]{:S(2)}, u32[]{:S(2)}) collective-permute-start(bf16[26,1664]{1,0:T(8,128)(2,1)} %bitcast.44), channel_id=1, source_target_pairs={{1,256},{129,384},{256,1},{384,129},{3,258},{131,386},{258,3},{386... | collective-permute-start | bytes 259592 | tf_op jit(solution)/shard_map/ppermute | solution.py:223
  13.7 2.5 collective-permute-done.1
  16.2 3.2 %fusion.7 = bf16[26,1664]{1,0:T(8,128)(2,1)S(1)} fusion(s32[1664]{0:T(1024)S(1)} %fusion.28, bf16[26,1664]{1,0:T(8,128)(2,1)S(1)} %collective-permute-done.1, pred[]{:T(512)S(6)} %eq.66, bf16[1,26,1664]{2,1,0:T(8,128)(2,1)} %param.9), kind=kOutput, calls=%fused_computation.8 | convolution fusion | flops 146838016 | bytes 266241 | tf_op jit(solution)/shard_map/dot_general | solution.py:219
  20.9 2.9 %fusion.8 = bf16[5,1664]{1,0:T(8,128)(2,1)S(1)} fusion(s32[1664]{0:T(1024)S(1)} %fusion.28, bf16[1664,20]{0,1:T(8,128)(2,1)} %param.10, s32[]{:T(128)S(6)} %select_n.194), kind=kOutput, calls=%fused_computation.9 | convolution fusion | flops 30466176 | bytes 49924 | tf_op jit(solution)/shard_map/dot_general | solution.py:219
  27.1 21.2 %all_to_all.15 = bf16[16,10,1664]{2,1,0:T(8,128)(2,1)S(1)} all-to-all(bf16[16,10,1664]{2,1,0:T(8,128)(2,1)S(1)} %broadcast_in_dim.39), channel_id=1, replica_groups=mesh['y'=4,'zh'=2,'zl'=8,'x'=4,'c'=2] {'y','x'}, dimensions={0} | all-to-all | bytes 1064960 | tf_op jit(solution)/shard_map/all_to_all | solution.py:243
  49.8 36.8 %all-gather.8.cloned.1.call-done = bf16[16,22,1664]{2,1,0:T(8,128)(2,1)} async-done(((bf16[1,22,1664]{2,1,0:T(8,128)(2,1)}), bf16[16,22,1664]{2,1,0:T(8,128)(2,1)}) %all-gather.8.cloned.1.call-update) | async-done | bytes 1171472 | tf_op jit(solution)/shard_map/all_gather | solution.py:241
  88.9 5.0 %collective-permute-start.11 = (bf16[176,1664]{1,0:T(8,128)(2,1)}, bf16[176,1664]{1,0:T(8,128)(2,1)}, u32[]{:S(2)}, u32[]{:S(2)}) collective-permute-start(bf16[176,1664]{1,0:T(8,128)(2,1)} %reshape.211), channel_id=1, source_target_pairs={{0,128},{1,385},{128,256},{129,1},{256,384},{257,129},{384,0},{385... | collective-permute-start | bytes 1757192 | tf_op jit(solution)/shard_map/ppermute | solution.py:185
  94.9 3.9 %collective-permute-start.2 = (bf16[176,1664]{1,0:T(8,128)(2,1)}, bf16[176,1664]{1,0:T(8,128)(2,1)}, u32[]{:S(2)}, u32[]{:S(2)}) collective-permute-start(bf16[176,1664]{1,0:T(8,128)(2,1)} %reshape.209), channel_id=1, source_target_pairs={{0,2},{1,7},{2,4},{3,1},{4,6},{5,3},{6,0},{7,5},{8,10},{9,15},{10,... | collective-permute-start | bytes 1757192 | tf_op jit(solution)/shard_map/ppermute | solution.py:185
  101.0 5.0 %collective-permute-start.15 = (bf16[176,1664]{1,0:T(8,128)(2,1)}, bf16[176,1664]{1,0:T(8,128)(2,1)}, u32[]{:S(2)}, u32[]{:S(2)}) collective-permute-start(bf16[176,1664]{1,0:T(8,128)(2,1)} %collective-permute-done.11), channel_id=1, source_target_pairs={{0,128},{1,385},{128,256},{129,1},{256,384},{257,129},{384,0},{385... | collective-permute-start | bytes 1757192 | tf_op jit(solution)/shard_map/ppermute | solution.py:185
  106.1 5.1 %collective-permute-start.6 = (bf16[176,1664]{1,0:T(8,128)(2,1)}, bf16[176,1664]{1,0:T(8,128)(2,1)}, u32[]{:S(2)}, u32[]{:S(2)}) collective-permute-start(bf16[176,1664]{1,0:T(8,128)(2,1)} %collective-permute-done.2), channel_id=1, source_target_pairs={{0,2},{1,7},{2,4},{3,1},{4,6},{5,3},{6,0},{7,5},{8,10},{9,15},{10,... | collective-permute-start | bytes 1757192 | tf_op jit(solution)/shard_map/ppermute | solution.py:185
  113.1 5.3 %collective-permute-start.16 = (bf16[176,1664]{1,0:T(8,128)(2,1)}, bf16[176,1664]{1,0:T(8,128)(2,1)}, u32[]{:S(2)}, u32[]{:S(2)}) collective-permute-start(bf16[176,1664]{1,0:T(8,128)(2,1)} %collective-permute-done.15), channel_id=1, source_target_pairs={{0,128},{1,385},{128,256},{129,1},{256,384},{257,129},{384,0},{385... | collective-permute-start | bytes 1757192 | tf_op jit(solution)/shard_map/ppermute | solution.py:185
  119.6 4.0 %collective-permute-start.7 = (bf16[176,1664]{1,0:T(8,128)(2,1)}, bf16[176,1664]{1,0:T(8,128)(2,1)S(1)}, u32[]{:S(2)}, u32[]{:S(2)}) collective-permute-start(bf16[176,1664]{1,0:T(8,128)(2,1)} %collective-permute-done.6), channel_id=1, source_target_pairs={{0,2},{1,7},{2,4},{3,1},{4,6},{5,3},{6,0},{7,5},{8,10},{9,15},{10,... | collective-permute-start | bytes 1757192 | tf_op jit(solution)/shard_map/ppermute | solution.py:185
  138.1 5.2 %collective-permute-done.12.refs_9_ = bf16[2,176,1664]{2,1,0:T(8,128)(2,1)S(1)} collective-permute-done((bf16[2,176,1664]{2,1,0:T(8,128)(2,1)S(1)}, bf16[2,176,1664]{2,1,0:T(8,128)(2,1)S(1)}, u32[]{:S(2)}, u32[]{:S(2)}) %collective-permute-start.12) | collective-permute-done | bytes 1171488 | tf_op jit(solution)/shard_map/ppermute | solution.py:185
  143.3 5.2 %collective-permute-start.13 = (bf16[2,176,1664]{2,1,0:T(8,128)(2,1)S(1)}, bf16[2,176,1664]{2,1,0:T(8,128)(2,1)}, u32[]{:S(2)}, u32[]{:S(2)}) collective-permute-start(bf16[2,176,1664]{2,1,0:T(8,128)(2,1)S(1)} %collective-permute-done.12.refs_9_), channel_id=1, source_target_pairs={{0,2},{1,7},{2,4},{3,1},{4,6},{5,3},{6,0},{7,5},{8,10},{9,15},{10,... | collective-permute-start | bytes 3514376 | tf_op jit(solution)/shard_map/ppermute | solution.py:185
  153.2 2.7 collective-permute-done.17.refs_13_
  155.9 5.2 %collective-permute-start.18 = (bf16[2,176,1664]{2,1,0:T(8,128)(2,1)S(1)}, bf16[2,176,1664]{2,1,0:T(8,128)(2,1)}, u32[]{:S(2)}, u32[]{:S(2)}) collective-permute-start(bf16[2,176,1664]{2,1,0:T(8,128)(2,1)S(1)} %collective-permute-done.17.refs_13_), channel_id=1, source_target_pairs={{0,2},{1,7},{2,4},{3,1},{4,6},{5,3},{6,0},{7,5},{8,10},{9,15},{10,... | collective-permute-start | bytes 3514376 | tf_op jit(solution)/shard_map/ppermute | solution.py:185
  161.1 2.4 collective-permute-start.9
  164.7 3.7 %collective-permute-done.13.refs_10_ = bf16[2,176,1664]{2,1,0:T(8,128)(2,1)} collective-permute-done((bf16[2,176,1664]{2,1,0:T(8,128)(2,1)S(1)}, bf16[2,176,1664]{2,1,0:T(8,128)(2,1)}, u32[]{:S(2)}, u32[]{:S(2)}) %collective-permute-start.13) | collective-permute-done | bytes 1171488 | tf_op jit(solution)/shard_map/ppermute | solution.py:185
  168.4 5.2 %collective-permute-start.14 = (bf16[2,176,1664]{2,1,0:T(8,128)(2,1)}, bf16[2,176,1664]{2,1,0:T(8,128)(2,1)}, u32[]{:S(2)}, u32[]{:S(2)}) collective-permute-start(bf16[2,176,1664]{2,1,0:T(8,128)(2,1)} %collective-permute-done.13.refs_10_), channel_id=1, source_target_pairs={{0,2},{1,7},{2,4},{3,1},{4,6},{5,3},{6,0},{7,5},{8,10},{9,15},{10,... | collective-permute-start | bytes 3514376 | tf_op jit(solution)/shard_map/ppermute | solution.py:185
  173.7 2.4 collective-permute-start.5
  176.1 4.8 %collective-permute-done.18.refs_14_ = bf16[2,176,1664]{2,1,0:T(8,128)(2,1)} collective-permute-done((bf16[2,176,1664]{2,1,0:T(8,128)(2,1)S(1)}, bf16[2,176,1664]{2,1,0:T(8,128)(2,1)}, u32[]{:S(2)}, u32[]{:S(2)}) %collective-permute-start.18) | collective-permute-done | bytes 1171488 | tf_op jit(solution)/shard_map/ppermute | solution.py:185
  181.0 5.2 %collective-permute-start.19 = (bf16[2,176,1664]{2,1,0:T(8,128)(2,1)}, bf16[2,176,1664]{2,1,0:T(8,128)(2,1)}, u32[]{:S(2)}, u32[]{:S(2)}) collective-permute-start(bf16[2,176,1664]{2,1,0:T(8,128)(2,1)} %collective-permute-done.18.refs_14_), channel_id=1, source_target_pairs={{0,2},{1,7},{2,4},{3,1},{4,6},{5,3},{6,0},{7,5},{8,10},{9,15},{10,... | collective-permute-start | bytes 3514376 | tf_op jit(solution)/shard_map/ppermute | solution.py:185
  188.7 2.5 fusion.6
  191.2 12.3 %collective-permute-start = (bf16[128,1664]{1,0:T(8,128)(2,1)S(1)}, bf16[128,1664]{1,0:T(8,128)(2,1)}, u32[]{:S(2)}, u32[]{:S(2)}) collective-permute-start(bf16[128,1664]{1,0:T(8,128)(2,1)S(1)} %fusion.6), channel_id=1, source_target_pairs={{0,1},{1,0},{2,3},{3,2},{4,5},{5,4},{6,7},{7,6},{8,9},{9,8},{10,11... | collective-permute-start | bytes 1277960 | tf_op jit(solution)/shard_map/ppermute | solution.py:18
  206.0 3.4 %copy-done.1 = bf16[2560,1664]{1,0:T(8,128)(2,1)S(1)} copy-done((bf16[2560,1664]{1,0:T(8,128)(2,1)S(1)}, bf16[2560,1664]{1,0:T(8,128)(2,1)}, u32[]{:S(2)}) %copy-start.1) | copy-done | bytes 8519704
  209.4 3.3 %shard_map.95 = bf16[256,1280]{1,0:T(8,128)(2,1)S(1)} custom-call(bf16[16,160,1664]{2,1,0:T(8,128)(2,1)S(1)} %bitcast.36), custom_call_target="tpu_custom_call" | custom-call | flops 838860800 | bytes 4259840 | tf_op jit(solution)/shard_map/pallas_call | solution.py:82
  215.1 9.3 %shard_map.94 = bf16[128,1664]{1,0:T(8,128)(2,1)S(1)} custom-call(s32[3]{0:T(128)S(1)} %pad_add_fusion.place_ref, bf16[128,1664]{1,0:T(8,128)(2,1)S(1)} %broadcast_select_fusion.act_ref, bf16[2,176,1664]{2,1,0:T(8,128)(2,1)S(1)} %copy-done.3, bf16[2,176,1664]{2,1,0:T(8,128)(2,1)S(1)} %copy-done.9, bf16[2,176,1664]{2,1,0:T(8,128)(2,1)} %collective-permute-done.4.refs_2_, ...), custom_call_target="tpu_custom_call" | custom-call | flops 2835349504 | bytes 22151168 | tf_op jit(solution)/shard_map/pallas_call | solution.py:171
  224.4 7.0 %collective-permute-start.21 = (bf16[128,1664]{1,0:T(8,128)(2,1)S(1)}, bf16[128,1664]{1,0:T(8,128)(2,1)S(1)}, u32[]{:S(2)}, u32[]{:S(2)}) collective-permute-start(bf16[128,1664]{1,0:T(8,128)(2,1)S(1)} %shard_map.94), channel_id=1, source_target_pairs={{0,1},{1,0},{2,3},{3,2},{4,5},{5,4},{6,7},{7,6},{8,9},{9,8},{10,11... | collective-permute-start | bytes 1277960 | tf_op jit(solution)/shard_map/ppermute | solution.py:18
  232.7 12.2 %shard_map.96 = f32[8,256]{1,0:T(8,128)S(1)} custom-call(s32[3]{0:T(128)S(1)} %pad_add_fusion.place_ref, bf16[128,1664]{1,0:T(8,128)(2,1)S(1)} %collective-permute-done.21.act_ref, bf16[2,176,1664]{2,1,0:T(8,128)(2,1)S(1)} %copy-done.3, bf16[2,176,1664]{2,1,0:T(8,128)(2,1)S(1)} %copy-done.9, bf16[2,176,1664]{2,1,0:T(8,128)(2,1)} %collective-permute-done.4.refs_2_, ...), custom_call_target="tpu_custom_call" | custom-call | flops 2835349504 | bytes 22151168 | tf_op jit(solution)/shard_map/pallas_call | solution.py:171
  248.0 18.7 %all_to_all.16 = f32[16,1,256]{2,1,0:T(1,128)S(1)} all-to-all(f32[16,1,256]{2,1,0:T(1,128)S(1)} %broadcast_in_dim.41), channel_id=1, replica_groups=mesh['y'=4,'zh'=2,'zl'=8,'x'=4,'c'=2] {'zh','zl'}, dimensions={0} | all-to-all | bytes 32768 | tf_op jit(solution)/shard_map/all_to_all | solution.py:262
  267.4 6.1 %all-to-all-start.2 = ((f32[16,16,256]{2,1,0:T(8,128)}), f32[16,16,256]{2,1,0:T(8,128)S(1)}, u32[]{:S(2)}, u32[]{:S(2)}) async-start(f32[16,16,256]{2,1,0:T(8,128)} %broadcast_in_dim.43), calls=%async_computation.2 | async-start | bytes 524288 | tf_op jit(solution)/shard_map/all_to_all | solution.py:263
  273.7 7.4 %all-to-all-done.2 = f32[16,16,256]{2,1,0:T(8,128)S(1)} async-done(((f32[16,16,256]{2,1,0:T(8,128)}), f32[16,16,256]{2,1,0:T(8,128)S(1)}, u32[]{:S(2)}, u32[]{:S(2)}) %all-to-all-start.2) | async-done | bytes 262176 | tf_op jit(solution)/shard_map/all_to_all | solution.py:263
  (111 shorter events, 48.5 us)
Async XLA Ops:
  7.2 181.5 %copy-start = (bf16[4,128,1664]{2,1,0:T(8,128)(2,1)S(1)}, bf16[4,128,1664]{2,1,0:T(8,128)(2,1)}, u32[]{:S(2)}) copy-start(bf16[4,128,1664]{2,1,0:T(8,128)(2,1)} %param.7) | copy-start | bytes 5111812
  7.2 79.3 %all-gather.8.cloned.1.call-start = ((), (), s32[]{:S(2)}) async-start(), calls=%async_computation.4 | async-start | bytes 1357824 | tf_op jit(solution)/shard_map/all_gather | solution.py:241
  7.2 8.9 %collective-permute-start.1 = (bf16[26,1664]{1,0:T(8,128)(2,1)}, bf16[26,1664]{1,0:T(8,128)(2,1)S(1)}, u32[]{:S(2)}, u32[]{:S(2)}) collective-permute-start(bf16[26,1664]{1,0:T(8,128)(2,1)} %bitcast.44), channel_id=1, source_target_pairs={{1,256},{129,384},{256,1},{384,129},{3,258},{131,386},{258,3},{386... | collective-permute-start | bytes 259592 | tf_op jit(solution)/shard_map/ppermute | solution.py:223
  13.6 6.4 %copy-start.15 = (bf16[4,1280]{1,0:T(4,128)(2,1)S(1)}, bf16[4,1280]{1,0:T(4,128)(2,1)}, u32[]{:S(2)}) copy-start(bf16[4,1280]{1,0:T(4,128)(2,1)} %param.8) | copy-start | bytes 30724
  20.0 185.9 %all-gather.6.cloned.1.call-start = ((), (), s32[]{:S(2)}) async-start(), calls=%async_computation.3 | async-start | bytes 9052160 | tf_op jit(solution)/shard_map/all_gather | solution.py:252
  23.9 3.1 %collective-permute-start.20 = (bf16[6,1664]{1,0:T(8,128)(2,1)S(1)}, bf16[6,1664]{1,0:T(8,128)(2,1)S(1)}, u32[]{:S(2)}, u32[]{:S(2)}) collective-permute-start(bf16[6,1664]{1,0:T(8,128)(2,1)S(1)} %broadcast_select_fusion.1), channel_id=1, source_target_pairs={{0,1},{1,0},{2,3},{3,2},{4,5},{5,4},{6,7},{7,6},{8,9},{9,8},{10,11... | collective-permute-start | bytes 59912 | tf_op jit(solution)/shard_map/ppermute | solution.py:18
  88.9 12.1 %collective-permute-start.11 = (bf16[176,1664]{1,0:T(8,128)(2,1)}, bf16[176,1664]{1,0:T(8,128)(2,1)}, u32[]{:S(2)}, u32[]{:S(2)}) collective-permute-start(bf16[176,1664]{1,0:T(8,128)(2,1)} %reshape.211), channel_id=1, source_target_pairs={{0,128},{1,385},{128,256},{129,1},{256,384},{257,129},{384,0},{385... | collective-permute-start | bytes 1757192 | tf_op jit(solution)/shard_map/ppermute | solution.py:185
  94.9 11.2 %collective-permute-start.2 = (bf16[176,1664]{1,0:T(8,128)(2,1)}, bf16[176,1664]{1,0:T(8,128)(2,1)}, u32[]{:S(2)}, u32[]{:S(2)}) collective-permute-start(bf16[176,1664]{1,0:T(8,128)(2,1)} %reshape.209), channel_id=1, source_target_pairs={{0,2},{1,7},{2,4},{3,1},{4,6},{5,3},{6,0},{7,5},{8,10},{9,15},{10,... | collective-permute-start | bytes 1757192 | tf_op jit(solution)/shard_map/ppermute | solution.py:185
  101.0 12.1 %collective-permute-start.15 = (bf16[176,1664]{1,0:T(8,128)(2,1)}, bf16[176,1664]{1,0:T(8,128)(2,1)}, u32[]{:S(2)}, u32[]{:S(2)}) collective-permute-start(bf16[176,1664]{1,0:T(8,128)(2,1)} %collective-permute-done.11), channel_id=1, source_target_pairs={{0,128},{1,385},{128,256},{129,1},{256,384},{257,129},{384,0},{385... | collective-permute-start | bytes 1757192 | tf_op jit(solution)/shard_map/ppermute | solution.py:185
  106.1 13.4 %collective-permute-start.6 = (bf16[176,1664]{1,0:T(8,128)(2,1)}, bf16[176,1664]{1,0:T(8,128)(2,1)}, u32[]{:S(2)}, u32[]{:S(2)}) collective-permute-start(bf16[176,1664]{1,0:T(8,128)(2,1)} %collective-permute-done.2), channel_id=1, source_target_pairs={{0,2},{1,7},{2,4},{3,1},{4,6},{5,3},{6,0},{7,5},{8,10},{9,15},{10,... | collective-permute-start | bytes 1757192 | tf_op jit(solution)/shard_map/ppermute | solution.py:185
  113.1 17.5 %collective-permute-start.16 = (bf16[176,1664]{1,0:T(8,128)(2,1)}, bf16[176,1664]{1,0:T(8,128)(2,1)}, u32[]{:S(2)}, u32[]{:S(2)}) collective-permute-start(bf16[176,1664]{1,0:T(8,128)(2,1)} %collective-permute-done.15), channel_id=1, source_target_pairs={{0,128},{1,385},{128,256},{129,1},{256,384},{257,129},{384,0},{385... | collective-permute-start | bytes 1757192 | tf_op jit(solution)/shard_map/ppermute | solution.py:185
  119.6 14.4 %collective-permute-start.7 = (bf16[176,1664]{1,0:T(8,128)(2,1)}, bf16[176,1664]{1,0:T(8,128)(2,1)S(1)}, u32[]{:S(2)}, u32[]{:S(2)}) collective-permute-start(bf16[176,1664]{1,0:T(8,128)(2,1)} %collective-permute-done.6), channel_id=1, source_target_pairs={{0,2},{1,7},{2,4},{3,1},{4,6},{5,3},{6,0},{7,5},{8,10},{9,15},{10,... | collective-permute-start | bytes 1757192 | tf_op jit(solution)/shard_map/ppermute | solution.py:185
  125.0 18.3 %collective-permute-start.12 = (bf16[2,176,1664]{2,1,0:T(8,128)(2,1)S(1)}, bf16[2,176,1664]{2,1,0:T(8,128)(2,1)S(1)}, u32[]{:S(2)}, u32[]{:S(2)}) collective-permute-start(bf16[2,176,1664]{2,1,0:T(8,128)(2,1)S(1)} %pad_maximum_fusion.2.refs_8_), channel_id=1, source_target_pairs={{0,2},{1,7},{2,4},{3,1},{4,6},{5,3},{6,0},{7,5},{8,10},{9,15},{10,... | collective-permute-start | bytes 3514376 | tf_op jit(solution)/shard_map/ppermute | solution.py:185
  128.2 21.4 %collective-permute-start.3 = (bf16[2,176,1664]{2,1,0:T(8,128)(2,1)S(1)}, bf16[2,176,1664]{2,1,0:T(8,128)(2,1)S(1)}, u32[]{:S(2)}, u32[]{:S(2)}) collective-permute-start(bf16[2,176,1664]{2,1,0:T(8,128)(2,1)S(1)} %pad_maximum_fusion.refs_0_), channel_id=1, source_target_pairs={{0,128},{1,385},{128,256},{129,1},{256,384},{257,129},{384,0},{385... | collective-permute-start | bytes 3514376 | tf_op jit(solution)/shard_map/ppermute | solution.py:185
  132.0 23.9 %collective-permute-start.17 = (bf16[2,176,1664]{2,1,0:T(8,128)(2,1)S(1)}, bf16[2,176,1664]{2,1,0:T(8,128)(2,1)S(1)}, u32[]{:S(2)}, u32[]{:S(2)}) collective-permute-start(bf16[2,176,1664]{2,1,0:T(8,128)(2,1)S(1)} %pad_maximum_fusion.3.refs_12_), channel_id=1, source_target_pairs={{0,2},{1,7},{2,4},{3,1},{4,6},{5,3},{6,0},{7,5},{8,10},{9,15},{10,... | collective-permute-start | bytes 3514376 | tf_op jit(solution)/shard_map/ppermute | solution.py:185
  135.1 26.0 %collective-permute-start.8 = (bf16[2,176,1664]{2,1,0:T(8,128)(2,1)S(1)}, bf16[2,176,1664]{2,1,0:T(8,128)(2,1)S(1)}, u32[]{:S(2)}, u32[]{:S(2)}) collective-permute-start(bf16[2,176,1664]{2,1,0:T(8,128)(2,1)S(1)} %pad_maximum_fusion.1.refs_4_), channel_id=1, source_target_pairs={{0,128},{1,385},{128,256},{129,1},{256,384},{257,129},{384,0},{385... | collective-permute-start | bytes 3514376 | tf_op jit(solution)/shard_map/ppermute | solution.py:185
  143.3 25.1 %collective-permute-start.13 = (bf16[2,176,1664]{2,1,0:T(8,128)(2,1)S(1)}, bf16[2,176,1664]{2,1,0:T(8,128)(2,1)}, u32[]{:S(2)}, u32[]{:S(2)}) collective-permute-start(bf16[2,176,1664]{2,1,0:T(8,128)(2,1)S(1)} %collective-permute-done.12.refs_9_), channel_id=1, source_target_pairs={{0,2},{1,7},{2,4},{3,1},{4,6},{5,3},{6,0},{7,5},{8,10},{9,15},{10,... | collective-permute-start | bytes 3514376 | tf_op jit(solution)/shard_map/ppermute | solution.py:185
  149.6 24.1 %collective-permute-start.4 = (bf16[2,176,1664]{2,1,0:T(8,128)(2,1)S(1)}, bf16[2,176,1664]{2,1,0:T(8,128)(2,1)}, u32[]{:S(2)}, u32[]{:S(2)}) collective-permute-start(bf16[2,176,1664]{2,1,0:T(8,128)(2,1)S(1)} %collective-permute-done.3.refs_1_), channel_id=1, source_target_pairs={{0,128},{1,385},{128,256},{129,1},{256,384},{257,129},{384,0},{385... | collective-permute-start | bytes 3514376 | tf_op jit(solution)/shard_map/ppermute | solution.py:185
  155.9 30.4 %copy-start.13 = (bf16[2,176,1664]{2,1,0:T(8,128)(2,1)}, bf16[2,176,1664]{2,1,0:T(8,128)(2,1)S(1)}, u32[]{:S(2)}) copy-start(bf16[2,176,1664]{2,1,0:T(8,128)(2,1)S(1)} %collective-permute-done.17.refs_13_) | copy-start | bytes 3514372
  155.9 25.1 %collective-permute-start.18 = (bf16[2,176,1664]{2,1,0:T(8,128)(2,1)S(1)}, bf16[2,176,1664]{2,1,0:T(8,128)(2,1)}, u32[]{:S(2)}, u32[]{:S(2)}) collective-permute-start(bf16[2,176,1664]{2,1,0:T(8,128)(2,1)S(1)} %collective-permute-done.17.refs_13_), channel_id=1, source_target_pairs={{0,2},{1,7},{2,4},{3,1},{4,6},{5,3},{6,0},{7,5},{8,10},{9,15},{10,... | collective-permute-start | bytes 3514376 | tf_op jit(solution)/shard_map/ppermute | solution.py:185
  161.1 25.1 %collective-permute-start.9 = (bf16[2,176,1664]{2,1,0:T(8,128)(2,1)S(1)}, bf16[2,176,1664]{2,1,0:T(8,128)(2,1)}, u32[]{:S(2)}, u32[]{:S(2)}) collective-permute-start(bf16[2,176,1664]{2,1,0:T(8,128)(2,1)S(1)} %collective-permute-done.8.refs_5_), channel_id=1, source_target_pairs={{0,128},{1,385},{128,256},{129,1},{256,384},{257,129},{384,0},{385... | collective-permute-start | bytes 3514376 | tf_op jit(solution)/shard_map/ppermute | solution.py:185
  168.4 46.6 %collective-permute-start.14 = (bf16[2,176,1664]{2,1,0:T(8,128)(2,1)}, bf16[2,176,1664]{2,1,0:T(8,128)(2,1)}, u32[]{:S(2)}, u32[]{:S(2)}) collective-permute-start(bf16[2,176,1664]{2,1,0:T(8,128)(2,1)} %collective-permute-done.13.refs_10_), channel_id=1, source_target_pairs={{0,2},{1,7},{2,4},{3,1},{4,6},{5,3},{6,0},{7,5},{8,10},{9,15},{10,... | collective-permute-start | bytes 3514376 | tf_op jit(solution)/shard_map/ppermute | solution.py:185
  173.7 41.3 %collective-permute-start.5 = (bf16[2,176,1664]{2,1,0:T(8,128)(2,1)}, bf16[2,176,1664]{2,1,0:T(8,128)(2,1)}, u32[]{:S(2)}, u32[]{:S(2)}) collective-permute-start(bf16[2,176,1664]{2,1,0:T(8,128)(2,1)} %collective-permute-done.4.refs_2_), channel_id=1, source_target_pairs={{0,128},{1,385},{128,256},{129,1},{256,384},{257,129},{384,0},{385... | collective-permute-start | bytes 3514376 | tf_op jit(solution)/shard_map/ppermute | solution.py:185
  181.0 34.0 %collective-permute-start.19 = (bf16[2,176,1664]{2,1,0:T(8,128)(2,1)}, bf16[2,176,1664]{2,1,0:T(8,128)(2,1)}, u32[]{:S(2)}, u32[]{:S(2)}) collective-permute-start(bf16[2,176,1664]{2,1,0:T(8,128)(2,1)} %collective-permute-done.18.refs_14_), channel_id=1, source_target_pairs={{0,2},{1,7},{2,4},{3,1},{4,6},{5,3},{6,0},{7,5},{8,10},{9,15},{10,... | collective-permute-start | bytes 3514376 | tf_op jit(solution)/shard_map/ppermute | solution.py:185
  186.2 28.8 %collective-permute-start.10 = (bf16[2,176,1664]{2,1,0:T(8,128)(2,1)}, bf16[2,176,1664]{2,1,0:T(8,128)(2,1)}, u32[]{:S(2)}, u32[]{:S(2)}) collective-permute-start(bf16[2,176,1664]{2,1,0:T(8,128)(2,1)} %collective-permute-done.9.refs_6_), channel_id=1, source_target_pairs={{0,128},{1,385},{128,256},{129,1},{256,384},{257,129},{384,0},{385... | collective-permute-start | bytes 3514376 | tf_op jit(solution)/shard_map/ppermute | solution.py:185
  191.2 12.4 %copy-start.14 = (bf16[128,1664]{1,0:T(8,128)(2,1)}, bf16[128,1664]{1,0:T(8,128)(2,1)S(1)}, u32[]{:S(2)}) copy-start(bf16[128,1664]{1,0:T(8,128)(2,1)S(1)} %fusion.6) | copy-start | bytes 1277956
  191.2 13.6 %collective-permute-start = (bf16[128,1664]{1,0:T(8,128)(2,1)S(1)}, bf16[128,1664]{1,0:T(8,128)(2,1)}, u32[]{:S(2)}, u32[]{:S(2)}) collective-permute-start(bf16[128,1664]{1,0:T(8,128)(2,1)S(1)} %fusion.6), channel_id=1, source_target_pairs={{0,1},{1,0},{2,3},{3,2},{4,5},{5,4},{6,7},{7,6},{8,9},{9,8},{10,11... | collective-permute-start | bytes 1277960 | tf_op jit(solution)/shard_map/ppermute | solution.py:18
  212.7 20.0 %collective-permute-start.22 = (bf16[256,1280]{1,0:T(8,128)(2,1)S(1)}, bf16[256,1280]{1,0:T(8,128)(2,1)S(1)}, u32[]{:S(2)}, u32[]{:S(2)}) collective-permute-start(bf16[256,1280]{1,0:T(8,128)(2,1)S(1)} %shard_map.95), channel_id=1, source_target_pairs={{0,1},{1,0},{2,3},{3,2},{4,5},{5,4},{6,7},{7,6},{8,9},{9,8},{10,11... | collective-permute-start | bytes 1966088 | tf_op jit(solution)/shard_map/ppermute | solution.py:18
  224.4 8.4 %collective-permute-start.21 = (bf16[128,1664]{1,0:T(8,128)(2,1)S(1)}, bf16[128,1664]{1,0:T(8,128)(2,1)S(1)}, u32[]{:S(2)}, u32[]{:S(2)}) collective-permute-start(bf16[128,1664]{1,0:T(8,128)(2,1)S(1)} %shard_map.94), channel_id=1, source_target_pairs={{0,1},{1,0},{2,3},{3,2},{4,5},{5,4},{6,7},{7,6},{8,9},{9,8},{10,11... | collective-permute-start | bytes 1277960 | tf_op jit(solution)/shard_map/ppermute | solution.py:18
  232.0 41.6 %copy-start.16 = (s32[256]{0:T(256)S(1)}, s32[256]{0:T(256)}, u32[]{:S(2)}) copy-start(s32[256]{0:T(256)} %param.13) | copy-start | bytes 3076
  244.9 3.1 %collective-permute-start.23 = (f32[1,256]{1,0:T(1,128)S(1)}, f32[1,256]{1,0:T(1,128)S(1)}, u32[]{:S(2)}, u32[]{:S(2)}) collective-permute-start(f32[1,256]{1,0:T(1,128)S(1)} %slice.51), channel_id=1, source_target_pairs={{0,1},{1,0},{2,3},{3,2},{4,5},{5,4},{6,7},{7,6},{8,9},{9,8},{10,11... | collective-permute-start | bytes 3080 | tf_op jit(solution)/shard_map/ppermute | solution.py:18
  267.4 13.7 %all-to-all-start.2 = ((f32[16,16,256]{2,1,0:T(8,128)}), f32[16,16,256]{2,1,0:T(8,128)S(1)}, u32[]{:S(2)}, u32[]{:S(2)}) async-start(f32[16,16,256]{2,1,0:T(8,128)} %broadcast_in_dim.43), calls=%async_computation.2 | async-start | bytes 524288 | tf_op jit(solution)/shard_map/all_to_all | solution.py:263
  (12 other events, 42.9 us)
Sparse Core Ops, SparseCore 0:
  20.1 66.3 all-gather.7
  88.6 113.8 all-gather.5

commit v3 on v2

--- a/solution.py
+++ b/solution.py
@@ -188,17 +188,48 @@
     )
 
 
-def gather_plane(block, axis_one, axis_two):
-    line = [block]
-    for _ in range(3):
-        line.append(hop(line[-1], axis_one))
+def gather_plane(block_one, block_two):
+    axes = (("x", "y"), ("y", "x"))
+    start = [block_one, block_two]
+    first = [hop(start[i], axes[i][0]) for i in range(2)]
+    near = [jnp.stack([start[i], first[i]]) for i in range(2)]
+    second = [hop(first[i], axes[i][0]) for i in range(2)]
+    near_one = [hop(near[i], axes[i][1]) for i in range(2)]
+    second, near_one = lax.optimization_barrier((second, near_one))
+    third = [hop(second[i], axes[i][0]) for i in range(2)]
+    near_two = [hop(near_one[i], axes[i][1]) for i in range(2)]
+    third, near_two = lax.optimization_barrier((third, near_two))
+    far = [jnp.stack([second[i], third[i]]) for i in range(2)]
+    far_one = [hop(far[i], axes[i][1]) for i in range(2)]
+    near_three = [hop(near_two[i], axes[i][1]) for i in range(2)]
+    far_two = [hop(far_one[i], axes[i][1]) for i in range(2)]
+    far_three = [hop(far_two[i], axes[i][1]) for i in range(2)]
     pairs = []
-    for pair in (jnp.stack(line[:2]), jnp.stack(line[2:])):
-        pairs.append(pair)
-        for _ in range(3):
-            pair = hop(pair, axis_two)
-            pairs.append(pair)
+    for i in range(2):
+        pairs += [near[i], near_one[i], near_two[i], near_three[i]]
+        pairs += [far[i], far_one[i], far_two[i], far_three[i]]
     return pairs
+
+
+def ahead_on_ring(value, steps):
+    return lax.ppermute(value, Z, [((i + steps) % 16, i) for i in range(16)])
+
+
+def gather_ring(block, position):
+    near = {0: block}
+    for ahead in (8, 4, 12):
+        near[ahead] = ahead_on_ring(block, ahead)
+    stack = jnp.stack([near[ahead] for ahead in (0, 4, 8, 12)])
+    one, three = ahead_on_ring(stack, 1), ahead_on_ring(stack, -1)
+    two_a = ahead_on_ring(jnp.stack([near[0], near[4]]), 2)
+    two_b = ahead_on_ring(jnp.stack([near[0], near[12]]), -2)
+    blocks = {2: two_a[0], 6: two_a[1], 14: two_b[0], 10: two_b[1]}
+    for k in range(4):
+        blocks[4 * k] = stack[k]
+        blocks[4 * k + 1] = one[k]
+        blocks[(4 * k + 15) % 16] = three[k]
+    line = jnp.stack([blocks[k % 16] for k in range(32)])
+    return lax.dynamic_slice_in_dim(line, (16 - position) % 16, 16, 0)
 
 
 def on_device(images, text_pooled, image_weight, proj_image, proj_text, logit_scale, pairing):
@@ -238,11 +269,10 @@
     image = ordered(lax.dynamic_index_in_dim(images, within, 0, False))
     image = jnp.where(at_home, image, swap(image))
 
-    column = lax.all_gather(weight[:head], Z, axis=0).reshape(2, 8 * head, width)
     small = jnp.concatenate([weight[head:], extra])
-    spread = lax.all_to_all(
-        jnp.broadcast_to(small[None], (16,) + small.shape), ("y", "x"), 0, 0, tiled=True
-    )
+    small, block = lax.optimization_barrier((small, weight[:head]))
+    spread = lax.all_gather(small, ("y", "x"), axis=0)
+    column = gather_ring(block, zh * 8 + zl).reshape(2, 8 * head, width)
     weight_part = spread[:, :tail].reshape(2, 2, 4, tail, width).transpose(1, 0, 2, 3, 4)
     plane_rows = jnp.concatenate([
         weight_part.reshape(16 * tail, width),
@@ -250,7 +280,7 @@
         spread[:, tail + share],
     ])
     ring = lax.all_gather(plane_rows, Z, axis=0)
-    pieces = gather_plane(column[0], "x", "y") + gather_plane(column[1], "y", "x")
+    pieces = gather_plane(column[0], column[1])
 
     units = swap(text_units(ring, 16 * tail, share, 256, text_width))
     place = jnp.stack([x, y, 2 * c - 1]).astype(jnp.int32)

time: 292 us -> 331 us (1.13)
  starting transfers between devices: 106 us -> 133 us
  local copies, waits for them, and re-layouts: 16 us -> 36.5 us
  blocking collectives: 39.9 us -> 36.3 us
    all_gather x1 -> x0, waiting for transfers between devices: 36.8 us -> none  [on_device(): lax.all_gather(weight[:head], Z, axis=0).reshape(2, 8 * head, width)]
    ppermute x0 -> x7, starting transfers between devices: none -> 31.9 us  [ahead_on_ring(): return lax.ppermute(value, Z, [((i + steps) % 16, i) for i in range(16)])]
    ppermute x18, waiting for transfers between devices: 20.7 us -> 48.4 us  [hop(): lax.ppermute(value, (axis, 'c'), [(i * 2 + c, (i + 1 - 2 * c) % 4 * 2 + c...]
    all_to_all x1 -> x0, blocking collectives: 21.2 us -> none  [on_device(): lax.all_to_all(jnp.broadcast_to(small[None], (16,) + small.shape), ('y',...]
    all_gather x0 -> x1, blocking collectives: none -> 19.3 us  [on_device(): spread = lax.all_gather(small, ('y', 'x'), axis=0)]
    unnamed x37 -> x67, local copies, waits for them, and re-layouts: 8.36 us -> 27.4 us
    ppermute x18, starting transfers between devices: 67.3 us -> 56.3 us  [hop(): lax.ppermute(value, (axis, 'c'), [(i * 2 + c, (i + 1 - 2 * c) % 4 * 2 + c...]
    ppermute x5, starting transfers between devices: 25.8 us -> 35.7 us  [swap(): return lax.ppermute(value, 'c', [(0, 1), (1, 0)])]
  transfers between devices with their start and end apart: 27 -> 33, of which waited for: 14 -> 12; matrix products, arithmetic and copies ran while one was open for 6% -> 10% of each run, Pallas kernels for 4% -> 4%
where the time goes in v3:
time: 331 us; the launch traced here: 329 us
  starting transfers between devices  133 us (40%)
  waiting for transfers between devices  69.1 us (21%)
  local copies, waits for them, and re-layouts  36.5 us (11%)
  blocking collectives  36.3 us (11%)
  Pallas kernels  24.8 us (7%)
  between operations  15.5 us (5%)
  matrix products  7.71 us (2%)
  other arithmetic  5.93 us (2%)
    ppermute x18, starting transfers between devices, hop(): lax.ppermute(value, (axis, 'c'), [(i * 2 + c, (i + 1 - 2 * c) % 4 * 2 + c...  56.3 us
    ppermute x18, waiting for transfers between devices, hop(): lax.ppermute(value, (axis, 'c'), [(i * 2 + c, (i + 1 - 2 * c) % 4 * 2 + c...  48.4 us
    ppermute x5, starting transfers between devices, swap(): return lax.ppermute(value, 'c', [(0, 1), (1, 0)])  35.7 us
    ppermute x7, starting transfers between devices, ahead_on_ring(): return lax.ppermute(value, Z, [((i + steps) % 16, i) for i in range(16)])  31.9 us
    unnamed x67, local copies, waits for them, and re-layouts  27.4 us
    pallas_call x2, Pallas kernels, tower(): pl.pallas_call(functools.partial(tower_kernel, head, tail, share, last),...  21.5 us
    all_gather x1, blocking collectives, on_device(): spread = lax.all_gather(small, ('y', 'x'), axis=0)  19.3 us
    all_to_all x1, blocking collectives, on_device(): lax.all_to_all(jnp.broadcast_to(row[None], (16, 1, count)), Z, 0, 0, tile...  17 us
  transfers between devices with their start and end apart: 33, of which 12 were waited for; matrix products, arithmetic and copies ran while one was open for 10% of the time, Pallas kernels for 4%

profile of v3, /device:TPU:1, one launch (start us, length us, event | category | flops | bytes accessed | tf_op | source)
XLA Modules:
  0.0 328.9 jit_solution(5026994945469168326)
XLA Ops:
  8.9 2.9 fusion.8
  11.9 8.8 %collective-permute-start.2 = (bf16[6,1664]{1,0:T(8,128)(2,1)S(1)}, bf16[6,1664]{1,0:T(8,128)(2,1)S(1)}, u32[]{:S(2)}, u32[]{:S(2)}) collective-permute-start(bf16[6,1664]{1,0:T(8,128)(2,1)S(1)} %broadcast_select_fusion.1), channel_id=1, source_target_pairs={{0,1},{1,0},{2,3},{3,2},{4,5},{5,4},{6,7},{7,6},{8,9},{9,8},{10,11... | collective-permute-start | bytes 59912 | tf_op jit(solution)/shard_map/ppermute | solution.py:18
  22.7 5.5 %collective-permute-done.1 = bf16[26,1664]{1,0:T(8,128)(2,1)S(1)} collective-permute-done((bf16[26,1664]{1,0:T(8,128)(2,1)S(1)}, bf16[26,1664]{1,0:T(8,128)(2,1)S(1)}, u32[]{:S(2)}, u32[]{:S(2)}) %collective-permute-start.1) | collective-permute-done | bytes 86560 | tf_op jit(solution)/shard_map/ppermute | solution.py:254
  30.6 3.4 %collective-permute-start.5 = (bf16[22,1664]{1,0:T(8,128)(2,1)S(1)}, bf16[22,1664]{1,0:T(8,128)(2,1)S(1)}, u32[]{:S(2)}, u32[]{:S(2)}) collective-permute-start(bf16[22,1664]{1,0:T(8,128)(2,1)S(1)} %slice.89), channel_id=1, source_target_pairs={{96,0},{104,8},{112,16},{120,24},{0,32},{8,40},{16,48},{24,56},{32... | collective-permute-start | bytes 219656 | tf_op jit(solution)/shard_map/ppermute | solution.py:215
  34.0 10.6 %collective-permute-start.4 = (bf16[22,1664]{1,0:T(8,128)(2,1)S(1)}, bf16[22,1664]{1,0:T(8,128)(2,1)S(1)}, u32[]{:S(2)}, u32[]{:S(2)}) collective-permute-start(bf16[22,1664]{1,0:T(8,128)(2,1)S(1)} %slice.89), channel_id=1, source_target_pairs={{64,0},{72,8},{80,16},{88,24},{96,32},{104,40},{112,48},{120,56},{... | collective-permute-start | bytes 219656 | tf_op jit(solution)/shard_map/ppermute | solution.py:215
  44.7 5.2 %collective-permute-start.3 = (bf16[22,1664]{1,0:T(8,128)(2,1)S(1)}, bf16[22,1664]{1,0:T(8,128)(2,1)S(1)}, u32[]{:S(2)}, u32[]{:S(2)}) collective-permute-start(bf16[22,1664]{1,0:T(8,128)(2,1)S(1)} %slice.89), channel_id=1, source_target_pairs={{32,0},{40,8},{48,16},{56,24},{64,32},{72,40},{80,48},{88,56},{96,... | collective-permute-start | bytes 219656 | tf_op jit(solution)/shard_map/ppermute | solution.py:215
  50.5 19.3 %all-gather.2 = bf16[16,10,1664]{2,1,0:T(8,128)(2,1)S(1)} all-gather(bf16[1,10,1664]{2,1,0:T(8,128)(2,1)S(1)} %bitcast.62), channel_id=2, replica_groups=mesh['y'=4,'zh'=2,'zl'=8,'x'=4,'c'=2] {'y','x'}, dimensions={0}, use_global_device_ids=true | all-gather | bytes 565760 | tf_op jit(solution)/shard_map/all_gather | solution.py:274
  73.3 3.4 %collective-permute-start.8 = (bf16[4,22,1664]{2,1,0:T(8,128)(2,1)S(1)}, bf16[4,22,1664]{2,1,0:T(8,128)(2,1)S(1)}, u32[]{:S(2)}, u32[]{:S(2)}) collective-permute-start(bf16[4,22,1664]{2,1,0:T(8,128)(2,1)S(1)} %pad_maximum_fusion.5), channel_id=1, source_target_pairs={{120,0},{0,8},{8,16},{16,24},{24,32},{32,40},{40,48},{48,56},{56,6... | collective-permute-start | bytes 878600 | tf_op jit(solution)/shard_map/ppermute | solution.py:215
  76.7 3.1 collective-permute-start.9
  79.8 4.3 %collective-permute-start.7 = (bf16[2,22,1664]{2,1,0:T(8,128)(2,1)S(1)}, bf16[2,22,1664]{2,1,0:T(8,128)(2,1)S(1)}, u32[]{:S(2)}, u32[]{:S(2)}) collective-permute-start(bf16[2,22,1664]{2,1,0:T(8,128)(2,1)S(1)} %get-tuple-element.29), channel_id=1, source_target_pairs={{16,0},{24,8},{32,16},{40,24},{48,32},{56,40},{64,48},{72,56},{80,... | collective-permute-start | bytes 439304 | tf_op jit(solution)/shard_map/ppermute | solution.py:215
  84.8 4.9 %collective-permute-done.7 = bf16[2,22,1664]{2,1,0:T(8,128)(2,1)S(1)} collective-permute-done((bf16[2,22,1664]{2,1,0:T(8,128)(2,1)S(1)}, bf16[2,22,1664]{2,1,0:T(8,128)(2,1)S(1)}, u32[]{:S(2)}, u32[]{:S(2)}) %collective-permute-start.7) | collective-permute-done | bytes 146464 | tf_op jit(solution)/shard_map/ppermute | solution.py:215
  111.1 4.1 %collective-permute-start.12 = (bf16[176,1664]{1,0:T(8,128)(2,1)}, bf16[176,1664]{1,0:T(8,128)(2,1)}, u32[]{:S(2)}, u32[]{:S(2)}) collective-permute-start(bf16[176,1664]{1,0:T(8,128)(2,1)} %squeeze.19), channel_id=1, source_target_pairs={{0,128},{1,385},{128,256},{129,1},{256,384},{257,129},{384,0},{385... | collective-permute-start | bytes 1757192 | tf_op jit(solution)/shard_map/ppermute | solution.py:185
  123.7 4.1 %collective-permute-start.15 = (bf16[2,176,1664]{2,1,0:T(8,128)(2,1)S(1)}, bf16[2,176,1664]{2,1,0:T(8,128)(2,1)S(1)}, u32[]{:S(2)}, u32[]{:S(2)}) collective-permute-start(bf16[2,176,1664]{2,1,0:T(8,128)(2,1)S(1)} %pad_maximum_fusion.1.refs_8_), channel_id=1, source_target_pairs={{0,2},{1,7},{2,4},{3,1},{4,6},{5,3},{6,0},{7,5},{8,10},{9,15},{10,... | collective-permute-start | bytes 3514376 | tf_op jit(solution)/shard_map/ppermute | solution.py:185
  129.0 3.7 %collective-permute-start.14 = (bf16[2,176,1664]{2,1,0:T(8,128)(2,1)S(1)}, bf16[2,176,1664]{2,1,0:T(8,128)(2,1)S(1)}, u32[]{:S(2)}, u32[]{:S(2)}) collective-permute-start(bf16[2,176,1664]{2,1,0:T(8,128)(2,1)S(1)} %pad_maximum_fusion.refs_0_), channel_id=1, source_target_pairs={{0,128},{1,385},{128,256},{129,1},{256,384},{257,129},{384,0},{385... | collective-permute-start | bytes 3514376 | tf_op jit(solution)/shard_map/ppermute | solution.py:185
  138.6 8.6 %collective-permute-done.11 = bf16[176,1664]{1,0:T(8,128)(2,1)S(1)} collective-permute-done((bf16[176,1664]{1,0:T(8,128)(2,1)}, bf16[176,1664]{1,0:T(8,128)(2,1)S(1)}, u32[]{:S(2)}, u32[]{:S(2)}) %collective-permute-start.11) | collective-permute-done | bytes 585760 | tf_op jit(solution)/shard_map/ppermute | solution.py:185
  147.2 5.3 %collective-permute-done.13 = bf16[176,1664]{1,0:T(8,128)(2,1)S(1)} collective-permute-done((bf16[176,1664]{1,0:T(8,128)(2,1)}, bf16[176,1664]{1,0:T(8,128)(2,1)S(1)}, u32[]{:S(2)}, u32[]{:S(2)}) %collective-permute-start.13) | collective-permute-done | bytes 585760 | tf_op jit(solution)/shard_map/ppermute | solution.py:185
  152.5 4.9 %collective-permute-start.18 = (bf16[2,176,1664]{2,1,0:T(8,128)(2,1)S(1)}, bf16[2,176,1664]{2,1,0:T(8,128)(2,1)}, u32[]{:S(2)}, u32[]{:S(2)}) collective-permute-start(bf16[2,176,1664]{2,1,0:T(8,128)(2,1)S(1)} %collective-permute-done.14.refs_1_), channel_id=1, source_target_pairs={{0,128},{1,385},{128,256},{129,1},{256,384},{257,129},{384,0},{385... | collective-permute-start | bytes 3514376 | tf_op jit(solution)/shard_map/ppermute | solution.py:185
  165.6 16.3 %collective-permute-done.16 = bf16[176,1664]{1,0:T(8,128)(2,1)S(1)} collective-permute-done((bf16[176,1664]{1,0:T(8,128)(2,1)S(1)}, bf16[176,1664]{1,0:T(8,128)(2,1)S(1)}, u32[]{:S(2)}, u32[]{:S(2)}) %collective-permute-start.16) | collective-permute-done | bytes 585760 | tf_op jit(solution)/shard_map/ppermute | solution.py:185
  182.1 4.1 %collective-permute-start.25 = (bf16[2,176,1664]{2,1,0:T(8,128)(2,1)S(1)}, bf16[2,176,1664]{2,1,0:T(8,128)(2,1)S(1)}, u32[]{:S(2)}, u32[]{:S(2)}) collective-permute-start(bf16[2,176,1664]{2,1,0:T(8,128)(2,1)S(1)} %pad_maximum_fusion.3.refs_12_), channel_id=1, source_target_pairs={{0,2},{1,7},{2,4},{3,1},{4,6},{5,3},{6,0},{7,5},{8,10},{9,15},{10,... | collective-permute-start | bytes 3514376 | tf_op jit(solution)/shard_map/ppermute | solution.py:185
  189.3 9.9 %collective-permute-done.25.refs_13_ = bf16[2,176,1664]{2,1,0:T(8,128)(2,1)S(1)} collective-permute-done((bf16[2,176,1664]{2,1,0:T(8,128)(2,1)S(1)}, bf16[2,176,1664]{2,1,0:T(8,128)(2,1)S(1)}, u32[]{:S(2)}, u32[]{:S(2)}) %collective-permute-start.25) | collective-permute-done | bytes 1171488 | tf_op jit(solution)/shard_map/ppermute | solution.py:185
  199.2 5.0 %collective-permute-start.26 = (bf16[2,176,1664]{2,1,0:T(8,128)(2,1)S(1)}, bf16[2,176,1664]{2,1,0:T(8,128)(2,1)}, u32[]{:S(2)}, u32[]{:S(2)}) collective-permute-start(bf16[2,176,1664]{2,1,0:T(8,128)(2,1)S(1)} %collective-permute-done.25.refs_13_), channel_id=1, source_target_pairs={{0,2},{1,7},{2,4},{3,1},{4,6},{5,3},{6,0},{7,5},{8,10},{9,15},{10,... | collective-permute-start | bytes 3514376 | tf_op jit(solution)/shard_map/ppermute | solution.py:185
  211.5 5.8 %collective-permute-done.26.refs_14_ = bf16[2,176,1664]{2,1,0:T(8,128)(2,1)} collective-permute-done((bf16[2,176,1664]{2,1,0:T(8,128)(2,1)S(1)}, bf16[2,176,1664]{2,1,0:T(8,128)(2,1)}, u32[]{:S(2)}, u32[]{:S(2)}) %collective-permute-start.26) | collective-permute-done | bytes 1171488 | tf_op jit(solution)/shard_map/ppermute | solution.py:185
  217.3 5.1 %collective-permute-start.27 = (bf16[2,176,1664]{2,1,0:T(8,128)(2,1)}, bf16[2,176,1664]{2,1,0:T(8,128)(2,1)}, u32[]{:S(2)}, u32[]{:S(2)}) collective-permute-start(bf16[2,176,1664]{2,1,0:T(8,128)(2,1)} %collective-permute-done.26.refs_14_), channel_id=1, source_target_pairs={{0,2},{1,7},{2,4},{3,1},{4,6},{5,3},{6,0},{7,5},{8,10},{9,15},{10,... | collective-permute-start | bytes 3514376 | tf_op jit(solution)/shard_map/ppermute | solution.py:185
  227.8 14.3 %collective-permute-start = (bf16[128,1664]{1,0:T(8,128)(2,1)S(1)}, bf16[128,1664]{1,0:T(8,128)(2,1)}, u32[]{:S(2)}, u32[]{:S(2)}) collective-permute-start(bf16[128,1664]{1,0:T(8,128)(2,1)S(1)} %fusion.6), channel_id=1, source_target_pairs={{0,1},{1,0},{2,3},{3,2},{4,5},{5,4},{6,7},{7,6},{8,9},{9,8},{10,11... | collective-permute-start | bytes 1277960 | tf_op jit(solution)/shard_map/ppermute | solution.py:18
  244.7 3.4 %copy-done.1 = bf16[2560,1664]{1,0:T(8,128)(2,1)S(1)} copy-done((bf16[2560,1664]{1,0:T(8,128)(2,1)S(1)}, bf16[2560,1664]{1,0:T(8,128)(2,1)}, u32[]{:S(2)}) %copy-start.1) | copy-done | bytes 8519704
  248.1 3.3 shard_map.95
  253.8 9.3 %shard_map.94 = bf16[128,1664]{1,0:T(8,128)(2,1)S(1)} custom-call(s32[3]{0:T(128)S(1)} %pad_add_fusion.place_ref, bf16[128,1664]{1,0:T(8,128)(2,1)S(1)} %broadcast_select_fusion.act_ref, bf16[2,176,1664]{2,1,0:T(8,128)(2,1)S(1)} %copy-done.3, bf16[2,176,1664]{2,1,0:T(8,128)(2,1)S(1)} %copy-done.9, bf16[2,176,1664]{2,1,0:T(8,128)(2,1)} %collective-permute-done.18.refs_2_, ...), custom_call_target="tpu_custom_call" | custom-call | flops 2835349504 | bytes 22151168 | tf_op jit(solution)/shard_map/pallas_call | solution.py:171
  263.1 8.0 %collective-permute-start.28 = (bf16[128,1664]{1,0:T(8,128)(2,1)S(1)}, bf16[128,1664]{1,0:T(8,128)(2,1)S(1)}, u32[]{:S(2)}, u32[]{:S(2)}) collective-permute-start(bf16[128,1664]{1,0:T(8,128)(2,1)S(1)} %shard_map.94), channel_id=1, source_target_pairs={{0,1},{1,0},{2,3},{3,2},{4,5},{5,4},{6,7},{7,6},{8,9},{9,8},{10,11... | collective-permute-start | bytes 1277960 | tf_op jit(solution)/shard_map/ppermute | solution.py:18
  272.5 12.2 %shard_map.96 = f32[8,256]{1,0:T(8,128)S(1)} custom-call(s32[3]{0:T(128)S(1)} %pad_add_fusion.place_ref, bf16[128,1664]{1,0:T(8,128)(2,1)S(1)} %collective-permute-done.28.act_ref, bf16[2,176,1664]{2,1,0:T(8,128)(2,1)S(1)} %copy-done.3, bf16[2,176,1664]{2,1,0:T(8,128)(2,1)S(1)} %copy-done.9, bf16[2,176,1664]{2,1,0:T(8,128)(2,1)} %collective-permute-done.18.refs_2_, ...), custom_call_target="tpu_custom_call" | custom-call | flops 2835349504 | bytes 22151168 | tf_op jit(solution)/shard_map/pallas_call | solution.py:171
  287.8 17.0 %all_to_all.10 = f32[16,1,256]{2,1,0:T(1,128)S(1)} all-to-all(f32[16,1,256]{2,1,0:T(1,128)S(1)} %broadcast_in_dim.34), channel_id=1, replica_groups=mesh['y'=4,'zh'=2,'zl'=8,'x'=4,'c'=2] {'zh','zl'}, dimensions={0} | all-to-all | bytes 32768 | tf_op jit(solution)/shard_map/all_to_all | solution.py:292
  305.5 7.1 %all-to-all-start.1 = ((f32[16,16,256]{2,1,0:T(8,128)}), f32[16,16,256]{2,1,0:T(8,128)S(1)}, u32[]{:S(2)}, u32[]{:S(2)}) async-start(f32[16,16,256]{2,1,0:T(8,128)} %broadcast_in_dim.36), calls=%async_computation.1 | async-start | bytes 524288 | tf_op jit(solution)/shard_map/all_to_all | solution.py:293
  312.9 7.4 %all-to-all-done.1 = f32[16,16,256]{2,1,0:T(8,128)S(1)} async-done(((f32[16,16,256]{2,1,0:T(8,128)}), f32[16,16,256]{2,1,0:T(8,128)S(1)}, u32[]{:S(2)}, u32[]{:S(2)}) %all-to-all-start.1) | async-done | bytes 262176 | tf_op jit(solution)/shard_map/all_to_all | solution.py:293
  (155 shorter events, 83.2 us)
Async XLA Ops:
  7.2 237.5 %all-gather.5.cloned.1.call-start = ((), (), s32[]{:S(2)}) async-start(), calls=%async_computation.2 | async-start | bytes 9052160 | tf_op jit(solution)/shard_map/all_gather | solution.py:282
  11.9 10.8 %collective-permute-start.2 = (bf16[6,1664]{1,0:T(8,128)(2,1)S(1)}, bf16[6,1664]{1,0:T(8,128)(2,1)S(1)}, u32[]{:S(2)}, u32[]{:S(2)}) collective-permute-start(bf16[6,1664]{1,0:T(8,128)(2,1)S(1)} %broadcast_select_fusion.1), channel_id=1, source_target_pairs={{0,1},{1,0},{2,3},{3,2},{4,5},{5,4},{6,7},{7,6},{8,9},{9,8},{10,11... | collective-permute-start | bytes 59912 | tf_op jit(solution)/shard_map/ppermute | solution.py:18
  20.7 7.5 %collective-permute-start.1 = (bf16[26,1664]{1,0:T(8,128)(2,1)S(1)}, bf16[26,1664]{1,0:T(8,128)(2,1)S(1)}, u32[]{:S(2)}, u32[]{:S(2)}) collective-permute-start(bf16[26,1664]{1,0:T(8,128)(2,1)S(1)} %bitcast.66), channel_id=1, source_target_pairs={{1,256},{129,384},{256,1},{384,129},{3,258},{131,386},{258,3},{386... | collective-permute-start | bytes 259592 | tf_op jit(solution)/shard_map/ppermute | solution.py:254
  30.6 39.8 %collective-permute-start.5 = (bf16[22,1664]{1,0:T(8,128)(2,1)S(1)}, bf16[22,1664]{1,0:T(8,128)(2,1)S(1)}, u32[]{:S(2)}, u32[]{:S(2)}) collective-permute-start(bf16[22,1664]{1,0:T(8,128)(2,1)S(1)} %slice.89), channel_id=1, source_target_pairs={{96,0},{104,8},{112,16},{120,24},{0,32},{8,40},{16,48},{24,56},{32... | collective-permute-start | bytes 219656 | tf_op jit(solution)/shard_map/ppermute | solution.py:215
  34.0 36.4 %collective-permute-start.4 = (bf16[22,1664]{1,0:T(8,128)(2,1)S(1)}, bf16[22,1664]{1,0:T(8,128)(2,1)S(1)}, u32[]{:S(2)}, u32[]{:S(2)}) collective-permute-start(bf16[22,1664]{1,0:T(8,128)(2,1)S(1)} %slice.89), channel_id=1, source_target_pairs={{64,0},{72,8},{80,16},{88,24},{96,32},{104,40},{112,48},{120,56},{... | collective-permute-start | bytes 219656 | tf_op jit(solution)/shard_map/ppermute | solution.py:215
  44.7 25.7 %collective-permute-start.3 = (bf16[22,1664]{1,0:T(8,128)(2,1)S(1)}, bf16[22,1664]{1,0:T(8,128)(2,1)S(1)}, u32[]{:S(2)}, u32[]{:S(2)}) collective-permute-start(bf16[22,1664]{1,0:T(8,128)(2,1)S(1)} %slice.89), channel_id=1, source_target_pairs={{32,0},{40,8},{48,16},{56,24},{64,32},{72,40},{80,48},{88,56},{96,... | collective-permute-start | bytes 219656 | tf_op jit(solution)/shard_map/ppermute | solution.py:215
  70.5 13.6 %collective-permute-start.6 = (bf16[4,22,1664]{2,1,0:T(8,128)(2,1)S(1)}, bf16[4,22,1664]{2,1,0:T(8,128)(2,1)S(1)}, u32[]{:S(2)}, u32[]{:S(2)}) collective-permute-start(bf16[4,22,1664]{2,1,0:T(8,128)(2,1)S(1)} %pad_maximum_fusion.5), channel_id=1, source_target_pairs={{8,0},{16,8},{24,16},{32,24},{40,32},{48,40},{56,48},{64,56},{72,6... | collective-permute-start | bytes 878600 | tf_op jit(solution)/shard_map/ppermute | solution.py:215
  73.3 17.0 %collective-permute-start.8 = (bf16[4,22,1664]{2,1,0:T(8,128)(2,1)S(1)}, bf16[4,22,1664]{2,1,0:T(8,128)(2,1)S(1)}, u32[]{:S(2)}, u32[]{:S(2)}) collective-permute-start(bf16[4,22,1664]{2,1,0:T(8,128)(2,1)S(1)} %pad_maximum_fusion.5), channel_id=1, source_target_pairs={{120,0},{0,8},{8,16},{16,24},{24,32},{32,40},{40,48},{48,56},{56,6... | collective-permute-start | bytes 878600 | tf_op jit(solution)/shard_map/ppermute | solution.py:215
  76.7 18.1 %collective-permute-start.9 = (bf16[2,22,1664]{2,1,0:T(8,128)(2,1)S(1)}, bf16[2,22,1664]{2,1,0:T(8,128)(2,1)S(1)}, u32[]{:S(2)}, u32[]{:S(2)}) collective-permute-start(bf16[2,22,1664]{2,1,0:T(8,128)(2,1)S(1)} %get-tuple-element.28), channel_id=1, source_target_pairs={{112,0},{120,8},{0,16},{8,24},{16,32},{24,40},{32,48},{40,56},{48,... | collective-permute-start | bytes 439304 | tf_op jit(solution)/shard_map/ppermute | solution.py:215
  79.8 9.8 %collective-permute-start.7 = (bf16[2,22,1664]{2,1,0:T(8,128)(2,1)S(1)}, bf16[2,22,1664]{2,1,0:T(8,128)(2,1)S(1)}, u32[]{:S(2)}, u32[]{:S(2)}) collective-permute-start(bf16[2,22,1664]{2,1,0:T(8,128)(2,1)S(1)} %get-tuple-element.29), channel_id=1, source_target_pairs={{16,0},{24,8},{32,16},{40,24},{48,32},{56,40},{64,48},{72,56},{80,... | collective-permute-start | bytes 439304 | tf_op jit(solution)/shard_map/ppermute | solution.py:215
  111.1 11.2 %collective-permute-start.12 = (bf16[176,1664]{1,0:T(8,128)(2,1)}, bf16[176,1664]{1,0:T(8,128)(2,1)}, u32[]{:S(2)}, u32[]{:S(2)}) collective-permute-start(bf16[176,1664]{1,0:T(8,128)(2,1)} %squeeze.19), channel_id=1, source_target_pairs={{0,128},{1,385},{128,256},{129,1},{256,384},{257,129},{384,0},{385... | collective-permute-start | bytes 1757192 | tf_op jit(solution)/shard_map/ppermute | solution.py:185
  116.2 11.5 %collective-permute-start.10 = (bf16[176,1664]{1,0:T(8,128)(2,1)}, bf16[176,1664]{1,0:T(8,128)(2,1)}, u32[]{:S(2)}, u32[]{:S(2)}) collective-permute-start(bf16[176,1664]{1,0:T(8,128)(2,1)} %squeeze.18), channel_id=1, source_target_pairs={{0,2},{1,7},{2,4},{3,1},{4,6},{5,3},{6,0},{7,5},{8,10},{9,15},{10,... | collective-permute-start | bytes 1757192 | tf_op jit(solution)/shard_map/ppermute | solution.py:185
  123.7 28.8 %collective-permute-start.15 = (bf16[2,176,1664]{2,1,0:T(8,128)(2,1)S(1)}, bf16[2,176,1664]{2,1,0:T(8,128)(2,1)S(1)}, u32[]{:S(2)}, u32[]{:S(2)}) collective-permute-start(bf16[2,176,1664]{2,1,0:T(8,128)(2,1)S(1)} %pad_maximum_fusion.1.refs_8_), channel_id=1, source_target_pairs={{0,2},{1,7},{2,4},{3,1},{4,6},{5,3},{6,0},{7,5},{8,10},{9,15},{10,... | collective-permute-start | bytes 3514376 | tf_op jit(solution)/shard_map/ppermute | solution.py:185
  129.0 23.5 %collective-permute-start.14 = (bf16[2,176,1664]{2,1,0:T(8,128)(2,1)S(1)}, bf16[2,176,1664]{2,1,0:T(8,128)(2,1)S(1)}, u32[]{:S(2)}, u32[]{:S(2)}) collective-permute-start(bf16[2,176,1664]{2,1,0:T(8,128)(2,1)S(1)} %pad_maximum_fusion.refs_0_), channel_id=1, source_target_pairs={{0,128},{1,385},{128,256},{129,1},{256,384},{257,129},{384,0},{385... | collective-permute-start | bytes 3514376 | tf_op jit(solution)/shard_map/ppermute | solution.py:185
  133.7 13.5 %collective-permute-start.11 = (bf16[176,1664]{1,0:T(8,128)(2,1)}, bf16[176,1664]{1,0:T(8,128)(2,1)S(1)}, u32[]{:S(2)}, u32[]{:S(2)}) collective-permute-start(bf16[176,1664]{1,0:T(8,128)(2,1)} %collective-permute-done.10), channel_id=1, source_target_pairs={{0,2},{1,7},{2,4},{3,1},{4,6},{5,3},{6,0},{7,5},{8,10},{9,15},{10,... | collective-permute-start | bytes 1757192 | tf_op jit(solution)/shard_map/ppermute | solution.py:185
  136.6 15.9 %collective-permute-start.13 = (bf16[176,1664]{1,0:T(8,128)(2,1)}, bf16[176,1664]{1,0:T(8,128)(2,1)S(1)}, u32[]{:S(2)}, u32[]{:S(2)}) collective-permute-start(bf16[176,1664]{1,0:T(8,128)(2,1)} %collective-permute-done.12), channel_id=1, source_target_pairs={{0,128},{1,385},{128,256},{129,1},{256,384},{257,129},{384,0},{385... | collective-permute-start | bytes 1757192 | tf_op jit(solution)/shard_map/ppermute | solution.py:185
  152.5 29.4 %collective-permute-start.18 = (bf16[2,176,1664]{2,1,0:T(8,128)(2,1)S(1)}, bf16[2,176,1664]{2,1,0:T(8,128)(2,1)}, u32[]{:S(2)}, u32[]{:S(2)}) collective-permute-start(bf16[2,176,1664]{2,1,0:T(8,128)(2,1)S(1)} %collective-permute-done.14.refs_1_), channel_id=1, source_target_pairs={{0,128},{1,385},{128,256},{129,1},{256,384},{257,129},{384,0},{385... | collective-permute-start | bytes 3514376 | tf_op jit(solution)/shard_map/ppermute | solution.py:185
  158.4 23.5 %collective-permute-start.19 = (bf16[2,176,1664]{2,1,0:T(8,128)(2,1)S(1)}, bf16[2,176,1664]{2,1,0:T(8,128)(2,1)}, u32[]{:S(2)}, u32[]{:S(2)}) collective-permute-start(bf16[2,176,1664]{2,1,0:T(8,128)(2,1)S(1)} %collective-permute-done.15.refs_9_), channel_id=1, source_target_pairs={{0,2},{1,7},{2,4},{3,1},{4,6},{5,3},{6,0},{7,5},{8,10},{9,15},{10,... | collective-permute-start | bytes 3514376 | tf_op jit(solution)/shard_map/ppermute | solution.py:185
  161.3 20.7 %collective-permute-start.16 = (bf16[176,1664]{1,0:T(8,128)(2,1)S(1)}, bf16[176,1664]{1,0:T(8,128)(2,1)S(1)}, u32[]{:S(2)}, u32[]{:S(2)}) collective-permute-start(bf16[176,1664]{1,0:T(8,128)(2,1)S(1)} %collective-permute-done.11), channel_id=1, source_target_pairs={{0,2},{1,7},{2,4},{3,1},{4,6},{5,3},{6,0},{7,5},{8,10},{9,15},{10,... | collective-permute-start | bytes 1757192 | tf_op jit(solution)/shard_map/ppermute | solution.py:185
  163.7 18.2 %collective-permute-start.17 = (bf16[176,1664]{1,0:T(8,128)(2,1)S(1)}, bf16[176,1664]{1,0:T(8,128)(2,1)S(1)}, u32[]{:S(2)}, u32[]{:S(2)}) collective-permute-start(bf16[176,1664]{1,0:T(8,128)(2,1)S(1)} %collective-permute-done.13), channel_id=1, source_target_pairs={{0,128},{1,385},{128,256},{129,1},{256,384},{257,129},{384,0},{385... | collective-permute-start | bytes 1757192 | tf_op jit(solution)/shard_map/ppermute | solution.py:185
  182.1 17.1 %collective-permute-start.25 = (bf16[2,176,1664]{2,1,0:T(8,128)(2,1)S(1)}, bf16[2,176,1664]{2,1,0:T(8,128)(2,1)S(1)}, u32[]{:S(2)}, u32[]{:S(2)}) collective-permute-start(bf16[2,176,1664]{2,1,0:T(8,128)(2,1)S(1)} %pad_maximum_fusion.3.refs_12_), channel_id=1, source_target_pairs={{0,2},{1,7},{2,4},{3,1},{4,6},{5,3},{6,0},{7,5},{8,10},{9,15},{10,... | collective-permute-start | bytes 3514376 | tf_op jit(solution)/shard_map/ppermute | solution.py:185
  186.3 17.9 %collective-permute-start.21 = (bf16[2,176,1664]{2,1,0:T(8,128)(2,1)S(1)}, bf16[2,176,1664]{2,1,0:T(8,128)(2,1)S(1)}, u32[]{:S(2)}, u32[]{:S(2)}) collective-permute-start(bf16[2,176,1664]{2,1,0:T(8,128)(2,1)S(1)} %pad_maximum_fusion.2.refs_4_), channel_id=1, source_target_pairs={{0,128},{1,385},{128,256},{129,1},{256,384},{257,129},{384,0},{385... | collective-permute-start | bytes 3514376 | tf_op jit(solution)/shard_map/ppermute | solution.py:185
  199.2 18.1 %collective-permute-start.26 = (bf16[2,176,1664]{2,1,0:T(8,128)(2,1)S(1)}, bf16[2,176,1664]{2,1,0:T(8,128)(2,1)}, u32[]{:S(2)}, u32[]{:S(2)}) collective-permute-start(bf16[2,176,1664]{2,1,0:T(8,128)(2,1)S(1)} %collective-permute-done.25.refs_13_), channel_id=1, source_target_pairs={{0,2},{1,7},{2,4},{3,1},{4,6},{5,3},{6,0},{7,5},{8,10},{9,15},{10,... | collective-permute-start | bytes 3514376 | tf_op jit(solution)/shard_map/ppermute | solution.py:185
  204.2 18.1 %collective-permute-start.22 = (bf16[2,176,1664]{2,1,0:T(8,128)(2,1)S(1)}, bf16[2,176,1664]{2,1,0:T(8,128)(2,1)}, u32[]{:S(2)}, u32[]{:S(2)}) collective-permute-start(bf16[2,176,1664]{2,1,0:T(8,128)(2,1)S(1)} %collective-permute-done.21.refs_5_), channel_id=1, source_target_pairs={{0,128},{1,385},{128,256},{129,1},{256,384},{257,129},{384,0},{385... | collective-permute-start | bytes 3514376 | tf_op jit(solution)/shard_map/ppermute | solution.py:185
  207.6 46.1 %collective-permute-start.20 = (bf16[2,176,1664]{2,1,0:T(8,128)(2,1)}, bf16[2,176,1664]{2,1,0:T(8,128)(2,1)}, u32[]{:S(2)}, u32[]{:S(2)}) collective-permute-start(bf16[2,176,1664]{2,1,0:T(8,128)(2,1)} %collective-permute-done.18.refs_2_), channel_id=1, source_target_pairs={{0,128},{1,385},{128,256},{129,1},{256,384},{257,129},{384,0},{385... | collective-permute-start | bytes 3514376 | tf_op jit(solution)/shard_map/ppermute | solution.py:185
  209.6 44.1 %collective-permute-start.24 = (bf16[2,176,1664]{2,1,0:T(8,128)(2,1)}, bf16[2,176,1664]{2,1,0:T(8,128)(2,1)}, u32[]{:S(2)}, u32[]{:S(2)}) collective-permute-start(bf16[2,176,1664]{2,1,0:T(8,128)(2,1)} %collective-permute-done.19.refs_10_), channel_id=1, source_target_pairs={{0,2},{1,7},{2,4},{3,1},{4,6},{5,3},{6,0},{7,5},{8,10},{9,15},{10,... | collective-permute-start | bytes 3514376 | tf_op jit(solution)/shard_map/ppermute | solution.py:185
  217.3 36.4 %collective-permute-start.27 = (bf16[2,176,1664]{2,1,0:T(8,128)(2,1)}, bf16[2,176,1664]{2,1,0:T(8,128)(2,1)}, u32[]{:S(2)}, u32[]{:S(2)}) collective-permute-start(bf16[2,176,1664]{2,1,0:T(8,128)(2,1)} %collective-permute-done.26.refs_14_), channel_id=1, source_target_pairs={{0,2},{1,7},{2,4},{3,1},{4,6},{5,3},{6,0},{7,5},{8,10},{9,15},{10,... | collective-permute-start | bytes 3514376 | tf_op jit(solution)/shard_map/ppermute | solution.py:185
  222.4 31.3 %collective-permute-start.23 = (bf16[2,176,1664]{2,1,0:T(8,128)(2,1)}, bf16[2,176,1664]{2,1,0:T(8,128)(2,1)}, u32[]{:S(2)}, u32[]{:S(2)}) collective-permute-start(bf16[2,176,1664]{2,1,0:T(8,128)(2,1)} %collective-permute-done.22.refs_6_), channel_id=1, source_target_pairs={{0,128},{1,385},{128,256},{129,1},{256,384},{257,129},{384,0},{385... | collective-permute-start | bytes 3514376 | tf_op jit(solution)/shard_map/ppermute | solution.py:185
  227.8 15.8 %collective-permute-start = (bf16[128,1664]{1,0:T(8,128)(2,1)S(1)}, bf16[128,1664]{1,0:T(8,128)(2,1)}, u32[]{:S(2)}, u32[]{:S(2)}) collective-permute-start(bf16[128,1664]{1,0:T(8,128)(2,1)S(1)} %fusion.6), channel_id=1, source_target_pairs={{0,1},{1,0},{2,3},{3,2},{4,5},{5,4},{6,7},{7,6},{8,9},{9,8},{10,11... | collective-permute-start | bytes 1277960 | tf_op jit(solution)/shard_map/ppermute | solution.py:18
  251.4 21.1 %collective-permute-start.29 = (bf16[256,1280]{1,0:T(8,128)(2,1)S(1)}, bf16[256,1280]{1,0:T(8,128)(2,1)S(1)}, u32[]{:S(2)}, u32[]{:S(2)}) collective-permute-start(bf16[256,1280]{1,0:T(8,128)(2,1)S(1)} %shard_map.95), channel_id=1, source_target_pairs={{0,1},{1,0},{2,3},{3,2},{4,5},{5,4},{6,7},{7,6},{8,9},{9,8},{10,11... | collective-permute-start | bytes 1966088 | tf_op jit(solution)/shard_map/ppermute | solution.py:18
  263.1 9.4 %collective-permute-start.28 = (bf16[128,1664]{1,0:T(8,128)(2,1)S(1)}, bf16[128,1664]{1,0:T(8,128)(2,1)S(1)}, u32[]{:S(2)}, u32[]{:S(2)}) collective-permute-start(bf16[128,1664]{1,0:T(8,128)(2,1)S(1)} %shard_map.94), channel_id=1, source_target_pairs={{0,1},{1,0},{2,3},{3,2},{4,5},{5,4},{6,7},{7,6},{8,9},{9,8},{10,11... | collective-permute-start | bytes 1277960 | tf_op jit(solution)/shard_map/ppermute | solution.py:18
  305.5 14.7 %all-to-all-start.1 = ((f32[16,16,256]{2,1,0:T(8,128)}), f32[16,16,256]{2,1,0:T(8,128)S(1)}, u32[]{:S(2)}, u32[]{:S(2)}) async-start(f32[16,16,256]{2,1,0:T(8,128)} %broadcast_in_dim.36), calls=%async_computation.1 | async-start | bytes 524288 | tf_op jit(solution)/shard_map/all_to_all | solution.py:293
  (18 other events, 441.2 us)
Sparse Core Ops, SparseCore 0:
  73.4 109.1 all-gather.4

commit v4 on v3

--- a/solution.py
+++ b/solution.py
@@ -98,7 +98,7 @@
 
 
 def tower_kernel(head, tail, share, last, place_ref, act_ref, *refs):
-    pieces, ring, refs = refs[:16], refs[16], refs[17:]
+    pieces, ring, refs = refs[:24], refs[24], refs[25:]
     if last:
         scale_ref, units_ref, row_ref, act, weight, normed, sems, proj, extra_sem = refs
     else:
@@ -118,7 +118,8 @@
                 )
         for inner in range(4):
             for outer in range(4):
-                source = pieces[zh * 8 + (inner // 2) * 4 + outer].at[inner % 2]
+                source = pieces[zh * 12 + min(inner, 2) * 4 + outer]
+                source = source if inner < 2 else source.at[inner - 2]
                 by_x, by_y = (inner, outer) if zh == 0 else (outer, inner)
                 from_x, from_y = (x + 4 + sign * by_x) % 4, (y + 4 + sign * by_y) % 4
                 layer = 2 * (from_y % 2) + zh
@@ -171,7 +172,7 @@
     return pl.pallas_call(
         functools.partial(tower_kernel, head, tail, share, last),
         out_shape=out_shape,
-        in_specs=[smem, vmem] + [anywhere] * 17 + more_specs,
+        in_specs=[smem, vmem] + [anywhere] * 25 + more_specs,
         out_specs=vmem,
         scratch_shapes=scratch,
         compiler_params=pltpu.CompilerParams(vmem_limit_bytes=40 * 1024 * 1024),
@@ -189,30 +190,32 @@
 
 
 def gather_plane(block_one, block_two):
-    axes = (("x", "y"), ("y", "x"))
-    start = [block_one, block_two]
-    first = [hop(start[i], axes[i][0]) for i in range(2)]
-    near = [jnp.stack([start[i], first[i]]) for i in range(2)]
-    second = [hop(first[i], axes[i][0]) for i in range(2)]
-    near_one = [hop(near[i], axes[i][1]) for i in range(2)]
-    second, near_one = lax.optimization_barrier((second, near_one))
-    third = [hop(second[i], axes[i][0]) for i in range(2)]
-    near_two = [hop(near_one[i], axes[i][1]) for i in range(2)]
-    third, near_two = lax.optimization_barrier((third, near_two))
-    far = [jnp.stack([second[i], third[i]]) for i in range(2)]
-    far_one = [hop(far[i], axes[i][1]) for i in range(2)]
-    near_three = [hop(near_two[i], axes[i][1]) for i in range(2)]
-    far_two = [hop(far_one[i], axes[i][1]) for i in range(2)]
-    far_three = [hop(far_two[i], axes[i][1]) for i in range(2)]
-    pairs = []
-    for i in range(2):
-        pairs += [near[i], near_one[i], near_two[i], near_three[i]]
-        pairs += [far[i], far_one[i], far_two[i], far_three[i]]
-    return pairs
+    pieces = []
+    for block, axis_one, axis_two in ((block_one, "x", "y"), (block_two, "y", "x")):
+        own = [block, hop(block, axis_two)]
+        one, own[1] = lax.optimization_barrier((hop(block, axis_one), own[1]))
+        near = [one, hop(one, axis_two)]
+        two, near[1] = lax.optimization_barrier((hop(one, axis_one), near[1]))
+        pair = [jnp.stack([two, hop(two, axis_one)])]
+        for chain in (own, near, pair):
+            while len(chain) < 4:
+                chain.append(hop(chain[-1], axis_two))
+            pieces += chain
+    return pieces
 
 
 def ahead_on_ring(value, steps):
     return lax.ppermute(value, Z, [((i + steps) % 16, i) for i in range(16)])
+
+
+def line_kernel(position_ref, stack, one, two_a, two_b, three, out_ref):
+    for k in range(4):
+        blocks = (
+            (4 * k, stack[k]), (4 * k + 1, one[k]), (4 * k + 15, three[k]),
+            ((2, 6)[k] if k < 2 else (14, 10)[k - 2], two_a[k] if k < 2 else two_b[k - 2]),
+        )
+        for ahead, block in blocks:
+            out_ref[(position_ref[0] + ahead) % 16] = block
 
 
 def gather_ring(block, position):
@@ -221,15 +224,16 @@
         near[ahead] = ahead_on_ring(block, ahead)
     stack = jnp.stack([near[ahead] for ahead in (0, 4, 8, 12)])
     one, three = ahead_on_ring(stack, 1), ahead_on_ring(stack, -1)
-    two_a = ahead_on_ring(jnp.stack([near[0], near[4]]), 2)
+    two_a = ahead_on_ring(stack[:2], 2)
     two_b = ahead_on_ring(jnp.stack([near[0], near[12]]), -2)
-    blocks = {2: two_a[0], 6: two_a[1], 14: two_b[0], 10: two_b[1]}
-    for k in range(4):
-        blocks[4 * k] = stack[k]
-        blocks[4 * k + 1] = one[k]
-        blocks[(4 * k + 15) % 16] = three[k]
-    line = jnp.stack([blocks[k % 16] for k in range(32)])
-    return lax.dynamic_slice_in_dim(line, (16 - position) % 16, 16, 0)
+    vmem = pl.BlockSpec(memory_space=pltpu.VMEM)
+    return pl.pallas_call(
+        line_kernel,
+        out_shape=jax.ShapeDtypeStruct((16,) + block.shape, block.dtype),
+        in_specs=[pl.BlockSpec(memory_space=pltpu.SMEM)] + [vmem] * 5,
+        out_specs=vmem,
+        compiler_params=pltpu.CompilerParams(vmem_limit_bytes=16 * 1024 * 1024),
+    )(position[None], stack, one, two_a, two_b, three)
 
 
 def on_device(images, text_pooled, image_weight, proj_image, proj_text, logit_scale, pairing):
@@ -270,6 +274,7 @@
     image = jnp.where(at_home, image, swap(image))
 
     small = jnp.concatenate([weight[head:], extra])
+    small = jnp.pad(small, ((0, 24 - small.shape[0]), (0, 0)))
     small, block = lax.optimization_barrier((small, weight[:head]))
     spread = lax.all_gather(small, ("y", "x"), axis=0)
     column = gather_ring(block, zh * 8 + zl).reshape(2, 8 * head, width)
@@ -279,6 +284,7 @@
         spread[:, tail:tail + share].reshape(16 * share, width),
         spread[:, tail + share],
     ])
+    plane_rows, column = lax.optimization_barrier((plane_rows, column))
     ring = lax.all_gather(plane_rows, Z, axis=0)
     pieces = gather_plane(column[0], column[1])
 

time: 331 us -> 313 us (0.946)
  starting transfers between devices: 133 us -> 156 us
  local copies, waits for them, and re-layouts: 36.5 us -> 21.8 us
  waiting for transfers between devices: 69.1 us -> 54.8 us
  blocking collectives: 36.3 us -> 23.2 us
    ppermute x18 -> x24, waiting for transfers between devices: 48.4 us -> 23.7 us  [hop(): lax.ppermute(value, (axis, 'c'), [(i * 2 + c, (i + 1 - 2 * c) % 4 * 2 + c...]
    ppermute x18 -> x24, starting transfers between devices: 56.3 us -> 80.4 us  [hop(): lax.ppermute(value, (axis, 'c'), [(i * 2 + c, (i + 1 - 2 * c) % 4 * 2 + c...]
    all_gather x1 -> x0, blocking collectives: 19.3 us -> none  [on_device(): spread = lax.all_gather(small, ('y', 'x'), axis=0)]
    unnamed x67 -> x60, local copies, waits for them, and re-layouts: 27.4 us -> 11 us
    ppermute x7, waiting for transfers between devices: 4.9 us -> 13.7 us  [ahead_on_ring(): return lax.ppermute(value, Z, [((i + steps) % 16, i) for i in range(16)])]
    all_to_all x1, blocking collectives: 17 us -> 23.2 us  [on_device(): lax.all_to_all(jnp.broadcast_to(row[None], (16, 1, count)), Z, 0, 0, tile...]
  transfers between devices with their start and end apart: 33 -> 40, of which waited for: 12 -> 18; matrix products, arithmetic and copies ran while one was open for 10% -> 2% of each run, Pallas kernels for 4% -> 4%
where the time goes in v4:
time: 313 us; the launch traced here: 311 us
  starting transfers between devices  156 us (50%)
  waiting for transfers between devices  54.8 us (18%)
  Pallas kernels  25.1 us (8%)
  blocking collectives  23.2 us (7%)
  local copies, waits for them, and re-layouts  21.8 us (7%)
  between operations  15.6 us (5%)
  matrix products  8.57 us (3%)
  other arithmetic  5.76 us (2%)
    ppermute x24, starting transfers between devices, hop(): lax.ppermute(value, (axis, 'c'), [(i * 2 + c, (i + 1 - 2 * c) % 4 * 2 + c...  80.4 us
    ppermute x5, starting transfers between devices, swap(): return lax.ppermute(value, 'c', [(0, 1), (1, 0)])  34.2 us
    ppermute x7, starting transfers between devices, ahead_on_ring(): return lax.ppermute(value, Z, [((i + steps) % 16, i) for i in range(16)])  33.1 us
    ppermute x24, waiting for transfers between devices, hop(): lax.ppermute(value, (axis, 'c'), [(i * 2 + c, (i + 1 - 2 * c) % 4 * 2 + c...  23.7 us
    all_to_all x1, blocking collectives, on_device(): lax.all_to_all(jnp.broadcast_to(row[None], (16, 1, count)), Z, 0, 0, tile...  23.2 us
    pallas_call x2, Pallas kernels, tower(): pl.pallas_call(functools.partial(tower_kernel, head, tail, share, last),...  21.6 us
    ppermute x7, waiting for transfers between devices, ahead_on_ring(): return lax.ppermute(value, Z, [((i + steps) % 16, i) for i in range(16)])  13.7 us
    unnamed x60, local copies, waits for them, and re-layouts  11 us
  transfers between devices with their start and end apart: 40, of which 18 were waited for; matrix products, arithmetic and copies ran while one was open for 2% of the time, Pallas kernels for 4%

profile of v4, /device:TPU:1, one launch (start us, length us, event | category | flops | bytes accessed | tf_op | source)
XLA Modules:
  0.0 310.7 jit_solution(13225638845233488651)
XLA Ops:
  11.9 8.8 %collective-permute-start.2 = (bf16[6,1664]{1,0:T(8,128)(2,1)S(1)}, bf16[6,1664]{1,0:T(8,128)(2,1)S(1)}, u32[]{:S(2)}, u32[]{:S(2)}) collective-permute-start(bf16[6,1664]{1,0:T(8,128)(2,1)S(1)} %broadcast_select_fusion.1), channel_id=1, source_target_pairs={{0,1},{1,0},{2,3},{3,2},{4,5},{5,4},{6,7},{7,6},{8,9},{9,8},{10,11... | collective-permute-start | bytes 59912 | tf_op jit(solution)/shard_map/ppermute | solution.py:18
  22.7 5.5 %collective-permute-done.1 = bf16[26,1664]{1,0:T(8,128)(2,1)S(1)} collective-permute-done((bf16[26,1664]{1,0:T(8,128)(2,1)S(1)}, bf16[26,1664]{1,0:T(8,128)(2,1)S(1)}, u32[]{:S(2)}, u32[]{:S(2)}) %collective-permute-start.1) | collective-permute-done | bytes 86560 | tf_op jit(solution)/shard_map/ppermute | solution.py:258
  31.3 3.5 %collective-permute-start.5 = (bf16[22,1664]{1,0:T(8,128)(2,1)S(1)}, bf16[22,1664]{1,0:T(8,128)(2,1)S(1)}, u32[]{:S(2)}, u32[]{:S(2)}) collective-permute-start(bf16[22,1664]{1,0:T(8,128)(2,1)S(1)} %slice.35), channel_id=1, source_target_pairs={{96,0},{104,8},{112,16},{120,24},{0,32},{8,40},{16,48},{24,56},{32... | collective-permute-start | bytes 219656 | tf_op jit(solution)/shard_map/ppermute | solution.py:208
  34.8 10.6 %collective-permute-start.4 = (bf16[22,1664]{1,0:T(8,128)(2,1)S(1)}, bf16[22,1664]{1,0:T(8,128)(2,1)S(1)}, u32[]{:S(2)}, u32[]{:S(2)}) collective-permute-start(bf16[22,1664]{1,0:T(8,128)(2,1)S(1)} %slice.35), channel_id=1, source_target_pairs={{64,0},{72,8},{80,16},{88,24},{96,32},{104,40},{112,48},{120,56},{... | collective-permute-start | bytes 219656 | tf_op jit(solution)/shard_map/ppermute | solution.py:208
  45.4 5.2 %collective-permute-start.3 = (bf16[22,1664]{1,0:T(8,128)(2,1)S(1)}, bf16[22,1664]{1,0:T(8,128)(2,1)S(1)}, u32[]{:S(2)}, u32[]{:S(2)}) collective-permute-start(bf16[22,1664]{1,0:T(8,128)(2,1)S(1)} %slice.35), channel_id=1, source_target_pairs={{32,0},{40,8},{48,16},{56,24},{64,32},{72,40},{80,48},{88,56},{96,... | collective-permute-start | bytes 219656 | tf_op jit(solution)/shard_map/ppermute | solution.py:208
  50.9 6.9 %collective-permute-done.3 = bf16[22,1664]{1,0:T(8,128)(2,1)S(1)} collective-permute-done((bf16[22,1664]{1,0:T(8,128)(2,1)S(1)}, bf16[22,1664]{1,0:T(8,128)(2,1)S(1)}, u32[]{:S(2)}, u32[]{:S(2)}) %collective-permute-start.3) | collective-permute-done | bytes 73248 | tf_op jit(solution)/shard_map/ppermute | solution.py:208
  59.8 4.6 %collective-permute-start.6 = (bf16[4,22,1664]{2,1,0:T(8,128)(2,1)S(1)}, bf16[4,22,1664]{2,1,0:T(8,128)(2,1)S(1)}, u32[]{:S(2)}, u32[]{:S(2)}) collective-permute-start(bf16[4,22,1664]{2,1,0:T(8,128)(2,1)S(1)} %pad_maximum_fusion.3.stack), channel_id=1, source_target_pairs={{8,0},{16,8},{24,16},{32,24},{40,32},{48,40},{56,48},{64,56},{72,6... | collective-permute-start | bytes 878600 | tf_op jit(solution)/shard_map/ppermute | solution.py:208
  66.3 5.5 %collective-permute-start.7 = (bf16[2,22,1664]{2,1,0:T(8,128)(2,1)S(1)}, bf16[2,22,1664]{2,1,0:T(8,128)(2,1)S(1)}, u32[]{:S(2)}, u32[]{:S(2)}) collective-permute-start(bf16[2,22,1664]{2,1,0:T(8,128)(2,1)S(1)} %get-tuple-element.33), channel_id=1, source_target_pairs={{16,0},{24,8},{32,16},{40,24},{48,32},{56,40},{64,48},{72,56},{80,... | collective-permute-start | bytes 439304 | tf_op jit(solution)/shard_map/ppermute | solution.py:208
  71.8 3.8 %collective-permute-done.8.two_b = bf16[2,22,1664]{2,1,0:T(8,128)(2,1)S(1)} collective-permute-done((bf16[2,22,1664]{2,1,0:T(8,128)(2,1)S(1)}, bf16[2,22,1664]{2,1,0:T(8,128)(2,1)S(1)}, u32[]{:S(2)}, u32[]{:S(2)}) %collective-permute-start.8) | collective-permute-done | bytes 146464 | tf_op jit(solution)/shard_map/ppermute | solution.py:208
  95.7 4.0 %collective-permute-start.11 = (bf16[176,1664]{1,0:T(8,128)(2,1)S(1)}, bf16[176,1664]{1,0:T(8,128)(2,1)S(1)}, u32[]{:S(2)}, u32[]{:S(2)}) collective-permute-start(bf16[176,1664]{1,0:T(8,128)(2,1)S(1)} %get-tuple-element.31.refs_0_), channel_id=1, source_target_pairs={{0,128},{1,385},{128,256},{129,1},{256,384},{257,129},{384,0},{385... | collective-permute-start | bytes 1757192 | tf_op jit(solution)/shard_map/ppermute | solution.py:186
  112.5 4.3 %collective-permute-start.14 = (bf16[176,1664]{1,0:T(8,128)(2,1)S(1)}, bf16[176,1664]{1,0:T(8,128)(2,1)S(1)}, u32[]{:S(2)}, u32[]{:S(2)}) collective-permute-start(bf16[176,1664]{1,0:T(8,128)(2,1)S(1)} %collective-permute-done.10.refs_4_), channel_id=1, source_target_pairs={{0,2},{1,7},{2,4},{3,1},{4,6},{5,3},{6,0},{7,5},{8,10},{9,15},{10,... | collective-permute-start | bytes 1757192 | tf_op jit(solution)/shard_map/ppermute | solution.py:186
  124.0 5.0 %collective-permute-start.18 = (bf16[176,1664]{1,0:T(8,128)(2,1)S(1)}, bf16[176,1664]{1,0:T(8,128)(2,1)S(1)}, u32[]{:S(2)}, u32[]{:S(2)}) collective-permute-start(bf16[176,1664]{1,0:T(8,128)(2,1)S(1)} %collective-permute-done.14), channel_id=1, source_target_pairs={{0,2},{1,7},{2,4},{3,1},{4,6},{5,3},{6,0},{7,5},{8,10},{9,15},{10,... | collective-permute-start | bytes 1757192 | tf_op jit(solution)/shard_map/ppermute | solution.py:186
  131.6 3.7 %collective-permute-start.30 = (bf16[176,1664]{1,0:T(8,128)(2,1)S(1)}, bf16[176,1664]{1,0:T(8,128)(2,1)S(1)}, u32[]{:S(2)}, u32[]{:S(2)}) collective-permute-start(bf16[176,1664]{1,0:T(8,128)(2,1)S(1)} %collective-permute-done.26), channel_id=1, source_target_pairs={{0,128},{1,385},{128,256},{129,1},{256,384},{257,129},{384,0},{385... | collective-permute-start | bytes 1757192 | tf_op jit(solution)/shard_map/ppermute | solution.py:186
  138.9 3.6 %collective-permute-done.30 = bf16[176,1664]{1,0:T(8,128)(2,1)S(1)} collective-permute-done((bf16[176,1664]{1,0:T(8,128)(2,1)S(1)}, bf16[176,1664]{1,0:T(8,128)(2,1)S(1)}, u32[]{:S(2)}, u32[]{:S(2)}) %collective-permute-start.30) | collective-permute-done | bytes 585760 | tf_op jit(solution)/shard_map/ppermute | solution.py:186
  142.7 3.7 %collective-permute-start.31 = (bf16[2,176,1664]{2,1,0:T(8,128)(2,1)S(1)}, bf16[2,176,1664]{2,1,0:T(8,128)(2,1)S(1)}, u32[]{:S(2)}, u32[]{:S(2)}) collective-permute-start(bf16[2,176,1664]{2,1,0:T(8,128)(2,1)S(1)} %pad_maximum_fusion.1.refs_20_), channel_id=1, source_target_pairs={{0,2},{1,7},{2,4},{3,1},{4,6},{5,3},{6,0},{7,5},{8,10},{9,15},{10,... | collective-permute-start | bytes 3514376 | tf_op jit(solution)/shard_map/ppermute | solution.py:186
  146.4 8.7 %collective-permute-done.19.refs_9_ = bf16[2,176,1664]{2,1,0:T(8,128)(2,1)S(1)} collective-permute-done((bf16[2,176,1664]{2,1,0:T(8,128)(2,1)S(1)}, bf16[2,176,1664]{2,1,0:T(8,128)(2,1)S(1)}, u32[]{:S(2)}, u32[]{:S(2)}) %collective-permute-start.19) | collective-permute-done | bytes 1171488 | tf_op jit(solution)/shard_map/ppermute | solution.py:186
  155.1 4.9 %collective-permute-start.20 = (bf16[2,176,1664]{2,1,0:T(8,128)(2,1)S(1)}, bf16[2,176,1664]{2,1,0:T(8,128)(2,1)}, u32[]{:S(2)}, u32[]{:S(2)}) collective-permute-start(bf16[2,176,1664]{2,1,0:T(8,128)(2,1)S(1)} %collective-permute-done.19.refs_9_), channel_id=1, source_target_pairs={{0,128},{1,385},{128,256},{129,1},{256,384},{257,129},{384,0},{385... | collective-permute-start | bytes 3514376 | tf_op jit(solution)/shard_map/ppermute | solution.py:186
  160.0 4.8 %collective-permute-start.32 = (bf16[2,176,1664]{2,1,0:T(8,128)(2,1)S(1)}, bf16[2,176,1664]{2,1,0:T(8,128)(2,1)}, u32[]{:S(2)}, u32[]{:S(2)}) collective-permute-start(bf16[2,176,1664]{2,1,0:T(8,128)(2,1)S(1)} %collective-permute-done.31.refs_21_), channel_id=1, source_target_pairs={{0,2},{1,7},{2,4},{3,1},{4,6},{5,3},{6,0},{7,5},{8,10},{9,15},{10,... | collective-permute-start | bytes 3514376 | tf_op jit(solution)/shard_map/ppermute | solution.py:186
  166.8 3.8 %collective-permute-start.12 = (bf16[176,1664]{1,0:T(8,128)(2,1)S(1)}, bf16[176,1664]{1,0:T(8,128)(2,1)S(1)}, u32[]{:S(2)}, u32[]{:S(2)}) collective-permute-start(bf16[176,1664]{1,0:T(8,128)(2,1)S(1)} %collective-permute-done.11.refs_1_), channel_id=1, source_target_pairs={{0,128},{1,385},{128,256},{129,1},{256,384},{257,129},{384,0},{385... | collective-permute-start | bytes 1757192 | tf_op jit(solution)/shard_map/ppermute | solution.py:186
  174.0 6.6 %collective-permute-start = (bf16[128,1664]{1,0:T(8,128)(2,1)}, bf16[128,1664]{1,0:T(8,128)(2,1)S(1)}, u32[]{:S(2)}, u32[]{:S(2)}) collective-permute-start(bf16[128,1664]{1,0:T(8,128)(2,1)} %fusion.6), channel_id=1, source_target_pairs={{0,1},{1,0},{2,3},{3,2},{4,5},{5,4},{6,7},{7,6},{8,9},{9,8},{10,11... | collective-permute-start | bytes 1277960 | tf_op jit(solution)/shard_map/ppermute | solution.py:18
  180.6 3.6 %collective-permute-done.24.refs_14_ = bf16[176,1664]{1,0:T(8,128)(2,1)} collective-permute-done((bf16[176,1664]{1,0:T(8,128)(2,1)S(1)}, bf16[176,1664]{1,0:T(8,128)(2,1)}, u32[]{:S(2)}, u32[]{:S(2)}) %collective-permute-start.24) | collective-permute-done | bytes 585760 | tf_op jit(solution)/shard_map/ppermute | solution.py:186
  184.2 5.4 %collective-permute-start.25 = (bf16[176,1664]{1,0:T(8,128)(2,1)}, bf16[176,1664]{1,0:T(8,128)(2,1)}, u32[]{:S(2)}, u32[]{:S(2)}) collective-permute-start(bf16[176,1664]{1,0:T(8,128)(2,1)} %collective-permute-done.24.refs_14_), channel_id=1, source_target_pairs={{0,2},{1,7},{2,4},{3,1},{4,6},{5,3},{6,0},{7,5},{8,10},{9,15},{10,... | collective-permute-start | bytes 1757192 | tf_op jit(solution)/shard_map/ppermute | solution.py:186
  191.6 3.6 %collective-permute-start.16 = (bf16[176,1664]{1,0:T(8,128)(2,1)}, bf16[176,1664]{1,0:T(8,128)(2,1)}, u32[]{:S(2)}, u32[]{:S(2)}) collective-permute-start(bf16[176,1664]{1,0:T(8,128)(2,1)} %collective-permute-done.15.refs_5_), channel_id=1, source_target_pairs={{0,128},{1,385},{128,256},{129,1},{256,384},{257,129},{384,0},{385... | collective-permute-start | bytes 1757192 | tf_op jit(solution)/shard_map/ppermute | solution.py:186
  202.9 5.0 %collective-permute-start.29 = (bf16[176,1664]{1,0:T(8,128)(2,1)}, bf16[176,1664]{1,0:T(8,128)(2,1)}, u32[]{:S(2)}, u32[]{:S(2)}) collective-permute-start(bf16[176,1664]{1,0:T(8,128)(2,1)} %collective-permute-done.28.refs_18_), channel_id=1, source_target_pairs={{0,2},{1,7},{2,4},{3,1},{4,6},{5,3},{6,0},{7,5},{8,10},{9,15},{10,... | collective-permute-start | bytes 1757192 | tf_op jit(solution)/shard_map/ppermute | solution.py:186
  208.0 3.6 %collective-permute-start.17 = (bf16[176,1664]{1,0:T(8,128)(2,1)}, bf16[176,1664]{1,0:T(8,128)(2,1)}, u32[]{:S(2)}, u32[]{:S(2)}) collective-permute-start(bf16[176,1664]{1,0:T(8,128)(2,1)} %collective-permute-done.16.refs_6_), channel_id=1, source_target_pairs={{0,128},{1,385},{128,256},{129,1},{256,384},{257,129},{384,0},{385... | collective-permute-start | bytes 1757192 | tf_op jit(solution)/shard_map/ppermute | solution.py:186
  221.6 10.2 %collective-permute-start.35 = (bf16[256,1280]{1,0:T(8,128)(2,1)S(1)}, bf16[256,1280]{1,0:T(8,128)(2,1)S(1)}, u32[]{:S(2)}, u32[]{:S(2)}) collective-permute-start(bf16[256,1280]{1,0:T(8,128)(2,1)S(1)} %shard_map.96), channel_id=1, source_target_pairs={{0,1},{1,0},{2,3},{3,2},{4,5},{5,4},{6,7},{7,6},{8,9},{9,8},{10,11... | collective-permute-start | bytes 1966088 | tf_op jit(solution)/shard_map/ppermute | solution.py:18
  231.9 9.5 %shard_map.95 = bf16[128,1664]{1,0:T(8,128)(2,1)S(1)} custom-call(s32[3]{0:T(128)S(1)} %pad_add_fusion.place_ref, bf16[128,1664]{1,0:T(8,128)(2,1)S(1)} %copy-done.16, bf16[176,1664]{1,0:T(8,128)(2,1)S(1)} %copy-done.3, bf16[176,1664]{1,0:T(8,128)(2,1)S(1)} %copy-done.7, bf16[176,1664]{1,0:T(8,128)(2,1)S(1)} %copy-done.15, ...), custom_call_target="tpu_custom_call" | custom-call | flops 2835349504 | bytes 22151168 | tf_op jit(solution)/shard_map/pallas_call | solution.py:172
  241.4 6.2 %collective-permute-start.34 = (bf16[128,1664]{1,0:T(8,128)(2,1)S(1)}, bf16[128,1664]{1,0:T(8,128)(2,1)S(1)}, u32[]{:S(2)}, u32[]{:S(2)}) collective-permute-start(bf16[128,1664]{1,0:T(8,128)(2,1)S(1)} %shard_map.95), channel_id=1, source_target_pairs={{0,1},{1,0},{2,3},{3,2},{4,5},{5,4},{6,7},{7,6},{8,9},{9,8},{10,11... | collective-permute-start | bytes 1277960 | tf_op jit(solution)/shard_map/ppermute | solution.py:18
  249.0 12.2 %shard_map.97 = f32[8,256]{1,0:T(8,128)S(1)} custom-call(s32[3]{0:T(128)S(1)} %pad_add_fusion.place_ref, bf16[128,1664]{1,0:T(8,128)(2,1)S(1)} %collective-permute-done.34.act_ref, bf16[176,1664]{1,0:T(8,128)(2,1)S(1)} %copy-done.3, bf16[176,1664]{1,0:T(8,128)(2,1)S(1)} %copy-done.7, bf16[176,1664]{1,0:T(8,128)(2,1)S(1)} %copy-done.15, ...), custom_call_target="tpu_custom_call" | custom-call | flops 2835349504 | bytes 22151168 | tf_op jit(solution)/shard_map/pallas_call | solution.py:172
  264.3 23.2 %all_to_all.10 = f32[16,1,256]{2,1,0:T(1,128)S(1)} all-to-all(f32[16,1,256]{2,1,0:T(1,128)S(1)} %broadcast_in_dim.38), channel_id=1, replica_groups=mesh['y'=4,'zh'=2,'zl'=8,'x'=4,'c'=2] {'zh','zl'}, dimensions={0} | all-to-all | bytes 32768 | tf_op jit(solution)/shard_map/all_to_all | solution.py:298
  288.3 6.2 %all-to-all-start.1 = ((f32[16,16,256]{2,1,0:T(8,128)}), f32[16,16,256]{2,1,0:T(8,128)S(1)}, u32[]{:S(2)}, u32[]{:S(2)}) async-start(f32[16,16,256]{2,1,0:T(8,128)} %broadcast_in_dim.40), calls=%async_computation.1 | async-start | bytes 524288 | tf_op jit(solution)/shard_map/all_to_all | solution.py:299
  294.7 7.4 %all-to-all-done.1 = f32[16,16,256]{2,1,0:T(8,128)S(1)} async-done(((f32[16,16,256]{2,1,0:T(8,128)}), f32[16,16,256]{2,1,0:T(8,128)S(1)}, u32[]{:S(2)}, u32[]{:S(2)}) %all-to-all-start.1) | async-done | bytes 262176 | tf_op jit(solution)/shard_map/all_to_all | solution.py:299
  (157 shorter events, 91.4 us)
Async XLA Ops:
  7.2 80.4 %all-gather.5.cloned.1.call-start = ((), (), s32[]{:S(2)}) async-start(), calls=%async_computation.2 | async-start | bytes 1357824 | tf_op jit(solution)/shard_map/all_gather | solution.py:279
  31.3 182.3 %all-gather.7.cloned.1.call-start = ((), (), s32[]{:S(2)}) async-start(), calls=%async_computation.3 | async-start | bytes 9052160 | tf_op jit(solution)/shard_map/all_gather | solution.py:288
  31.3 19.3 %collective-permute-start.5 = (bf16[22,1664]{1,0:T(8,128)(2,1)S(1)}, bf16[22,1664]{1,0:T(8,128)(2,1)S(1)}, u32[]{:S(2)}, u32[]{:S(2)}) collective-permute-start(bf16[22,1664]{1,0:T(8,128)(2,1)S(1)} %slice.35), channel_id=1, source_target_pairs={{96,0},{104,8},{112,16},{120,24},{0,32},{8,40},{16,48},{24,56},{32... | collective-permute-start | bytes 219656 | tf_op jit(solution)/shard_map/ppermute | solution.py:208
  34.8 16.1 %collective-permute-start.4 = (bf16[22,1664]{1,0:T(8,128)(2,1)S(1)}, bf16[22,1664]{1,0:T(8,128)(2,1)S(1)}, u32[]{:S(2)}, u32[]{:S(2)}) collective-permute-start(bf16[22,1664]{1,0:T(8,128)(2,1)S(1)} %slice.35), channel_id=1, source_target_pairs={{64,0},{72,8},{80,16},{88,24},{96,32},{104,40},{112,48},{120,56},{... | collective-permute-start | bytes 219656 | tf_op jit(solution)/shard_map/ppermute | solution.py:208
  45.4 12.4 %collective-permute-start.3 = (bf16[22,1664]{1,0:T(8,128)(2,1)S(1)}, bf16[22,1664]{1,0:T(8,128)(2,1)S(1)}, u32[]{:S(2)}, u32[]{:S(2)}) collective-permute-start(bf16[22,1664]{1,0:T(8,128)(2,1)S(1)} %slice.35), channel_id=1, source_target_pairs={{32,0},{40,8},{48,16},{56,24},{64,32},{72,40},{80,48},{88,56},{96,... | collective-permute-start | bytes 219656 | tf_op jit(solution)/shard_map/ppermute | solution.py:208
  57.8 21.2 %collective-permute-start.9 = (bf16[4,22,1664]{2,1,0:T(8,128)(2,1)S(1)}, bf16[4,22,1664]{2,1,0:T(8,128)(2,1)S(1)}, u32[]{:S(2)}, u32[]{:S(2)}) collective-permute-start(bf16[4,22,1664]{2,1,0:T(8,128)(2,1)S(1)} %pad_maximum_fusion.3.stack), channel_id=1, source_target_pairs={{120,0},{0,8},{8,16},{16,24},{24,32},{32,40},{40,48},{48,56},{56,6... | collective-permute-start | bytes 878600 | tf_op jit(solution)/shard_map/ppermute | solution.py:208
  59.8 20.0 %collective-permute-start.6 = (bf16[4,22,1664]{2,1,0:T(8,128)(2,1)S(1)}, bf16[4,22,1664]{2,1,0:T(8,128)(2,1)S(1)}, u32[]{:S(2)}, u32[]{:S(2)}) collective-permute-start(bf16[4,22,1664]{2,1,0:T(8,128)(2,1)S(1)} %pad_maximum_fusion.3.stack), channel_id=1, source_target_pairs={{8,0},{16,8},{24,16},{32,24},{40,32},{48,40},{56,48},{64,56},{72,6... | collective-permute-start | bytes 878600 | tf_op jit(solution)/shard_map/ppermute | solution.py:208
  66.3 12.1 %collective-permute-start.7 = (bf16[2,22,1664]{2,1,0:T(8,128)(2,1)S(1)}, bf16[2,22,1664]{2,1,0:T(8,128)(2,1)S(1)}, u32[]{:S(2)}, u32[]{:S(2)}) collective-permute-start(bf16[2,22,1664]{2,1,0:T(8,128)(2,1)S(1)} %get-tuple-element.33), channel_id=1, source_target_pairs={{16,0},{24,8},{32,16},{40,24},{48,32},{56,40},{64,48},{72,56},{80,... | collective-permute-start | bytes 439304 | tf_op jit(solution)/shard_map/ppermute | solution.py:208
  95.7 12.6 %collective-permute-start.11 = (bf16[176,1664]{1,0:T(8,128)(2,1)S(1)}, bf16[176,1664]{1,0:T(8,128)(2,1)S(1)}, u32[]{:S(2)}, u32[]{:S(2)}) collective-permute-start(bf16[176,1664]{1,0:T(8,128)(2,1)S(1)} %get-tuple-element.31.refs_0_), channel_id=1, source_target_pairs={{0,128},{1,385},{128,256},{129,1},{256,384},{257,129},{384,0},{385... | collective-permute-start | bytes 1757192 | tf_op jit(solution)/shard_map/ppermute | solution.py:186
  103.1 14.6 %collective-permute-start.23 = (bf16[176,1664]{1,0:T(8,128)(2,1)S(1)}, bf16[176,1664]{1,0:T(8,128)(2,1)S(1)}, u32[]{:S(2)}, u32[]{:S(2)}) collective-permute-start(bf16[176,1664]{1,0:T(8,128)(2,1)S(1)} %get-tuple-element.30.refs_12_), channel_id=1, source_target_pairs={{0,2},{1,7},{2,4},{3,1},{4,6},{5,3},{6,0},{7,5},{8,10},{9,15},{10,... | collective-permute-start | bytes 1757192 | tf_op jit(solution)/shard_map/ppermute | solution.py:186
  105.8 11.8 %collective-permute-start.22 = (bf16[176,1664]{1,0:T(8,128)(2,1)S(1)}, bf16[176,1664]{1,0:T(8,128)(2,1)S(1)}, u32[]{:S(2)}, u32[]{:S(2)}) collective-permute-start(bf16[176,1664]{1,0:T(8,128)(2,1)S(1)} %get-tuple-element.30.refs_12_), channel_id=1, source_target_pairs={{0,128},{1,385},{128,256},{129,1},{256,384},{257,129},{384,0},{385... | collective-permute-start | bytes 1757192 | tf_op jit(solution)/shard_map/ppermute | solution.py:186
  110.6 13.4 %collective-permute-start.15 = (bf16[176,1664]{1,0:T(8,128)(2,1)S(1)}, bf16[176,1664]{1,0:T(8,128)(2,1)}, u32[]{:S(2)}, u32[]{:S(2)}) collective-permute-start(bf16[176,1664]{1,0:T(8,128)(2,1)S(1)} %collective-permute-done.10.refs_4_), channel_id=1, source_target_pairs={{0,128},{1,385},{128,256},{129,1},{256,384},{257,129},{384,0},{385... | collective-permute-start | bytes 1757192 | tf_op jit(solution)/shard_map/ppermute | solution.py:186
  112.5 11.5 %collective-permute-start.14 = (bf16[176,1664]{1,0:T(8,128)(2,1)S(1)}, bf16[176,1664]{1,0:T(8,128)(2,1)S(1)}, u32[]{:S(2)}, u32[]{:S(2)}) collective-permute-start(bf16[176,1664]{1,0:T(8,128)(2,1)S(1)} %collective-permute-done.10.refs_4_), channel_id=1, source_target_pairs={{0,2},{1,7},{2,4},{3,1},{4,6},{5,3},{6,0},{7,5},{8,10},{9,15},{10,... | collective-permute-start | bytes 1757192 | tf_op jit(solution)/shard_map/ppermute | solution.py:186
  117.6 12.2 %collective-permute-start.27 = (bf16[176,1664]{1,0:T(8,128)(2,1)S(1)}, bf16[176,1664]{1,0:T(8,128)(2,1)}, u32[]{:S(2)}, u32[]{:S(2)}) collective-permute-start(bf16[176,1664]{1,0:T(8,128)(2,1)S(1)} %collective-permute-done.22.refs_16_), channel_id=1, source_target_pairs={{0,2},{1,7},{2,4},{3,1},{4,6},{5,3},{6,0},{7,5},{8,10},{9,15},{10,... | collective-permute-start | bytes 1757192 | tf_op jit(solution)/shard_map/ppermute | solution.py:186
  124.0 12.1 %collective-permute-start.18 = (bf16[176,1664]{1,0:T(8,128)(2,1)S(1)}, bf16[176,1664]{1,0:T(8,128)(2,1)S(1)}, u32[]{:S(2)}, u32[]{:S(2)}) collective-permute-start(bf16[176,1664]{1,0:T(8,128)(2,1)S(1)} %collective-permute-done.14), channel_id=1, source_target_pairs={{0,2},{1,7},{2,4},{3,1},{4,6},{5,3},{6,0},{7,5},{8,10},{9,15},{10,... | collective-permute-start | bytes 1757192 | tf_op jit(solution)/shard_map/ppermute | solution.py:186
  136.2 18.9 %collective-permute-start.19 = (bf16[2,176,1664]{2,1,0:T(8,128)(2,1)S(1)}, bf16[2,176,1664]{2,1,0:T(8,128)(2,1)S(1)}, u32[]{:S(2)}, u32[]{:S(2)}) collective-permute-start(bf16[2,176,1664]{2,1,0:T(8,128)(2,1)S(1)} %pad_maximum_fusion.refs_8_), channel_id=1, source_target_pairs={{0,128},{1,385},{128,256},{129,1},{256,384},{257,129},{384,0},{385... | collective-permute-start | bytes 3514376 | tf_op jit(solution)/shard_map/ppermute | solution.py:186
  142.7 17.3 %collective-permute-start.31 = (bf16[2,176,1664]{2,1,0:T(8,128)(2,1)S(1)}, bf16[2,176,1664]{2,1,0:T(8,128)(2,1)S(1)}, u32[]{:S(2)}, u32[]{:S(2)}) collective-permute-start(bf16[2,176,1664]{2,1,0:T(8,128)(2,1)S(1)} %pad_maximum_fusion.1.refs_20_), channel_id=1, source_target_pairs={{0,2},{1,7},{2,4},{3,1},{4,6},{5,3},{6,0},{7,5},{8,10},{9,15},{10,... | collective-permute-start | bytes 3514376 | tf_op jit(solution)/shard_map/ppermute | solution.py:186
  155.1 40.1 %collective-permute-start.20 = (bf16[2,176,1664]{2,1,0:T(8,128)(2,1)S(1)}, bf16[2,176,1664]{2,1,0:T(8,128)(2,1)}, u32[]{:S(2)}, u32[]{:S(2)}) collective-permute-start(bf16[2,176,1664]{2,1,0:T(8,128)(2,1)S(1)} %collective-permute-done.19.refs_9_), channel_id=1, source_target_pairs={{0,128},{1,385},{128,256},{129,1},{256,384},{257,129},{384,0},{385... | collective-permute-start | bytes 3514376 | tf_op jit(solution)/shard_map/ppermute | solution.py:186
  160.0 37.4 %collective-permute-start.32 = (bf16[2,176,1664]{2,1,0:T(8,128)(2,1)S(1)}, bf16[2,176,1664]{2,1,0:T(8,128)(2,1)}, u32[]{:S(2)}, u32[]{:S(2)}) collective-permute-start(bf16[2,176,1664]{2,1,0:T(8,128)(2,1)S(1)} %collective-permute-done.31.refs_21_), channel_id=1, source_target_pairs={{0,2},{1,7},{2,4},{3,1},{4,6},{5,3},{6,0},{7,5},{8,10},{9,15},{10,... | collective-permute-start | bytes 3514376 | tf_op jit(solution)/shard_map/ppermute | solution.py:186
  164.9 19.3 %collective-permute-start.24 = (bf16[176,1664]{1,0:T(8,128)(2,1)S(1)}, bf16[176,1664]{1,0:T(8,128)(2,1)}, u32[]{:S(2)}, u32[]{:S(2)}) collective-permute-start(bf16[176,1664]{1,0:T(8,128)(2,1)S(1)} %collective-permute-done.23.refs_13_), channel_id=1, source_target_pairs={{0,2},{1,7},{2,4},{3,1},{4,6},{5,3},{6,0},{7,5},{8,10},{9,15},{10,... | collective-permute-start | bytes 1757192 | tf_op jit(solution)/shard_map/ppermute | solution.py:186
  166.8 24.7 %collective-permute-start.12 = (bf16[176,1664]{1,0:T(8,128)(2,1)S(1)}, bf16[176,1664]{1,0:T(8,128)(2,1)S(1)}, u32[]{:S(2)}, u32[]{:S(2)}) collective-permute-start(bf16[176,1664]{1,0:T(8,128)(2,1)S(1)} %collective-permute-done.11.refs_1_), channel_id=1, source_target_pairs={{0,128},{1,385},{128,256},{129,1},{256,384},{257,129},{384,0},{385... | collective-permute-start | bytes 1757192 | tf_op jit(solution)/shard_map/ppermute | solution.py:186
  174.0 15.6 %collective-permute-start = (bf16[128,1664]{1,0:T(8,128)(2,1)}, bf16[128,1664]{1,0:T(8,128)(2,1)S(1)}, u32[]{:S(2)}, u32[]{:S(2)}) collective-permute-start(bf16[128,1664]{1,0:T(8,128)(2,1)} %fusion.6), channel_id=1, source_target_pairs={{0,1},{1,0},{2,3},{3,2},{4,5},{5,4},{6,7},{7,6},{8,9},{9,8},{10,11... | collective-permute-start | bytes 1277960 | tf_op jit(solution)/shard_map/ppermute | solution.py:18
  184.2 15.4 %collective-permute-start.25 = (bf16[176,1664]{1,0:T(8,128)(2,1)}, bf16[176,1664]{1,0:T(8,128)(2,1)}, u32[]{:S(2)}, u32[]{:S(2)}) collective-permute-start(bf16[176,1664]{1,0:T(8,128)(2,1)} %collective-permute-done.24.refs_14_), channel_id=1, source_target_pairs={{0,2},{1,7},{2,4},{3,1},{4,6},{5,3},{6,0},{7,5},{8,10},{9,15},{10,... | collective-permute-start | bytes 1757192 | tf_op jit(solution)/shard_map/ppermute | solution.py:186
  189.6 13.3 %collective-permute-start.28 = (bf16[176,1664]{1,0:T(8,128)(2,1)}, bf16[176,1664]{1,0:T(8,128)(2,1)}, u32[]{:S(2)}, u32[]{:S(2)}) collective-permute-start(bf16[176,1664]{1,0:T(8,128)(2,1)} %collective-permute-done.27.refs_17_), channel_id=1, source_target_pairs={{0,2},{1,7},{2,4},{3,1},{4,6},{5,3},{6,0},{7,5},{8,10},{9,15},{10,... | collective-permute-start | bytes 1757192 | tf_op jit(solution)/shard_map/ppermute | solution.py:186
  191.6 16.4 %collective-permute-start.16 = (bf16[176,1664]{1,0:T(8,128)(2,1)}, bf16[176,1664]{1,0:T(8,128)(2,1)}, u32[]{:S(2)}, u32[]{:S(2)}) collective-permute-start(bf16[176,1664]{1,0:T(8,128)(2,1)} %collective-permute-done.15.refs_5_), channel_id=1, source_target_pairs={{0,128},{1,385},{128,256},{129,1},{256,384},{257,129},{384,0},{385... | collective-permute-start | bytes 1757192 | tf_op jit(solution)/shard_map/ppermute | solution.py:186
  195.2 36.6 %collective-permute-start.21 = (bf16[2,176,1664]{2,1,0:T(8,128)(2,1)}, bf16[2,176,1664]{2,1,0:T(8,128)(2,1)}, u32[]{:S(2)}, u32[]{:S(2)}) collective-permute-start(bf16[2,176,1664]{2,1,0:T(8,128)(2,1)} %collective-permute-done.20.refs_10_), channel_id=1, source_target_pairs={{0,128},{1,385},{128,256},{129,1},{256,384},{257,129},{384,0},{385... | collective-permute-start | bytes 3514376 | tf_op jit(solution)/shard_map/ppermute | solution.py:186
  197.5 34.4 %collective-permute-start.33 = (bf16[2,176,1664]{2,1,0:T(8,128)(2,1)}, bf16[2,176,1664]{2,1,0:T(8,128)(2,1)}, u32[]{:S(2)}, u32[]{:S(2)}) collective-permute-start(bf16[2,176,1664]{2,1,0:T(8,128)(2,1)} %collective-permute-done.32.refs_22_), channel_id=1, source_target_pairs={{0,2},{1,7},{2,4},{3,1},{4,6},{5,3},{6,0},{7,5},{8,10},{9,15},{10,... | collective-permute-start | bytes 3514376 | tf_op jit(solution)/shard_map/ppermute | solution.py:186
  199.6 22.0 %collective-permute-start.13 = (bf16[176,1664]{1,0:T(8,128)(2,1)}, bf16[176,1664]{1,0:T(8,128)(2,1)}, u32[]{:S(2)}, u32[]{:S(2)}) collective-permute-start(bf16[176,1664]{1,0:T(8,128)(2,1)} %copy-done.14), channel_id=1, source_target_pairs={{0,128},{1,385},{128,256},{129,1},{256,384},{257,129},{384,0},{385... | collective-permute-start | bytes 1757192 | tf_op jit(solution)/shard_map/ppermute | solution.py:186
  202.9 28.9 %collective-permute-start.29 = (bf16[176,1664]{1,0:T(8,128)(2,1)}, bf16[176,1664]{1,0:T(8,128)(2,1)}, u32[]{:S(2)}, u32[]{:S(2)}) collective-permute-start(bf16[176,1664]{1,0:T(8,128)(2,1)} %collective-permute-done.28.refs_18_), channel_id=1, source_target_pairs={{0,2},{1,7},{2,4},{3,1},{4,6},{5,3},{6,0},{7,5},{8,10},{9,15},{10,... | collective-permute-start | bytes 1757192 | tf_op jit(solution)/shard_map/ppermute | solution.py:186
  208.0 23.8 %collective-permute-start.17 = (bf16[176,1664]{1,0:T(8,128)(2,1)}, bf16[176,1664]{1,0:T(8,128)(2,1)}, u32[]{:S(2)}, u32[]{:S(2)}) collective-permute-start(bf16[176,1664]{1,0:T(8,128)(2,1)} %collective-permute-done.16.refs_6_), channel_id=1, source_target_pairs={{0,128},{1,385},{128,256},{129,1},{256,384},{257,129},{384,0},{385... | collective-permute-start | bytes 1757192 | tf_op jit(solution)/shard_map/ppermute | solution.py:186
  221.6 27.4 %collective-permute-start.35 = (bf16[256,1280]{1,0:T(8,128)(2,1)S(1)}, bf16[256,1280]{1,0:T(8,128)(2,1)S(1)}, u32[]{:S(2)}, u32[]{:S(2)}) collective-permute-start(bf16[256,1280]{1,0:T(8,128)(2,1)S(1)} %shard_map.96), channel_id=1, source_target_pairs={{0,1},{1,0},{2,3},{3,2},{4,5},{5,4},{6,7},{7,6},{8,9},{9,8},{10,11... | collective-permute-start | bytes 1966088 | tf_op jit(solution)/shard_map/ppermute | solution.py:18
  288.3 13.7 %all-to-all-start.1 = ((f32[16,16,256]{2,1,0:T(8,128)}), f32[16,16,256]{2,1,0:T(8,128)S(1)}, u32[]{:S(2)}, u32[]{:S(2)}) async-start(f32[16,16,256]{2,1,0:T(8,128)} %broadcast_in_dim.40), calls=%async_computation.1 | async-start | bytes 524288 | tf_op jit(solution)/shard_map/all_to_all | solution.py:299
  (37 other events, 601.7 us)
Sparse Core Ops, SparseCore 0:
  31.4 56.1 all-gather.4
  95.7 107.5 all-gather.6

commit v5 on v0

v5 whole, which is shorter than its diff:
```python
import functools

import jax
import jax.numpy as jnp
from jax import lax
from jax.experimental import pallas as pl
from jax.experimental.pallas import tpu as pltpu
from jax.sharding import Mesh, PartitionSpec as P

AXES = ("y", "zh", "zl", "x", "c")
SIZES = (4, 2, 8, 4, 2)
Z = ("zh", "zl")
NT = (((1,), (1,)), ((), ()))
bf16, f32 = jnp.bfloat16, jnp.float32
VMEM, ANYWHERE = pl.BlockSpec(memory_space=pltpu.VMEM), pl.BlockSpec(memory_space=pl.ANY)
SMEM = pl.BlockSpec(memory_space=pltpu.SMEM)

FIRST, SECOND, FIRST_EXTRA, SECOND_EXTRA, TEXTS, BLOCK = 112, 96, 32, 48, 16, 160


def params(mebibytes):
    return pltpu.CompilerParams(vmem_limit_bytes=mebibytes * 1024 * 1024)


def normalize(values):
    values = values.astype(f32)
    center = jnp.mean(values, axis=-1, keepdims=True)
    spread = jnp.mean((values - center) ** 2, axis=-1, keepdims=True)
    return (values - center) / jnp.sqrt(spread + 1e-05)


def unit_rows(emb):
    square = jnp.sum(emb * emb, axis=1, keepdims=True)
    return (emb / jnp.sqrt(square + 1e-06)).astype(bf16)


def fetch(source, target, sem):
    copy = pltpu.make_async_copy(source, target, sem)
    copy.start()
    return copy


def weights_kernel(ring, weights, sem):
    copies = []
    for z in range(16):
        layer, row = z // 8, z % 8 * (FIRST + SECOND)
        for core, start, count in ((0, row, FIRST), (1, row + FIRST, SECOND)):
            copies.append(fetch(
                ring.at[z, core, pl.ds(0, count), :], weights.at[layer, pl.ds(start, count), :], sem
            ))
    for copy in copies:
        copy.wait()


def layer_weights(ring):
    width = ring.shape[-1]
    return pl.pallas_call(
        weights_kernel,
        out_shape=jax.ShapeDtypeStruct((2, width, width), bf16),
        in_specs=[ANYWHERE],
        out_specs=ANYWHERE,
        scratch_shapes=[pltpu.SemaphoreType.DMA],
        compiler_params=params(47),
        cost_estimate=pl.CostEstimate(flops=0, bytes_accessed=8 * width * width, transcendentals=0),
    )(ring)


def texts_kernel(ring, units_ref, proj, texts, sem):
    copies = []
    for z in range(16):
        row = z * (FIRST_EXTRA + SECOND_EXTRA)
        for core, source, target, count in (
            (0, FIRST, row, FIRST_EXTRA), (1, SECOND, row + FIRST_EXTRA, SECOND_EXTRA)
        ):
            copies.append(fetch(
                ring.at[z, core, pl.ds(source, count), :], proj.at[pl.ds(target, count), :], sem
            ))
        copies.append(fetch(
            ring.at[z, 0, pl.ds(FIRST + FIRST_EXTRA, TEXTS), :], texts.at[pl.ds(z * TEXTS, TEXTS), :], sem
        ))
    for copy in copies:
        copy.wait()
    count, width = units_ref.shape
    emb = lax.dot_general(texts[:, :width], proj[:, :width], NT, preferred_element_type=f32)
    held = lax.broadcasted_iota(jnp.int32, (count, count), 1)
    index = ((held >> 1) & 63) * 4 + (held >> 7) * 2 + (held & 1)
    order = (index == lax.broadcasted_iota(jnp.int32, (count, count), 0)).astype(bf16)
    units_ref[...] = jnp.dot(order, unit_rows(emb), preferred_element_type=f32).astype(bf16)


def projection_and_texts(ring, count, text_width):
    width = ring.shape[-1]
    rows = 16 * (FIRST_EXTRA + SECOND_EXTRA)
    return pl.pallas_call(
        texts_kernel,
        out_shape=(
            jax.ShapeDtypeStruct((count, text_width), bf16),
            jax.ShapeDtypeStruct((rows, width), bf16),
        ),
        in_specs=[ANYWHERE],
        out_specs=(VMEM, VMEM),
        scratch_shapes=[pltpu.VMEM((16 * TEXTS, width), bf16), pltpu.SemaphoreType.DMA],
        compiler_params=params(47),
        cost_estimate=pl.CostEstimate(
            flops=2 * count * text_width * rows, bytes_accessed=2 * rows * width, transcendentals=0
        ),
    )(ring)


def layers_kernel(act_ref, weights, out_ref, normed):
    width = act_ref.shape[1]
    out_ref[...] = act_ref[...]
    for layer in range(2):
        normed[...] = normalize(out_ref[...]).astype(bf16)
        for start in range(0, width, 256):
            cols = pl.ds(start, min(256, width - start))
            update = jnp.dot(normed[...], weights[layer, :, cols], preferred_element_type=f32)
            out_ref[:, cols] = (out_ref[:, cols].astype(f32) + jax.nn.gelu(update)).astype(bf16)


def two_layers(act, weights):
    tokens, width = act.shape
    return pl.pallas_call(
        layers_kernel,
        out_shape=jax.ShapeDtypeStruct(act.shape, bf16),
        in_specs=[VMEM, VMEM],
        out_specs=VMEM,
        scratch_shapes=[pltpu.VMEM(act.shape, bf16)],
        compiler_params=params(24),
        cost_estimate=pl.CostEstimate(
            flops=4 * tokens * width * width, bytes_accessed=4 * width * width, transcendentals=0
        ),
    )(act, weights)


def rows_kernel(scale_ref, act_one, act_two, proj, units, rows_ref):
    width = act_one.shape[1]
    pooled = [jnp.mean(normalize(act[...]), axis=0, keepdims=True) for act in (act_one, act_two)]
    row = lax.broadcasted_iota(jnp.int32, (8, width), 0)
    pooled = jnp.where(row == 0, pooled[0], pooled[1]).astype(bf16)
    emb = lax.dot_general(pooled, proj[...], NT, preferred_element_type=f32)
    rows_ref[...] = scale_ref[0] * lax.dot_general(
        unit_rows(emb), units[...], NT, preferred_element_type=f32
    )


def logit_rows(scale, act_one, act_two, proj, units):
    return pl.pallas_call(
        rows_kernel,
        out_shape=jax.ShapeDtypeStruct((8, units.shape[0]), f32),
        in_specs=[SMEM, VMEM, VMEM, VMEM, VMEM],
        out_specs=VMEM,
        compiler_params=params(24),
    )(scale, act_one, act_two, proj, units)[:2]


def on_device(images, text_pooled, image_weight, proj_image, proj_text, logit_scale, pairing):
    y, zh, zl, x, c = (lax.axis_index(name) for name in AXES)
    width, text_width = proj_image.shape[0], proj_text.shape[0]
    micro = images.shape[0]
    count = pairing.shape[0]

    half = proj_image.shape[1] // 2
    widen = ((0, 0), (0, width - text_width))
    projection = jnp.where(
        y == 3,
        lax.dynamic_slice_in_dim(proj_image, zh * half, half, 1).T,
        jnp.pad(lax.dynamic_slice_in_dim(proj_text, zh * half, half, 1).T, widen),
    )
    texts = jnp.pad(lax.dynamic_slice_in_dim(text_pooled, zh * 2, 2, 0), widen)
    block = jnp.concatenate([image_weight[0], projection, texts])
    rows = image_weight.shape[1]
    spread = lax.all_to_all(
        jnp.broadcast_to(block[None], (8,) + block.shape), ("x", "c"), 0, 0, tiled=True
    )
    weight_rows = spread[:, :rows].reshape(8 * rows, width)
    projection_rows = spread[:, rows:rows + half].reshape(8 * half, width)
    text_rows = spread[:, rows + half:].reshape(TEXTS, width)
    ring = lax.all_gather(
        jnp.where(
            c == 0,
            jnp.concatenate([weight_rows[:FIRST], projection_rows[:FIRST_EXTRA], text_rows]),
            jnp.concatenate([
                weight_rows[FIRST:], projection_rows[FIRST_EXTRA:], jnp.zeros((TEXTS, width), bf16)
            ]),
        ),
        Z + ("c",), axis=0, tiled=True,
    ).reshape(16, 2, BLOCK, width)
    weights = layer_weights(ring)
    units, projection = projection_and_texts(ring, count, text_width)
    units = lax.ppermute(units, "y", [(2, 3)])

    acts = [lax.dynamic_index_in_dim(images, zh * 2 + i, 0, False) for i in range(2)]
    for plane in range(4):
        acts = [two_layers(act, weights) for act in acts]
        if plane < 3:
            acts = [lax.ppermute(act, "y", [(plane, plane + 1)]) for act in acts]
        if plane == 1:
            acts[0], units = lax.optimization_barrier((acts[0], units))
    own_rows = logit_rows(logit_scale, acts[0], acts[1], projection, units)

    other_rows = lax.ppermute(own_rows, "c", [(0, 1), (1, 0)])
    both = jnp.where(
        c == 0, jnp.concatenate([own_rows, other_rows]), jnp.concatenate([other_rows, own_rows])
    )
    of_z = lax.all_to_all(jnp.broadcast_to(both[None], (16, 4, count)), Z, 0, 0, tiled=True)
    logits = lax.all_to_all(
        jnp.broadcast_to(of_z.reshape(1, 64, count), (16, 64, count)), ("y", "x"), 0, 0, tiled=True
    )[12:]
    by_place = logits.reshape(4, 2, 8, 2, 2, count)
    zero = jnp.int32(0)
    own_logits = lax.dynamic_slice(
        by_place, (x, zero, zl, c, zero, zero), (1, 2, 1, 1, 2, count)
    ).reshape(micro, count)
    row_start = ((zl * 4 + x) * 2 + c) * micro
    column_lse = jnp.log(jnp.sum(jnp.exp(logits.reshape(count, count)), axis=0))
    own_pairs = lax.dynamic_slice_in_dim(pairing, row_start, micro, 0)
    paired = own_pairs[:, None] == lax.broadcasted_iota(jnp.int32, (1, count), 1)
    positive = jnp.sum(jnp.where(paired, own_logits, 0.0), axis=1)
    image_loss = jnp.log(jnp.sum(jnp.exp(own_logits), axis=1)) - positive
    text_loss = jnp.sum(jnp.where(paired, column_lse[None, :], 0.0), axis=1) - positive
    columns = count // 8
    logit_block = lax.dynamic_slice_in_dim(own_logits, (y * 2 + zh) * columns, columns, 1)
    return (logit_block, image_loss, text_loss)


def solution(mesh):
    fine = Mesh(mesh.devices.reshape(SIZES), AXES)
    section, dp = ("y", "zh"), ("zl", "x", "c")
    in_specs = (
        P(dp, None, None),
        P(dp, None),
        P(section, dp, None),
        P(None, dp),
        P(None, dp),
        P(),
        P(),
    )
    out_specs = (P(dp, section), P(dp), P(dp))
    return jax.shard_map(on_device, mesh=fine, in_specs=in_specs, out_specs=out_specs, check_vma=False)
```

time: 1850 us -> 605 us (0.33)
  waiting for transfers between devices: 1000 us -> 138 us
  blocking collectives: 642 us -> 20 us
  Pallas kernels: 0 us -> 365 us
  starting transfers between devices: 139 us -> 46.3 us
  other arithmetic: 23.5 us -> 3.83 us
    psum x1 -> x0, waiting for transfers between devices: 769 us -> none  [on_device(): logits_all = scale_value * lax.psum(partial_dots, 'dp')]
    pallas_call x0 -> x11, Pallas kernels: none -> 365 us  [the longest x1 337 us: layer_weights(): pl.pallas_call(weights_kernel, out_shape=jax.ShapeDtypeStruct((2, width,...]
    all_gather x2 -> x0, blocking collectives: 351 us -> none  [the longest x1 220 us: on_device(): lax.all_gather(pooled_image, 'dp', axis=0, tiled=True)]
    psum x2 -> x0, blocking collectives: 291 us -> none  [the longest x1 210 us: on_device(): lax.psum((jnp.sum(image_part * image_part, axis=1), jnp.sum(text_part * t...]
    ppermute x11 -> x8, waiting for transfers between devices: 226 us -> 2 us  [the longest x6 1.2 us: on_device(): acts = [lax.ppermute(act, 'y', [(plane, plane + 1)]) for act in acts]]
    ppermute x11 -> x8, starting transfers between devices: 139 us -> 11.3 us  [the longest x6 7.6 us: on_device(): acts = [lax.ppermute(act, 'y', [(plane, plane + 1)]) for act in acts]]
    all_gather x1, waiting for transfers between devices: 4.99 us -> 106 us  [on_device(): lax.all_gather(jnp.where(c == 0, jnp.concatenate([weight_rows[:FIRST], pr...]
    all_to_all x0 -> x2, starting transfers between devices: none -> 35 us  [the longest x1 24.7 us: on_device(): lax.all_to_all(jnp.broadcast_to(of_z.reshape(1, 64, count), (16, 64, coun...]
  transfers between devices with their start and end apart: 13 -> 11, of which waited for: 13 -> 5; matrix products, arithmetic and copies ran while one was open for 0% -> 0% of each run, Pallas kernels for 0% -> 3%
where the time goes in v5:
time: 605 us; the launch traced here: 603 us
  Pallas kernels  365 us (60%)
  waiting for transfers between devices  138 us (23%)
  starting transfers between devices  46.3 us (8%)
  blocking collectives  20 us (3%)
  local copies, waits for them, and re-layouts  15.1 us (2%)
  between operations  15.1 us (2%)
    pallas_call x1, Pallas kernels, layer_weights(): pl.pallas_call(weights_kernel, out_shape=jax.ShapeDtypeStruct((2, width,...  337 us
    all_gather x1, waiting for transfers between devices, on_device(): lax.all_gather(jnp.where(c == 0, jnp.concatenate([weight_rows[:FIRST], pr...  106 us
    all_to_all x1, starting transfers between devices, on_device(): lax.all_to_all(jnp.broadcast_to(of_z.reshape(1, 64, count), (16, 64, coun...  24.7 us
    pallas_call x8, Pallas kernels, two_layers(): pl.pallas_call(layers_kernel, out_shape=jax.ShapeDtypeStruct(act.shape, b...  21.8 us
    all_to_all x1, blocking collectives, on_device(): lax.all_to_all(jnp.broadcast_to(both[None], (16, 4, count)), Z, 0, 0, til...  20 us
    all_to_all x1, waiting for transfers between devices, on_device(): lax.all_to_all(jnp.broadcast_to(block[None], (8,) + block.shape), ('x', '...  15.2 us
    all_to_all x1, waiting for transfers between devices, on_device(): lax.all_to_all(jnp.broadcast_to(of_z.reshape(1, 64, count), (16, 64, coun...  14.8 us
  transfers between devices with their start and end apart: 11, of which 5 were waited for; matrix products, arithmetic and copies ran while one was open for 0% of the time, Pallas kernels for 3%

profile of v5, /device:TPU:1, one launch (start us, length us, event | category | flops | bytes accessed | tf_op | source)
XLA Modules:
  0.0 603.0 jit_solution(4209943999029391690)
XLA Ops:
  7.2 0.8 copy-done
  8.7 0.9 bitcast_select_fusion
  9.7 0.9 fusion.1
  10.6 1.1 broadcast_in_dim.40
  11.7 10.3 %all-to-all-start = ((bf16[8,38,1664]{2,1,0:T(8,128)(2,1)}), bf16[8,38,1664]{2,1,0:T(8,128)(2,1)S(1)}, u32[]{:S(2)}, u32[]{:S(2)}) async-start(bf16[8,38,1664]{2,1,0:T(8,128)(2,1)} %broadcast_in_dim.40), calls=%async_computation | async-start | bytes 2129920 | tf_op jit(solution)/shard_map/all_to_all | solution.py:173
  22.1 15.2 %all-to-all-done = bf16[8,38,1664]{2,1,0:T(8,128)(2,1)S(1)} async-done(((bf16[8,38,1664]{2,1,0:T(8,128)(2,1)}), bf16[8,38,1664]{2,1,0:T(8,128)(2,1)S(1)}, u32[]{:S(2)}, u32[]{:S(2)}) %all-to-all-start) | async-done | bytes 1011744 | tf_op jit(solution)/shard_map/all_to_all | solution.py:173
  38.0 1.0 maximum_select_fusion
  39.0 1.2 dynamic-slice_bitcast_fusion
  40.3 105.6 %all-gather.2.cloned.1.call-done = bf16[5120,1664]{1,0:T(8,128)(2,1)} async-done(((bf16[160,1664]{1,0:T(8,128)(2,1)}), bf16[5120,1664]{1,0:T(8,128)(2,1)}) %all-gather.2.cloned.1.call-update) | async-done | bytes 17039376 | tf_op jit(solution)/shard_map/all_gather | solution.py:179
  145.9 336.6 %shard_map.94.weights = bf16[2,1664,1664]{2,1,0:T(8,128)(2,1)} custom-call(bf16[16,2,160,1664]{3,2,1,0:T(8,128)(2,1)} %bitcast.11), custom_call_target="tpu_custom_call" | custom-call | bytes 22151168 | tf_op jit(solution)/shard_map/pallas_call | solution.py:57
  482.6 4.1 copy-done.1
  486.7 2.7 shard_map.100
  489.4 3.1 collective-permute-start.4
  492.6 2.7 shard_map.95
  495.3 1.3 collective-permute-start
  496.6 4.3 shard_map.97
  501.7 4.1 copy-done.2
  505.8 2.7 shard_map.101
  508.5 0.9 collective-permute-start.5
  509.4 1.2 collective-permute-done.act_ref
  510.6 2.7 shard_map.96
  514.0 2.7 shard_map.102
  517.5 2.7 shard_map.98
  520.2 0.9 collective-permute-start.3
  521.8 2.7 shard_map.103.act_two
  524.5 2.7 shard_map.99.act_one
  527.3 2.3 shard_map.104
  529.5 3.0 collective-permute-start.7
  533.4 20.0 %all_to_all.15 = f32[16,4,256]{2,1,0:T(4,128)S(1)} all-to-all(f32[16,4,256]{2,1,0:T(4,128)S(1)} %broadcast_in_dim.42), channel_id=1, replica_groups=mesh['y'=4,'zh'=2,'zl'=8,'x'=4,'c'=2] {'zh','zl'}, dimensions={0} | all-to-all | bytes 131072 | tf_op jit(solution)/shard_map/all_to_all | solution.py:206
  553.4 1.1 broadcast_in_dim.44
  554.5 24.7 %all-to-all-start.2 = ((f32[16,64,256]{2,1,0:T(8,128)}), f32[16,64,256]{2,1,0:T(8,128)S(1)}, u32[]{:S(2)}, u32[]{:S(2)}) async-start(f32[16,64,256]{2,1,0:T(8,128)} %broadcast_in_dim.44), calls=%async_computation.2 | async-start | bytes 2097152 | tf_op jit(solution)/shard_map/all_to_all | solution.py:207
  579.4 14.8 %all-to-all-done.2 = f32[16,64,256]{2,1,0:T(8,128)S(1)} async-done(((f32[16,64,256]{2,1,0:T(8,128)}), f32[16,64,256]{2,1,0:T(8,128)S(1)}, u32[]{:S(2)}, u32[]{:S(2)}) %all-to-all-start.2) | async-done | bytes 1048608 | tf_op jit(solution)/shard_map/all_to_all | solution.py:207
  (48 shorter events, 6.5 us)
Async XLA Ops:
  7.2 0.8 copy-start
  11.7 25.6 %all-to-all-start = ((bf16[8,38,1664]{2,1,0:T(8,128)(2,1)}), bf16[8,38,1664]{2,1,0:T(8,128)(2,1)S(1)}, u32[]{:S(2)}, u32[]{:S(2)}) async-start(bf16[8,38,1664]{2,1,0:T(8,128)(2,1)} %broadcast_in_dim.40), calls=%async_computation | async-start | bytes 2129920 | tf_op jit(solution)/shard_map/all_to_all | solution.py:173
  22.0 123.9 %all-gather.2.cloned.1.call-start = ((), (), s32[]{:S(2)}) async-start(), calls=%async_computation.3 | async-start | bytes 17571840 | tf_op jit(solution)/shard_map/all_gather | solution.py:179
  482.5 4.1 copy-start.1
  489.4 12.2 %collective-permute-start.4 = (bf16[128,1664]{1,0:T(8,128)(2,1)S(1)}, bf16[128,1664]{1,0:T(8,128)(2,1)S(1)}, u32[]{:S(2)}, u32[]{:S(2)}) collective-permute-start(bf16[128,1664]{1,0:T(8,128)(2,1)S(1)} %shard_map.100), channel_id=1, source_target_pairs={{0,128},{1,129},{2,130},{3,131},{4,132},{5,133},{6,134},{7,135},{8... | collective-permute-start | bytes 1277960 | tf_op jit(solution)/shard_map/ppermute | solution.py:197
  495.3 15.3 %collective-permute-start = (bf16[128,1664]{1,0:T(8,128)(2,1)S(1)}, bf16[128,1664]{1,0:T(8,128)(2,1)S(1)}, u32[]{:S(2)}, u32[]{:S(2)}) collective-permute-start(bf16[128,1664]{1,0:T(8,128)(2,1)S(1)} %shard_map.95), channel_id=1, source_target_pairs={{0,128},{1,129},{2,130},{3,131},{4,132},{5,133},{6,134},{7,135},{8... | collective-permute-start | bytes 1277960 | tf_op jit(solution)/shard_map/ppermute | solution.py:197
  500.9 16.5 %collective-permute-start.2 = (bf16[256,1280]{1,0:T(8,128)(2,1)S(1)}, bf16[256,1280]{1,0:T(8,128)(2,1)S(1)}, u32[]{:S(2)}, u32[]{:S(2)}) collective-permute-start(bf16[256,1280]{1,0:T(8,128)(2,1)S(1)} %get-tuple-element.7), channel_id=1, source_target_pairs={{256,384},{257,385},{258,386},{259,387},{260,388},{261,389},{262,3... | collective-permute-start | bytes 1966088 | tf_op jit(solution)/shard_map/ppermute | solution.py:191
  501.7 4.1 copy-start.2
  508.5 5.5 collective-permute-start.5
  513.3 4.1 collective-permute-start.1
  516.8 5.0 collective-permute-start.6
  520.2 4.3 collective-permute-start.3
  529.5 3.8 collective-permute-start.7
  554.5 24.7 %copy-start.3 = (s32[256]{0:T(256)S(1)}, s32[256]{0:T(256)}, u32[]{:S(2)}) copy-start(s32[256]{0:T(256)} %param.13) | copy-start | bytes 3076
  554.5 39.7 %all-to-all-start.2 = ((f32[16,64,256]{2,1,0:T(8,128)}), f32[16,64,256]{2,1,0:T(8,128)S(1)}, u32[]{:S(2)}, u32[]{:S(2)}) async-start(f32[16,64,256]{2,1,0:T(8,128)} %broadcast_in_dim.44), calls=%async_computation.2 | async-start | bytes 2097152 | tf_op jit(solution)/shard_map/all_to_all | solution.py:207
Sparse Core Ops, SparseCore 0:
  39.2 106.6 all-gather.1

commit v6 on v5

v6 whole, which is shorter than its diff:
```python
import functools

import jax
import jax.numpy as jnp
from jax import lax
from jax.experimental import pallas as pl
from jax.experimental.pallas import tpu as pltpu
from jax.sharding import Mesh, PartitionSpec as P

AXES = ("y", "zh", "zl", "x", "c")
SIZES = (4, 2, 8, 4, 2)
Z = ("zh", "zl")
NT = (((1,), (1,)), ((), ()))
bf16, f32 = jnp.bfloat16, jnp.float32
VMEM, ANYWHERE = pl.BlockSpec(memory_space=pltpu.VMEM), pl.BlockSpec(memory_space=pl.ANY)
SMEM = pl.BlockSpec(memory_space=pltpu.SMEM)

FIRST, SECOND, TEXTS = 32, 48, 16


def params(mebibytes):
    return pltpu.CompilerParams(vmem_limit_bytes=mebibytes * 1024 * 1024)


def normalize(values):
    values = values.astype(f32)
    center = jnp.mean(values, axis=-1, keepdims=True)
    spread = jnp.mean((values - center) ** 2, axis=-1, keepdims=True)
    return (values - center) / jnp.sqrt(spread + 1e-05)


def unit_rows(emb):
    square = jnp.sum(emb * emb, axis=1, keepdims=True)
    return (emb / jnp.sqrt(square + 1e-06)).astype(bf16)


def fetch(source, target, sem):
    copy = pltpu.make_async_copy(source, target, sem)
    copy.start()
    return copy


def fetch_projection(ring, proj, sem):
    copies = []
    for z in range(16):
        row = z * (FIRST + SECOND)
        copies += [
            fetch(ring.at[z, 0, pl.ds(0, FIRST), :], proj.at[pl.ds(row, FIRST), :], sem),
            fetch(ring.at[z, 1, pl.ds(0, SECOND), :], proj.at[pl.ds(row + FIRST, SECOND), :], sem),
        ]
    return copies


def texts_kernel(ring, units_ref, proj, texts, sem):
    copies = fetch_projection(ring, proj, sem)
    for z in range(16):
        copies.append(fetch(
            ring.at[z, 0, pl.ds(FIRST, TEXTS), :], texts.at[pl.ds(z * TEXTS, TEXTS), :], sem
        ))
    for copy in copies:
        copy.wait()
    count, width = units_ref.shape
    emb = lax.dot_general(texts[:, :width], proj[:, :width], NT, preferred_element_type=f32)
    held = lax.broadcasted_iota(jnp.int32, (count, count), 1)
    index = ((held >> 1) & 63) * 4 + (held >> 7) * 2 + (held & 1)
    order = (index == lax.broadcasted_iota(jnp.int32, (count, count), 0)).astype(bf16)
    units_ref[...] = jnp.dot(order, unit_rows(emb), preferred_element_type=f32).astype(bf16)


def text_units(ring, count, text_width):
    width = ring.shape[-1]
    rows = 16 * (FIRST + SECOND)
    return pl.pallas_call(
        texts_kernel,
        out_shape=jax.ShapeDtypeStruct((count, text_width), bf16),
        in_specs=[ANYWHERE],
        out_specs=VMEM,
        scratch_shapes=[
            pltpu.VMEM((rows, width), bf16),
            pltpu.VMEM((16 * TEXTS, width), bf16),
            pltpu.SemaphoreType.DMA,
        ],
        compiler_params=params(24),
        cost_estimate=pl.CostEstimate(
            flops=2 * count * text_width * rows, bytes_accessed=2 * rows * width, transcendentals=0
        ),
    )(ring)


def images_kernel(act_one, act_two, ring, units_ref, proj, sem):
    copies = fetch_projection(ring, proj, sem)
    width = act_one.shape[1]
    pooled = [jnp.mean(normalize(act[...]), axis=0, keepdims=True) for act in (act_one, act_two)]
    row = lax.broadcasted_iota(jnp.int32, (16, width), 0)
    pooled = jnp.where(row == 0, pooled[0], pooled[1]).astype(bf16)
    for copy in copies:
        copy.wait()
    units_ref[...] = unit_rows(lax.dot_general(pooled, proj[...], NT, preferred_element_type=f32))


def image_units(act_one, act_two, ring):
    width = ring.shape[-1]
    rows = 16 * (FIRST + SECOND)
    return pl.pallas_call(
        images_kernel,
        out_shape=jax.ShapeDtypeStruct((16, rows), bf16),
        in_specs=[VMEM, VMEM, ANYWHERE],
        out_specs=VMEM,
        scratch_shapes=[pltpu.VMEM((rows, width), bf16), pltpu.SemaphoreType.DMA],
        compiler_params=params(24),
        cost_estimate=pl.CostEstimate(
            flops=32 * rows * width, bytes_accessed=2 * rows * width, transcendentals=0
        ),
    )(act_one, act_two, ring)


def layers_kernel(act_ref, weights, out_ref, normed):
    width = act_ref.shape[1]
    out_ref[...] = act_ref[...]
    for layer in range(2):
        normed[...] = normalize(out_ref[...]).astype(bf16)
        for start in range(0, width, 256):
            cols = pl.ds(start, min(256, width - start))
            update = jnp.dot(normed[...], weights[layer, :, cols], preferred_element_type=f32)
            out_ref[:, cols] = (out_ref[:, cols].astype(f32) + jax.nn.gelu(update)).astype(bf16)


def two_layers(act, weights):
    tokens, width = act.shape
    return pl.pallas_call(
        layers_kernel,
        out_shape=jax.ShapeDtypeStruct(act.shape, bf16),
        in_specs=[VMEM, VMEM],
        out_specs=VMEM,
        scratch_shapes=[pltpu.VMEM(act.shape, bf16)],
        compiler_params=params(24),
        cost_estimate=pl.CostEstimate(
            flops=4 * tokens * width * width, bytes_accessed=4 * width * width, transcendentals=0
        ),
    )(act, weights)


def on_device(images, text_pooled, image_weight, proj_image, proj_text, logit_scale, pairing):
    y, zh, zl, x, c = (lax.axis_index(name) for name in AXES)
    width, text_width = proj_image.shape[0], proj_text.shape[0]
    micro = images.shape[0]
    count = pairing.shape[0]

    half = proj_image.shape[1] // 2
    widen = ((0, 0), (0, width - text_width))
    projection = jnp.where(
        y == 3,
        lax.dynamic_slice_in_dim(proj_image, zh * half, half, 1).T,
        jnp.pad(lax.dynamic_slice_in_dim(proj_text, zh * half, half, 1).T, widen),
    )
    texts = jnp.pad(lax.dynamic_slice_in_dim(text_pooled, zh * 2, 2, 0), widen)
    extra = jnp.concatenate([projection, texts])

    def spread(block):
        return lax.all_to_all(
            jnp.broadcast_to(block[None], (8,) + block.shape), ("x", "c"), 0, 0, tiled=True
        )

    def of_core(first, second):
        return jnp.where(c == 0, first, second)

    def round_z(block):
        return lax.all_gather(block, Z + ("c",), axis=0, tiled=True)

    rows = spread(image_weight[0]).reshape(-1, width)
    part = rows.shape[0] // 2
    part_rows, extra = lax.optimization_barrier((of_core(rows[:part], rows[part:]), extra))
    weights = round_z(part_rows)
    extra = spread(extra)
    projection, texts = extra[:, :half].reshape(8 * half, width), extra[:, half:].reshape(TEXTS, width)
    extra = of_core(jnp.concatenate([projection[:FIRST], texts]), projection[FIRST:])
    weights, extra = lax.optimization_barrier((weights, extra))
    weights = weights.reshape(2, width, width)
    ring = round_z(extra).reshape(16, 2, SECOND, width)

    acts = [lax.dynamic_index_in_dim(images, zh * 2 + i, 0, False) for i in range(2)]
    for plane in range(4):
        acts = [two_layers(act, weights) for act in acts]
        if plane < 3:
            acts = [lax.ppermute(act, "y", [(plane, plane + 1)]) for act in acts]
    ring, acts = lax.optimization_barrier((ring, acts))
    images_back = lax.ppermute(image_units(acts[0], acts[1], ring), "y", [(3, 2)])
    own_rows = logit_scale[0] * lax.dot_general(
        images_back, text_units(ring, count, text_width), NT, preferred_element_type=f32
    )[:2]

    of_z = lax.all_to_all(jnp.broadcast_to(own_rows[None], (16, 2, count)), Z, 0, 0, tiled=True)
    by_place = of_z.reshape(2, 8, 2, count)
    zero = jnp.int32(0)
    of_dp = lax.dynamic_slice(by_place, (zero, zl, zero, zero), (2, 1, 2, count)).reshape(micro, count)
    sums = jnp.sum(jnp.exp(of_z), axis=(0, 1))
    sent = jnp.concatenate([of_dp, sums[None]])
    from_plane = lax.all_to_all(
        jnp.broadcast_to(sent[None], (16,) + sent.shape), ("y", "x"), 0, 0, tiled=True
    )[8:12]
    own_logits = lax.dynamic_index_in_dim(from_plane, x, 0, False)[:micro]
    column_lse = jnp.log(lax.psum(jnp.sum(from_plane[:, micro], axis=0), "c"))
    row_start = ((zl * 4 + x) * 2 + c) * micro
    own_pairs = lax.dynamic_slice_in_dim(pairing, row_start, micro, 0)
    paired = own_pairs[:, None] == lax.broadcasted_iota(jnp.int32, (1, count), 1)
    positive = jnp.sum(jnp.where(paired, own_logits, 0.0), axis=1)
    image_loss = jnp.log(jnp.sum(jnp.exp(own_logits), axis=1)) - positive
    text_loss = jnp.sum(jnp.where(paired, column_lse[None, :], 0.0), axis=1) - positive
    columns = count // 8
    logit_block = lax.dynamic_slice_in_dim(own_logits, (y * 2 + zh) * columns, columns, 1)
    return (logit_block, image_loss, text_loss)


def solution(mesh):
    fine = Mesh(mesh.devices.reshape(SIZES), AXES)
    section, dp = ("y", "zh"), ("zl", "x", "c")
    in_specs = (
        P(dp, None, None),
        P(dp, None),
        P(section, dp, None),
        P(None, dp),
        P(None, dp),
        P(),
        P(),
    )
    out_specs = (P(dp, section), P(dp), P(dp))
    return jax.shard_map(on_device, mesh=fine, in_specs=in_specs, out_specs=out_specs, check_vma=False)
```

time: 605 us -> 259 us (0.43)
  Pallas kernels: 365 us -> 36.8 us
  starting transfers between devices: 46.3 us -> 34.1 us
    pallas_call x3 -> x2, Pallas kernels: 343 us -> 15.8 us  [the longest x1 8.4 us: text_units(): pl.pallas_call(texts_kernel, out_shape=jax.ShapeDtypeStruct((count, text_...]
    ppermute x6, waiting for transfers between devices: 1.2 us -> 10.7 us  [on_device(): acts = [lax.ppermute(act, 'y', [(plane, plane + 1)]) for act in acts]]
    all_to_all x2 -> x3, starting transfers between devices: 35 us -> 25.6 us  [the longest x1 10.3 us: spread(): lax.all_to_all(jnp.broadcast_to(block[None], (8,) + block.shape), ('x', '...]
    all_to_all x1, blocking collectives: 20 us -> 11.7 us  [spread(): lax.all_to_all(jnp.broadcast_to(block[None], (8,) + block.shape), ('x', '...]
    all_gather x1 -> x2, waiting for transfers between devices: 106 us -> 99.2 us  [round_z(): return lax.all_gather(block, Z + ('c',), axis=0, tiled=True)]
    all_to_all x2 -> x3, waiting for transfers between devices: 30 us -> 29.6 us  [the longest x1 11.5 us: on_device(): lax.all_to_all(jnp.broadcast_to(own_rows[None], (16, 2, count)), Z, 0, 0,...]
  transfers between devices with their start and end apart: 11 -> 12, of which waited for: 5 -> 7; matrix products, arithmetic and copies ran while one was open for 0% -> 1% of each run, Pallas kernels for 3% -> 11%
where the time goes in v6:
time: 259 us; the launch traced here: 258 us
  waiting for transfers between devices  140 us (54%)
  Pallas kernels  36.8 us (14%)
  starting transfers between devices  34.1 us (13%)
  blocking collectives  17 us (7%)
  between operations  15 us (6%)
  local copies, waits for them, and re-layouts  12.6 us (5%)
    all_gather x2, waiting for transfers between devices, round_z(): return lax.all_gather(block, Z + ('c',), axis=0, tiled=True)  99.2 us
    pallas_call x8, Pallas kernels, two_layers(): pl.pallas_call(layers_kernel, out_shape=jax.ShapeDtypeStruct(act.shape, b...  21 us
    all_to_all x1, blocking collectives, spread(): lax.all_to_all(jnp.broadcast_to(block[None], (8,) + block.shape), ('x', '...  11.7 us
    all_to_all x1, waiting for transfers between devices, on_device(): lax.all_to_all(jnp.broadcast_to(own_rows[None], (16, 2, count)), Z, 0, 0,...  11.5 us
    all_to_all x1, waiting for transfers between devices, spread(): lax.all_to_all(jnp.broadcast_to(block[None], (8,) + block.shape), ('x', '...  11.3 us
    ppermute x6, waiting for transfers between devices, on_device(): acts = [lax.ppermute(act, 'y', [(plane, plane + 1)]) for act in acts]  10.7 us
    all_to_all x1, starting transfers between devices, spread(): lax.all_to_all(jnp.broadcast_to(block[None], (8,) + block.shape), ('x', '...  10.3 us
    pallas_call x1, Pallas kernels, text_units(): pl.pallas_call(texts_kernel, out_shape=jax.ShapeDtypeStruct((count, text_...  8.4 us
  transfers between devices with their start and end apart: 12, of which 7 were waited for; matrix products, arithmetic and copies ran while one was open for 1% of the time, Pallas kernels for 11%

profile of v6, /device:TPU:1, one launch (start us, length us, event | category | flops | bytes accessed | tf_op | source)
XLA Modules:
  0.0 257.9 jit_solution(8691018558494726530)
XLA Ops:
  7.2 2.0 broadcast_in_dim.23
  9.2 10.3 %all-to-all-start = ((bf16[8,26,1664]{2,1,0:T(8,128)(2,1)}), bf16[8,26,1664]{2,1,0:T(8,128)(2,1)S(1)}, u32[]{:S(2)}, u32[]{:S(2)}) async-start(bf16[8,26,1664]{2,1,0:T(8,128)(2,1)} %broadcast_in_dim.23), calls=%async_computation | async-start | bytes 1703936 | tf_op jit(solution)/shard_map/all_to_all | solution.py:160
  19.6 0.7 constant_dynamic-slice_fusion.1
  20.3 0.9 bitcast_select_fusion
  21.3 11.3 %all-to-all-done = bf16[8,26,1664]{2,1,0:T(8,128)(2,1)S(1)} async-done(((bf16[8,26,1664]{2,1,0:T(8,128)(2,1)}), bf16[8,26,1664]{2,1,0:T(8,128)(2,1)S(1)}, u32[]{:S(2)}, u32[]{:S(2)}) %all-to-all-start) | async-done | bytes 692256 | tf_op jit(solution)/shard_map/all_to_all | solution.py:160
  32.6 0.8 select_n.62
  33.5 11.7 %all_to_all.20 = bf16[8,12,1664]{2,1,0:T(8,128)(2,1)S(1)} all-to-all(bf16[8,12,1664]{2,1,0:T(8,128)(2,1)S(1)} %broadcast_in_dim.46), channel_id=1, replica_groups=mesh['y'=4,'zh'=2,'zl'=8,'x'=4,'c'=2] {'x','c'}, dimensions={0} | all-to-all | bytes 638976 | tf_op jit(solution)/shard_map/all_to_all | solution.py:160
  46.1 69.7 %all-gather.3.cloned.1.call-done = bf16[3328,1664]{1,0:T(8,128)(2,1)} async-done(((bf16[104,1664]{1,0:T(8,128)(2,1)}), bf16[3328,1664]{1,0:T(8,128)(2,1)}) %all-gather.3.cloned.1.call-update) | async-done | bytes 11075600 | tf_op jit(solution)/shard_map/all_gather | solution.py:168
  116.0 4.1 %copy-done.1 = bf16[3328,1664]{1,0:T(8,128)(2,1)S(1)} copy-done((bf16[3328,1664]{1,0:T(8,128)(2,1)S(1)}, bf16[3328,1664]{1,0:T(8,128)(2,1)}, u32[]{:S(2)}) %copy-start.1) | copy-done | bytes 11075608
  120.1 2.6 %shard_map.98 = bf16[128,1664]{1,0:T(8,128)(2,1)S(1)} custom-call(bf16[128,1664]{1,0:T(8,128)(2,1)S(1)} %get-tuple-element.20.act_ref, bf16[2,1664,1664]{2,1,0:T(8,128)(2,1)S(1)} %bitcast.29), custom_call_target="tpu_custom_call" | custom-call | flops 1417674752 | bytes 11075584 | tf_op jit(solution)/shard_map/pallas_call | solution.py:130
  122.7 3.3 %collective-permute-start.3 = (bf16[128,1664]{1,0:T(8,128)(2,1)S(1)}, bf16[128,1664]{1,0:T(8,128)(2,1)S(1)}, u32[]{:S(2)}, u32[]{:S(2)}) collective-permute-start(bf16[128,1664]{1,0:T(8,128)(2,1)S(1)} %shard_map.98), channel_id=1, source_target_pairs={{0,128},{1,129},{2,130},{3,131},{4,132},{5,133},{6,134},{7,135},{8... | collective-permute-start | bytes 1277960 | tf_op jit(solution)/shard_map/ppermute | solution.py:185
  126.0 2.6 %shard_map.94 = bf16[128,1664]{1,0:T(8,128)(2,1)S(1)} custom-call(bf16[128,1664]{1,0:T(8,128)(2,1)S(1)} %get-tuple-element.21.act_ref, bf16[2,1664,1664]{2,1,0:T(8,128)(2,1)S(1)} %bitcast.30), custom_call_target="tpu_custom_call" | custom-call | flops 1417674752 | bytes 11075584 | tf_op jit(solution)/shard_map/pallas_call | solution.py:130
  128.7 1.4 collective-permute-start
  130.0 4.9 %collective-permute-done.3.act_ref = bf16[128,1664]{1,0:T(8,128)(2,1)S(1)} collective-permute-done((bf16[128,1664]{1,0:T(8,128)(2,1)S(1)}, bf16[128,1664]{1,0:T(8,128)(2,1)S(1)}, u32[]{:S(2)}, u32[]{:S(2)}) %collective-permute-start.3) | collective-permute-done | bytes 426016 | tf_op jit(solution)/shard_map/ppermute | solution.py:185
  134.9 2.6 %shard_map.99 = bf16[128,1664]{1,0:T(8,128)(2,1)S(1)} custom-call(bf16[128,1664]{1,0:T(8,128)(2,1)S(1)} %collective-permute-done.3.act_ref, bf16[2,1664,1664]{2,1,0:T(8,128)(2,1)S(1)} %bitcast.31), custom_call_target="tpu_custom_call" | custom-call | flops 1417674752 | bytes 11075584 | tf_op jit(solution)/shard_map/pallas_call | solution.py:130
  138.3 5.8 %collective-permute-done.act_ref = bf16[128,1664]{1,0:T(8,128)(2,1)S(1)} collective-permute-done((bf16[128,1664]{1,0:T(8,128)(2,1)S(1)}, bf16[128,1664]{1,0:T(8,128)(2,1)S(1)}, u32[]{:S(2)}, u32[]{:S(2)}) %collective-permute-start) | collective-permute-done | bytes 426016 | tf_op jit(solution)/shard_map/ppermute | solution.py:185
  144.1 2.6 %shard_map.95 = bf16[128,1664]{1,0:T(8,128)(2,1)S(1)} custom-call(bf16[128,1664]{1,0:T(8,128)(2,1)S(1)} %collective-permute-done.act_ref, bf16[2,1664,1664]{2,1,0:T(8,128)(2,1)S(1)} %bitcast.32), custom_call_target="tpu_custom_call" | custom-call | flops 1417674752 | bytes 11075584 | tf_op jit(solution)/shard_map/pallas_call | solution.py:130
  146.7 0.9 collective-permute-start.1
  147.6 2.6 %shard_map.100 = bf16[128,1664]{1,0:T(8,128)(2,1)S(1)} custom-call(bf16[128,1664]{1,0:T(8,128)(2,1)S(1)} %collective-permute-done.4.act_ref, bf16[2,1664,1664]{2,1,0:T(8,128)(2,1)S(1)} %bitcast.33), custom_call_target="tpu_custom_call" | custom-call | flops 1417674752 | bytes 11075584 | tf_op jit(solution)/shard_map/pallas_call | solution.py:130
  150.9 2.6 %shard_map.96 = bf16[128,1664]{1,0:T(8,128)(2,1)S(1)} custom-call(bf16[128,1664]{1,0:T(8,128)(2,1)S(1)} %collective-permute-done.1.act_ref, bf16[2,1664,1664]{2,1,0:T(8,128)(2,1)S(1)} %bitcast.34), custom_call_target="tpu_custom_call" | custom-call | flops 1417674752 | bytes 11075584 | tf_op jit(solution)/shard_map/pallas_call | solution.py:130
  154.9 2.6 %shard_map.101.act_two = bf16[128,1664]{1,0:T(8,128)(2,1)S(1)} custom-call(bf16[128,1664]{1,0:T(8,128)(2,1)S(1)} %collective-permute-done.5.act_ref, bf16[2,1664,1664]{2,1,0:T(8,128)(2,1)S(1)} %bitcast.35), custom_call_target="tpu_custom_call" | custom-call | flops 1417674752 | bytes 11075584 | tf_op jit(solution)/shard_map/pallas_call | solution.py:130
  157.6 2.6 %shard_map.97.act_one = bf16[128,1664]{1,0:T(8,128)(2,1)S(1)} custom-call(bf16[128,1664]{1,0:T(8,128)(2,1)S(1)} %collective-permute-done.2.act_ref, bf16[2,1664,1664]{2,1,0:T(8,128)(2,1)S(1)} %bitcast.36), custom_call_target="tpu_custom_call" | custom-call | flops 1417674752 | bytes 11075584 | tf_op jit(solution)/shard_map/pallas_call | solution.py:130
  160.2 29.5 %all-gather.5.cloned.1.call-done = bf16[1536,1664]{1,0:T(8,128)(2,1)} async-done(((bf16[48,1664]{1,0:T(8,128)(2,1)}), bf16[1536,1664]{1,0:T(8,128)(2,1)}) %all-gather.5.cloned.1.call-update) | async-done | bytes 5111824 | tf_op jit(solution)/shard_map/all_gather | solution.py:168
  189.7 2.4 copy-done.3
  192.2 7.4 %shard_map.102 = bf16[16,1280]{1,0:T(8,128)(2,1)S(1)} custom-call(bf16[128,1664]{1,0:T(8,128)(2,1)S(1)} %shard_map.97.act_one, bf16[128,1664]{1,0:T(8,128)(2,1)S(1)} %shard_map.101.act_two, bf16[16,2,48,1664]{3,2,1,0:T(8,128)(2,1)S(1)} %bitcast.37), custom_call_target="tpu_custom_call" | custom-call | flops 68157440 | bytes 4259840 | tf_op jit(solution)/shard_map/pallas_call | solution.py:104
  199.6 0.9 collective-permute-start.6
  200.4 8.4 %shard_map.103 = bf16[256,1280]{1,0:T(8,128)(2,1)S(1)} custom-call(bf16[16,2,48,1664]{3,2,1,0:T(8,128)(2,1)S(1)} %bitcast.38), custom_call_target="tpu_custom_call" | custom-call | flops 838860800 | bytes 4259840 | tf_op jit(solution)/shard_map/pallas_call | solution.py:73
  209.8 7.1 %all-to-all-start.2 = ((f32[16,2,256]{2,1,0:T(2,128)}), f32[16,2,256]{2,1,0:T(2,128)S(1)}, u32[]{:S(2)}, u32[]{:S(2)}) async-start(f32[16,2,256]{2,1,0:T(2,128)} %broadcast_in_dim.47), calls=%async_computation.2 | async-start | bytes 65536 | tf_op jit(solution)/shard_map/all_to_all | solution.py:192
  216.9 11.5 %all-to-all-done.2 = f32[16,2,256]{2,1,0:T(2,128)S(1)} async-done(((f32[16,2,256]{2,1,0:T(2,128)}), f32[16,2,256]{2,1,0:T(2,128)S(1)}, u32[]{:S(2)}, u32[]{:S(2)}) %all-to-all-start.2) | async-done | bytes 32800 | tf_op jit(solution)/shard_map/all_to_all | solution.py:192
  229.2 8.2 %all-to-all-start.3 = ((f32[16,5,256]{2,1,0:T(8,128)}), f32[16,5,256]{2,1,0:T(8,128)S(1)}, u32[]{:S(2)}, u32[]{:S(2)}) async-start(f32[16,5,256]{2,1,0:T(8,128)} %broadcast_in_dim.49), calls=%async_computation.3 | async-start | bytes 262144 | tf_op jit(solution)/shard_map/all_to_all | solution.py:198
  237.4 6.8 %all-to-all-done.3 = f32[16,5,256]{2,1,0:T(8,128)S(1)} async-done(((f32[16,5,256]{2,1,0:T(8,128)}), f32[16,5,256]{2,1,0:T(8,128)S(1)}, u32[]{:S(2)}, u32[]{:S(2)}) %all-to-all-start.3) | async-done | bytes 81952 | tf_op jit(solution)/shard_map/all_to_all | solution.py:198
  244.3 5.4 %psum.7 = f32[256]{0:T(256)S(1)} all-reduce(f32[256]{0:T(256)S(1)} %slice_reduce_fusion), channel_id=1, replica_groups=mesh['y'=4,'zh'=2,'zl'=8,'x'=4,'c'=2] {'c'}, use_global_device_ids=true, to_apply=%region_4.5 | all-reduce | flops 256 | bytes 2048 | tf_op jit(solution)/shard_map/psum | solution.py:202
  (48 shorter events, 6.5 us)
Async XLA Ops:
  7.2 12.4 %copy-start = (bf16[1280,20]{0,1:T(8,128)(2,1)S(1)}, bf16[1280,20]{0,1:T(8,128)(2,1)}, u32[]{:S(2)}) copy-start(bf16[1280,20]{0,1:T(8,128)(2,1)} %param.11) | copy-start | bytes 153604
  7.2 108.7 %copy-start.4 = (bf16[4,128,1664]{2,1,0:T(8,128)(2,1)S(1)}, bf16[4,128,1664]{2,1,0:T(8,128)(2,1)}, u32[]{:S(2)}) copy-start(bf16[4,128,1664]{2,1,0:T(8,128)(2,1)} %param.7) | copy-start | bytes 5111812
  9.2 23.3 %all-to-all-start = ((bf16[8,26,1664]{2,1,0:T(8,128)(2,1)}), bf16[8,26,1664]{2,1,0:T(8,128)(2,1)S(1)}, u32[]{:S(2)}, u32[]{:S(2)}) async-start(bf16[8,26,1664]{2,1,0:T(8,128)(2,1)} %broadcast_in_dim.23), calls=%async_computation | async-start | bytes 1703936 | tf_op jit(solution)/shard_map/all_to_all | solution.py:160
  19.5 96.3 %all-gather.3.cloned.1.call-start = ((), (), s32[]{:S(2)}) async-start(), calls=%async_computation.4 | async-start | bytes 11421696 | tf_op jit(solution)/shard_map/all_gather | solution.py:168
  33.5 156.3 %all-gather.5.cloned.1.call-start = ((), (), s32[]{:S(2)}) async-start(), calls=%async_computation.5 | async-start | bytes 5271552 | tf_op jit(solution)/shard_map/all_gather | solution.py:168
  115.9 4.1 %copy-start.1 = (bf16[3328,1664]{1,0:T(8,128)(2,1)S(1)}, bf16[3328,1664]{1,0:T(8,128)(2,1)}, u32[]{:S(2)}) copy-start(bf16[3328,1664]{1,0:T(8,128)(2,1)} %all-gather.3.cloned.1.call-done) | copy-start | bytes 33226756
  120.1 5.9 %copy-start.2 = (bf16[3328,1664]{1,0:T(8,128)(2,1)S(1)}, bf16[3328,1664]{1,0:T(8,128)(2,1)}, u32[]{:S(2)}) copy-start(bf16[3328,1664]{1,0:T(8,128)(2,1)} %all-gather.3.cloned.1.call-done) | copy-start | bytes 33226756
  122.7 12.2 %collective-permute-start.3 = (bf16[128,1664]{1,0:T(8,128)(2,1)S(1)}, bf16[128,1664]{1,0:T(8,128)(2,1)S(1)}, u32[]{:S(2)}, u32[]{:S(2)}) collective-permute-start(bf16[128,1664]{1,0:T(8,128)(2,1)S(1)} %shard_map.98), channel_id=1, source_target_pairs={{0,128},{1,129},{2,130},{3,131},{4,132},{5,133},{6,134},{7,135},{8... | collective-permute-start | bytes 1277960 | tf_op jit(solution)/shard_map/ppermute | solution.py:185
  128.7 15.4 %collective-permute-start = (bf16[128,1664]{1,0:T(8,128)(2,1)S(1)}, bf16[128,1664]{1,0:T(8,128)(2,1)S(1)}, u32[]{:S(2)}, u32[]{:S(2)}) collective-permute-start(bf16[128,1664]{1,0:T(8,128)(2,1)S(1)} %shard_map.94), channel_id=1, source_target_pairs={{0,128},{1,129},{2,130},{3,131},{4,132},{5,133},{6,134},{7,135},{8... | collective-permute-start | bytes 1277960 | tf_op jit(solution)/shard_map/ppermute | solution.py:185
  137.6 10.0 %collective-permute-start.4 = (bf16[128,1664]{1,0:T(8,128)(2,1)S(1)}, bf16[128,1664]{1,0:T(8,128)(2,1)S(1)}, u32[]{:S(2)}, u32[]{:S(2)}) collective-permute-start(bf16[128,1664]{1,0:T(8,128)(2,1)S(1)} %shard_map.99), channel_id=1, source_target_pairs={{128,256},{129,257},{130,258},{131,259},{132,260},{133,261},{134,2... | collective-permute-start | bytes 1277960 | tf_op jit(solution)/shard_map/ppermute | solution.py:185
  146.7 4.2 %collective-permute-start.1 = (bf16[128,1664]{1,0:T(8,128)(2,1)S(1)}, bf16[128,1664]{1,0:T(8,128)(2,1)S(1)}, u32[]{:S(2)}, u32[]{:S(2)}) collective-permute-start(bf16[128,1664]{1,0:T(8,128)(2,1)S(1)} %shard_map.95), channel_id=1, source_target_pairs={{128,256},{129,257},{130,258},{131,259},{132,260},{133,261},{134,2... | collective-permute-start | bytes 1277960 | tf_op jit(solution)/shard_map/ppermute | solution.py:185
  150.2 4.7 %collective-permute-start.5 = (bf16[128,1664]{1,0:T(8,128)(2,1)S(1)}, bf16[128,1664]{1,0:T(8,128)(2,1)S(1)}, u32[]{:S(2)}, u32[]{:S(2)}) collective-permute-start(bf16[128,1664]{1,0:T(8,128)(2,1)S(1)} %shard_map.100), channel_id=1, source_target_pairs={{256,384},{257,385},{258,386},{259,387},{260,388},{261,389},{262,3... | collective-permute-start | bytes 1277960 | tf_op jit(solution)/shard_map/ppermute | solution.py:185
  153.5 4.0 %collective-permute-start.2 = (bf16[128,1664]{1,0:T(8,128)(2,1)S(1)}, bf16[128,1664]{1,0:T(8,128)(2,1)S(1)}, u32[]{:S(2)}, u32[]{:S(2)}) collective-permute-start(bf16[128,1664]{1,0:T(8,128)(2,1)S(1)} %shard_map.96), channel_id=1, source_target_pairs={{256,384},{257,385},{258,386},{259,387},{260,388},{261,389},{262,3... | collective-permute-start | bytes 1277960 | tf_op jit(solution)/shard_map/ppermute | solution.py:185
  189.7 2.4 copy-start.3
  192.2 45.2 %copy-start.5 = (s32[256]{0:T(256)S(1)}, s32[256]{0:T(256)}, u32[]{:S(2)}) copy-start(s32[256]{0:T(256)} %param.13) | copy-start | bytes 3076
  199.6 9.3 %collective-permute-start.6 = (bf16[16,1280]{1,0:T(8,128)(2,1)S(1)}, bf16[16,1280]{1,0:T(8,128)(2,1)S(1)}, u32[]{:S(2)}, u32[]{:S(2)}) collective-permute-start(bf16[16,1280]{1,0:T(8,128)(2,1)S(1)} %shard_map.102), channel_id=1, source_target_pairs={{384,256},{385,257},{386,258},{387,259},{388,260},{389,261},{390,2... | collective-permute-start | bytes 122888 | tf_op jit(solution)/shard_map/ppermute | solution.py:187
  209.8 18.6 %all-to-all-start.2 = ((f32[16,2,256]{2,1,0:T(2,128)}), f32[16,2,256]{2,1,0:T(2,128)S(1)}, u32[]{:S(2)}, u32[]{:S(2)}) async-start(f32[16,2,256]{2,1,0:T(2,128)} %broadcast_in_dim.47), calls=%async_computation.2 | async-start | bytes 65536 | tf_op jit(solution)/shard_map/all_to_all | solution.py:192
  229.2 15.1 %all-to-all-start.3 = ((f32[16,5,256]{2,1,0:T(8,128)}), f32[16,5,256]{2,1,0:T(8,128)S(1)}, u32[]{:S(2)}, u32[]{:S(2)}) async-start(f32[16,5,256]{2,1,0:T(8,128)} %broadcast_in_dim.49), calls=%async_computation.3 | async-start | bytes 262144 | tf_op jit(solution)/shard_map/all_to_all | solution.py:198
Sparse Core Ops, SparseCore 0:
  33.6 82.2 all-gather.2
  117.9 71.7 all-gather.4
